TPU v7x, 32 devices: a whole 2x2x4 slice. The times are simulated.
32 devices in a mesh: dp: 8 (over y, x, core), tensor: 4 (over z).
Axes of the slice: x: 2, y: 2, z: 4, core: 2. Of those that a mesh axis runs over, the one named last changes fastest.
Arguments:
- tokens: bfloat16 [8192, 2048], P(('dp', 'tensor')), may hold values from -6 to 6
- positions: int32 [8192], P('dp'), may hold values from 0 to 767, as said below
- cotangent: bfloat16 [8192, 2048], P(('dp', 'tensor')), may hold values from -18 to 18
- query_weight: float32 [2048, 2048], P('dp', 'tensor'), may hold values from -0.125 to 0.125
- query_first: float32 [2048, 2048], P('dp', 'tensor'), may hold values from -64 to 64
- query_second: float32 [2048, 2048], P('dp', 'tensor'), may hold values from 8.192 to 32.768
- keyval_weight: float32 [2, 2048, 256], P(None, ('dp', 'tensor')), may hold values from -0.125 to 0.125
- keyval_first: float32 [2, 2048, 256], P(None, ('dp', 'tensor')), may hold values from -128 to 128
- keyval_second: float32 [2, 2048, 256], P(None, ('dp', 'tensor')), may hold values from 32.768 to 131.072
- output_weight: float32 [2048, 2048], P('tensor', 'dp'), may hold values from -1 to 1
- output_first: float32 [2048, 2048], P('tensor', 'dp'), may hold values from -6 to 6
- output_second: float32 [2048, 2048], P('tensor', 'dp'), may hold values from 0.32768 to 1.31072
- gateup_weight: float32 [2, 2048, 5632], P(None, 'dp', 'tensor'), may hold values from -0.125 to 0.125
- gateup_first: float32 [2, 2048, 5632], P(None, 'dp', 'tensor'), may hold values from -20 to 20
- gateup_second: float32 [2, 2048, 5632], P(None, 'dp', 'tensor'), may hold values from 0.98304 to 4.096
- down_weight: float32 [5632, 2048], P('tensor', 'dp'), may hold values from -0.078125 to 0.078125
- down_first: float32 [5632, 2048], P('tensor', 'dp'), may hold values from -32 to 32
- down_second: float32 [5632, 2048], P('tensor', 'dp'), may hold values from 2.94912 to 11.4688
- gains: float32 [2, 2048], P(None, ('dp', 'tensor')), may hold values from 0.5 to 1.5
- gains_first: float32 [2, 2048], P(None, ('dp', 'tensor')), may hold values from -64 to 64
- gains_second: float32 [2, 2048], P(None, ('dp', 'tensor')), may hold values from 8.192 to 32.768
Outputs:
- block_out: float32 [8192, 2048], P(('dp', 'tensor'))
- layer_input_gradient: float32 [8192, 2048], P(('dp', 'tensor'))
- query_first_new: float32 [2048, 2048], P('dp', 'tensor')
- query_second_new: float32 [2048, 2048], P('dp', 'tensor')
- query_new: float32 [2048, 2048], P('dp', 'tensor')
- keyval_first_new: float32 [2, 2048, 256], P(None, ('dp', 'tensor'))
- keyval_second_new: float32 [2, 2048, 256], P(None, ('dp', 'tensor'))
- keyval_new: float32 [2, 2048, 256], P(None, ('dp', 'tensor'))
- output_first_new: float32 [2048, 2048], P('tensor', 'dp')
- output_second_new: float32 [2048, 2048], P('tensor', 'dp')
- output_new: float32 [2048, 2048], P('tensor', 'dp')
- gateup_first_new: float32 [2, 2048, 5632], P(None, 'dp', 'tensor')
- gateup_second_new: float32 [2, 2048, 5632], P(None, 'dp', 'tensor')
- gateup_new: float32 [2, 2048, 5632], P(None, 'dp', 'tensor')
- down_first_new: float32 [5632, 2048], P('tensor', 'dp')
- down_second_new: float32 [5632, 2048], P('tensor', 'dp')
- down_new: float32 [5632, 2048], P('tensor', 'dp')
- gains_first_new: float32 [2, 2048], P(None, ('dp', 'tensor'))
- gains_second_new: float32 [2, 2048], P(None, ('dp', 'tensor'))
- gains_new: float32 [2, 2048], P(None, ('dp', 'tensor'))
Inputs may be any that keep to these rules, and one draw needn't show every extreme that they name: Each sequence of 1024 tokens is three documents; positions count from 0 at each document's first token and rise by one; the middle document starts within the first 256 tokens and holds exactly 768 tokens.
All inputs are finite; a program needn't handle non-finite values.
Results may differ from a plain program's by a relative error of at most 0.015.
Values may be sent and summed in bfloat16 or wider, within the bound.
No kernel may reach another device: no remote copies, remote signals or barrier semaphores. Data moves between devices by JAX's collectives and lax.ppermute only.
A program may use at most 256 MiB of HBM per device.

v0:
```python
import jax
import jax.numpy as jnp
from jax import lax
from jax.sharding import PartitionSpec as P

KVH = 4
HD = 64
STEP = 10
GROUP = 8


EPS = 1e-05
BETA_ONE = 0.9
BETA_TWO = 0.999
ADAM_EPS = 1e-08
DECAY = 0.1
RATE_QUERY = 0.06
RATE_KEYVAL = 0.06
RATE_OUTPUT = 0.5
RATE_GATEUP = 0.06
RATE_DOWN = 0.04
RATE_GAINS = 1.5
CONTRACT_ROWS = (((0,), (0,)), ((), ()))
CONTRACT_COLS = (((1,), (1,)), ((), ()))


def rope_tables(positions, width):
    freqs = 10000.0 ** (-jnp.arange(0, width, 2, dtype=jnp.float32) / width)
    angles = positions.astype(jnp.float32)[:, None] * freqs[None, :]
    angles = jnp.concatenate([angles, angles], -1)
    return (jnp.cos(angles), jnp.sin(angles))


def rotate_half(values):
    half = values.shape[-1] // 2
    return jnp.concatenate([-values[..., half:], values[..., :half]], -1)


def rope(values, cosine, sine):
    return values * cosine[:, None, :] + rotate_half(values) * sine[:, None, :]


def rope_back(grad_vals, cosine, sine):
    return grad_vals * cosine[:, None, :] - rotate_half(grad_vals * sine[:, None, :])


def norm_statistics(rows_in):
    inverse_rms_entries = lax.rsqrt(jnp.mean(rows_in * rows_in, -1, keepdims=True) + EPS)
    return (rows_in * inverse_rms_entries, inverse_rms_entries)


def norm_backward_pass(normalized_gradient, unit_row_entries, inverse_rms_entries, gain_entries):
    scaled_rows = normalized_gradient * gain_entries
    return inverse_rms_entries * (
        scaled_rows - unit_row_entries * jnp.mean(scaled_rows * unit_row_entries, -1, keepdims=True)
    )


def matmul_rows(left, right):
    return lax.dot_general(left, right, CONTRACT_ROWS, preferred_element_type=jnp.float32)


def matmul_cols(left, right):
    return lax.dot_general(left, right, CONTRACT_COLS, preferred_element_type=jnp.float32)


def collect_norm_rows(rows_low):
    return lax.all_gather(rows_low, "tensor", axis=0, tiled=True)


def gather_back(rows_low):
    return lax.all_gather(rows_low, "tensor", axis=0, tiled=True)


def share_rows(partial_value):
    return lax.psum_scatter(partial_value, "tensor", scatter_dimension=0, tiled=True)


def score_block(query_block, keys_rep, row_start, pos_block):
    raw_scores = jnp.einsum(
        "qhd,khd->hqk", query_block, keys_rep, preferred_element_type=jnp.float32
    ) * HD ** (-0.5)
    query_rows = row_start + jnp.arange(query_block.shape[0])
    key_rows = jnp.arange(keys_rep.shape[0])
    allowed = (key_rows[None, :] <= query_rows[:, None]) & (
        key_rows[None, :] >= (query_rows - pos_block)[:, None]
    )
    return jnp.where(allowed[None], raw_scores, -1e30)


def attend_forward(queries, keys_rep, values_rep, positions):
    length = queries.shape[0]
    block_rows = min(512, length)

    def one_block(block_index):
        row_start = block_index * block_rows
        query_block = lax.dynamic_slice_in_dim(queries, row_start, block_rows, 0)
        pos_block = lax.dynamic_slice_in_dim(positions, row_start, block_rows, 0)
        scores = score_block(query_block, keys_rep, row_start, pos_block)
        row_max = jnp.max(scores, -1, keepdims=True)
        expo_vals = jnp.exp(scores - row_max)
        row_total = jnp.sum(expo_vals, -1, keepdims=True)
        prob_low = (expo_vals / row_total).astype(jnp.bfloat16)
        mixed = jnp.einsum("hqk,khd->qhd", prob_low, values_rep, preferred_element_type=jnp.float32)
        return (mixed.astype(jnp.bfloat16), (row_max + jnp.log(row_total))[..., 0])

    mixed_all, log_totals = lax.map(one_block, jnp.arange(length // block_rows))
    return (mixed_all.reshape(length, -1), log_totals)


def attend_backward(queries, keys_rep, values_rep, positions, log_totals, grad_mixed):
    length = queries.shape[0]
    block_rows = min(512, length)
    grad_heads = grad_mixed.reshape(queries.shape)

    def one_block(carry, pieces):
        grad_keys, grad_values = carry
        block_index, log_block = pieces
        row_start = block_index * block_rows
        query_block = lax.dynamic_slice_in_dim(queries, row_start, block_rows, 0)
        pos_block = lax.dynamic_slice_in_dim(positions, row_start, block_rows, 0)
        grad_block = lax.dynamic_slice_in_dim(grad_heads, row_start, block_rows, 0)
        scores = score_block(query_block, keys_rep, row_start, pos_block)
        prob_vals = jnp.exp(scores - log_block[..., None])
        grad_probs = jnp.einsum(
            "qhd,khd->hqk", grad_block, values_rep, preferred_element_type=jnp.float32
        )
        delta = jnp.sum(grad_probs * prob_vals, -1, keepdims=True)
        grad_scores = (prob_vals * (grad_probs - delta)).astype(jnp.bfloat16)
        grad_query = jnp.einsum(
            "hqk,khd->qhd", grad_scores, keys_rep, preferred_element_type=jnp.float32
        ) * HD ** (-0.5)
        grad_keys = grad_keys + jnp.einsum(
            "hqk,qhd->khd", grad_scores, query_block, preferred_element_type=jnp.float32
        ) * HD ** (-0.5)
        grad_values = grad_values + jnp.einsum(
            "hqk,qhd->khd",
            prob_vals.astype(jnp.bfloat16),
            grad_block,
            preferred_element_type=jnp.float32,
        )
        return ((grad_keys, grad_values), grad_query)

    zero_keys = jnp.zeros(keys_rep.shape, jnp.float32)
    (grad_keys, grad_values), grad_query = lax.scan(
        one_block, (zero_keys, zero_keys), (jnp.arange(length // block_rows), log_totals)
    )
    return (grad_query.reshape(queries.shape), grad_keys, grad_values)


def adamw(weight, first, second, grad, rate, decay):
    first_new = BETA_ONE * first + (1.0 - BETA_ONE) * grad
    second_new = BETA_TWO * second + (1.0 - BETA_TWO) * grad * grad
    fix_one = 1.0 - BETA_ONE**STEP
    fix_two = 1.0 - BETA_TWO**STEP
    direction = first_new / fix_one / (jnp.sqrt(second_new / fix_two) + ADAM_EPS)
    return (first_new, second_new, weight - rate * (direction + decay * weight))


def on_device(
    tokens,
    positions,
    cotangent,
    query_weight,
    query_first,
    query_second,
    keyval_weight,
    keyval_first,
    keyval_second,
    output_weight,
    output_first,
    output_second,
    gateup_weight,
    gateup_first,
    gateup_second,
    down_weight,
    down_first,
    down_second,
    gains,
    gains_first,
    gains_second,
):
    rank = lax.axis_index("tensor")
    query_low, output_low, gateup_low, down_low = (
        lax.all_gather(query_weight.astype(jnp.bfloat16), "dp", axis=0, tiled=True),
        lax.all_gather(output_weight.astype(jnp.bfloat16), "dp", axis=1, tiled=True),
        lax.all_gather(gateup_weight.astype(jnp.bfloat16), "dp", axis=1, tiled=True),
        lax.all_gather(down_weight.astype(jnp.bfloat16), "dp", axis=1, tiled=True),
    )
    keyval_all, gain_low = (
        lax.all_gather(keyval_weight.astype(jnp.bfloat16), ("dp", "tensor"), axis=1, tiled=True),
        lax.all_gather(gains.astype(jnp.bfloat16), ("dp", "tensor"), axis=1, tiled=True),
    )
    heads_here = query_low.shape[1] // HD
    kv_heads = max(1, heads_here // GROUP)
    repeat_count = heads_here // kv_heads
    kv_start = rank * heads_here // GROUP * HD
    keyval_low = lax.dynamic_slice_in_dim(keyval_all, kv_start, kv_heads * HD, 2)
    first_norm_gain = gain_low[0].astype(jnp.float32)
    second_norm_gain = gain_low[1].astype(jnp.float32)
    cosine, sine = rope_tables(positions, HD)
    first_unit_rows, first_inverse_rms = norm_statistics(tokens.astype(jnp.float32))
    first_normalized = collect_norm_rows((first_unit_rows * first_norm_gain).astype(jnp.bfloat16))
    length = first_normalized.shape[0]
    query_pre = jnp.dot(first_normalized, query_low, preferred_element_type=jnp.float32).reshape(
        length, heads_here, HD
    )
    key_pre = jnp.dot(first_normalized, keyval_low[0], preferred_element_type=jnp.float32).reshape(
        length, kv_heads, HD
    )
    value_low = (
        jnp.dot(first_normalized, keyval_low[1], preferred_element_type=jnp.float32)
        .astype(jnp.bfloat16)
        .reshape(length, kv_heads, HD)
    )
    queries = rope(query_pre, cosine, sine).astype(jnp.bfloat16)
    keys_low = rope(key_pre, cosine, sine).astype(jnp.bfloat16)
    keys_rep = jnp.repeat(keys_low, repeat_count, 1)
    values_rep = jnp.repeat(value_low, repeat_count, 1)
    mixed_low, log_totals = attend_forward(queries, keys_rep, values_rep, positions)
    attn_part = jnp.dot(mixed_low, output_low, preferred_element_type=jnp.float32)
    residual_stream = tokens.astype(jnp.float32) + share_rows(attn_part)
    second_unit_rows, second_inverse_rms = norm_statistics(residual_stream)
    second_normalized = collect_norm_rows(
        (second_unit_rows * second_norm_gain).astype(jnp.bfloat16)
    )
    gate_proj = jnp.dot(second_normalized, gateup_low[0], preferred_element_type=jnp.float32)
    up_proj = jnp.dot(second_normalized, gateup_low[1], preferred_element_type=jnp.float32)
    sigmoid_gate = jax.nn.sigmoid(gate_proj)
    hidden_low = (gate_proj * sigmoid_gate * up_proj).astype(jnp.bfloat16)
    mlp_part = jnp.dot(hidden_low, down_low, preferred_element_type=jnp.float32)
    block_out = residual_stream + share_rows(mlp_part)
    grad_full = gather_back(cotangent)
    grad_down = matmul_rows(hidden_low, grad_full)
    grad_hidden = matmul_cols(grad_full, down_low)
    grad_up = (grad_hidden * gate_proj * sigmoid_gate).astype(jnp.bfloat16)
    grad_gate = (
        grad_hidden * up_proj * sigmoid_gate * (1.0 + gate_proj * (1.0 - sigmoid_gate))
    ).astype(jnp.bfloat16)
    grad_gateup = jnp.stack(
        [matmul_rows(second_normalized, grad_gate), matmul_rows(second_normalized, grad_up)]
    )
    grad_normed_two = matmul_cols(grad_gate, gateup_low[0]) + matmul_cols(grad_up, gateup_low[1])
    second_branch_gradient = share_rows(grad_normed_two)
    residual_gradient = cotangent.astype(jnp.float32) + norm_backward_pass(
        second_branch_gradient, second_unit_rows, second_inverse_rms, second_norm_gain
    )
    back_attn = gather_back(residual_gradient.astype(jnp.bfloat16))
    second_gain_gradient = jnp.sum(second_branch_gradient * second_unit_rows, 0)
    grad_output = matmul_rows(mixed_low, back_attn)
    grad_mixed = matmul_cols(back_attn, output_low).astype(jnp.bfloat16)
    grad_query, grad_keys_rep, grad_values_rep = attend_backward(
        queries, keys_rep, values_rep, positions, log_totals, grad_mixed
    )
    grad_keys = jnp.sum(grad_keys_rep.reshape(length, kv_heads, repeat_count, HD), 2)
    grad_values = jnp.sum(grad_values_rep.reshape(length, kv_heads, repeat_count, HD), 2)
    grad_query_pre = rope_back(grad_query, cosine, sine).reshape(length, -1).astype(jnp.bfloat16)
    grad_key_pre = rope_back(grad_keys, cosine, sine).reshape(length, -1).astype(jnp.bfloat16)
    grad_value_low = grad_values.reshape(length, -1).astype(jnp.bfloat16)
    grad_query_w = matmul_rows(first_normalized, grad_query_pre)
    grad_kv_here = jnp.stack(
        [matmul_rows(first_normalized, grad_key_pre), matmul_rows(first_normalized, grad_value_low)]
    )
    grad_keyval = lax.dynamic_update_slice_in_dim(
        jnp.zeros((2, first_normalized.shape[1], KVH * HD), jnp.float32), grad_kv_here, kv_start, 2
    )
    grad_normed_one = (
        matmul_cols(grad_query_pre, query_low)
        + matmul_cols(grad_key_pre, keyval_low[0])
        + matmul_cols(grad_value_low, keyval_low[1])
    )
    first_branch_gradient = share_rows(grad_normed_one)
    layer_input_gradient = residual_gradient + norm_backward_pass(
        first_branch_gradient, first_unit_rows, first_inverse_rms, first_norm_gain
    )
    first_gain_gradient = jnp.sum(first_branch_gradient * first_unit_rows, 0)
    owned_query, owned_output, owned_gateup, owned_down = (
        lax.psum_scatter(grad_query_w, "dp", scatter_dimension=0, tiled=True),
        lax.psum_scatter(grad_output, "dp", scatter_dimension=1, tiled=True),
        lax.psum_scatter(grad_gateup, "dp", scatter_dimension=1, tiled=True),
        lax.psum_scatter(grad_down, "dp", scatter_dimension=1, tiled=True),
    )
    owned_keyval, owned_gains = (
        lax.psum_scatter(grad_keyval, ("dp", "tensor"), scatter_dimension=1, tiled=True),
        lax.psum_scatter(
            jnp.stack([first_gain_gradient, second_gain_gradient]),
            ("dp", "tensor"),
            scatter_dimension=1,
            tiled=True,
        ),
    )
    query_up = adamw(query_weight, query_first, query_second, owned_query, RATE_QUERY, DECAY)
    keyval_up = adamw(keyval_weight, keyval_first, keyval_second, owned_keyval, RATE_KEYVAL, DECAY)
    output_up = adamw(output_weight, output_first, output_second, owned_output, RATE_OUTPUT, DECAY)
    gateup_up = adamw(gateup_weight, gateup_first, gateup_second, owned_gateup, RATE_GATEUP, DECAY)
    down_up = adamw(down_weight, down_first, down_second, owned_down, RATE_DOWN, DECAY)
    gains_up = adamw(gains, gains_first, gains_second, owned_gains, RATE_GAINS, 0.0)
    return (
        block_out,
        layer_input_gradient,
        query_up[0],
        query_up[1],
        query_up[2],
        keyval_up[0],
        keyval_up[1],
        keyval_up[2],
        output_up[0],
        output_up[1],
        output_up[2],
        gateup_up[0],
        gateup_up[1],
        gateup_up[2],
        down_up[0],
        down_up[1],
        down_up[2],
        gains_up[0],
        gains_up[1],
        gains_up[2],
    )


def solution(mesh):
    placed = (
        P(("dp", "tensor"), None),
        P("dp"),
        P(("dp", "tensor"), None),
        P("dp", "tensor"),
        P("dp", "tensor"),
        P("dp", "tensor"),
        P(None, ("dp", "tensor"), None),
        P(None, ("dp", "tensor"), None),
        P(None, ("dp", "tensor"), None),
        P("tensor", "dp"),
        P("tensor", "dp"),
        P("tensor", "dp"),
        P(None, "dp", "tensor"),
        P(None, "dp", "tensor"),
        P(None, "dp", "tensor"),
        P("tensor", "dp"),
        P("tensor", "dp"),
        P("tensor", "dp"),
        P(None, ("dp", "tensor")),
        P(None, ("dp", "tensor")),
        P(None, ("dp", "tensor")),
    )
    return jax.shard_map(
        on_device,
        mesh=mesh,
        in_specs=placed,
        out_specs=(
            P(("dp", "tensor"), None),
            P(("dp", "tensor"), None),
            P("dp", "tensor"),
            P("dp", "tensor"),
            P("dp", "tensor"),
            P(None, ("dp", "tensor"), None),
            P(None, ("dp", "tensor"), None),
            P(None, ("dp", "tensor"), None),
            P("tensor", "dp"),
            P("tensor", "dp"),
            P("tensor", "dp"),
            P(None, "dp", "tensor"),
            P(None, "dp", "tensor"),
            P(None, "dp", "tensor"),
            P("tensor", "dp"),
            P("tensor", "dp"),
            P("tensor", "dp"),
            P(None, ("dp", "tensor")),
            P(None, ("dp", "tensor")),
            P(None, ("dp", "tensor")),
        ),
        check_vma=False,
    )
```

profile of v0, /device:TPU:0, one launch (start us, length us, event | category | flops | bytes accessed | tf_op | source)
XLA Modules:
  0.0 1875.3 jit_solution(3329377397342898918)
XLA Ops:
  9.6 69.3 %all-gather = bf16[32,64,2]{1,2,0:T(2,128)(2,1)S(1)} all-gather(bf16[1,64,2]{1,2,0:T(2,128)(2,1)S(1)} %convert_bitcast_fusion), channel_id=1, replica_groups=mesh['dp'=8,'tensor'=4] {'dp','tensor'}, dimensions={0}, use_global_device_ids=true | all-gather | bytes 8448 | tf_op jit(solution)/shard_map/all_gather | solution.py:192
  86.3 74.7 %all-gather.11.cloned.1.call-done = bf16[1024,2048]{1,0:T(8,128)(2,1)} async-done(((bf16[256,2048]{1,0:T(8,128)(2,1)}), bf16[1024,2048]{1,0:T(8,128)(2,1)}) %all-gather.11.cloned.1.call-update) | async-done | bytes 4194320 | tf_op jit(solution)/shard_map/all_gather | solution.py:68
  164.7 25.1 %all-gather.13.cloned.1.call-done = bf16[2048,512]{1,0:T(8,128)(2,1)} async-done(((bf16[256,512]{1,0:T(8,128)(2,1)}), bf16[2048,512]{1,0:T(8,128)(2,1)}) %all-gather.13.cloned.1.call-update) | async-done | bytes 2097168 | tf_op jit(solution)/shard_map/all_gather | solution.py:185
  201.9 30.4 %while.28 = (s32[]{:T(128)}, bf16[2,512,8,64]{1,3,2,0:T(8,128)(2,1)S(1)}, f32[2,8,512]{2,1,0:T(8,128)}, s32[2]{0:T(128)S(1)}, s32[1024]{0:T(1024)S(1)}, /*index=...) while((s32[]{:T(128)}, ...), condition=%wide.region_4.5_spmd.clone, body=%wide.region_1.4_spmd.clone.sunk | while | flops 1125905408 | bytes 53881032 | solution.py:107
  244.5 141.4 %reduce-scatter.13.cloned.1.call-done = f32[256,2048]{1,0:T(8,128)} async-done(((f32[1024,2048]{1,0:T(8,128)}), f32[256,2048]{1,0:T(8,128)}) %reduce-scatter.13.cloned.1.call-update) | async-done | bytes 2097168 | tf_op jit(solution)/shard_map/reduce_scatter | solution.py:76
  392.8 63.9 %all-gather.21.cloned.1.call-done = bf16[2,2048,1408]{2,1,0:T(8,128)(2,1)} async-done(((bf16[2,256,1408]{2,1,0:T(8,128)(2,1)}), bf16[2,2048,1408]{2,1,0:T(8,128)(2,1)}) %all-gather.21.cloned.1.call-update) | async-done | bytes 11534352 | tf_op jit(solution)/shard_map/all_gather | solution.py:187
  456.7 82.9 %all-gather.19.cloned.1.call-done = bf16[1024,2048]{1,0:T(8,128)(2,1)} async-done(((bf16[256,2048]{1,0:T(8,128)(2,1)}), bf16[1024,2048]{1,0:T(8,128)(2,1)}) %all-gather.19.cloned.1.call-update) | async-done | bytes 4194320 | tf_op jit(solution)/shard_map/all_gather | solution.py:68
  539.6 11.9 fusion.43
  559.9 60.6 %all-gather.25.cloned.1.call-done = bf16[1024,2048]{1,0:T(8,128)(2,1)} async-done(((bf16[256,2048]{1,0:T(8,128)(2,1)}), bf16[1024,2048]{1,0:T(8,128)(2,1)}) %all-gather.25.cloned.1.call-update) | async-done | bytes 4194320 | tf_op jit(solution)/shard_map/all_gather | solution.py:72
  620.5 45.4 %all-gather.23.cloned.1.call-done = bf16[1408,2048]{1,0:T(8,128)(2,1)} async-done(((bf16[1408,256]{1,0:T(8,128)(2,1)}), bf16[1408,2048]{1,0:T(8,128)(2,1)}) %all-gather.23.cloned.1.call-update) | async-done | bytes 5767184 | tf_op jit(solution)/shard_map/all_gather | solution.py:188
  665.9 15.7 multiply_convert_fusion.1
  681.6 10.8 fusion.40
  703.6 144.2 %reduce-scatter.17.cloned.1.call-done = f32[256,2048]{1,0:T(8,128)} async-done(((f32[1024,2048]{1,0:T(8,128)}), f32[256,2048]{1,0:T(8,128)}) %reduce-scatter.17.cloned.1.call-update) | async-done | bytes 2097168 | tf_op jit(solution)/shard_map/reduce_scatter | solution.py:76
  852.4 11.2 fusion.95
  863.8 70.3 %all-gather.27.cloned.1.call-done = bf16[1024,2048]{1,0:T(8,128)(2,1)} async-done(((bf16[256,2048]{1,0:T(8,128)(2,1)}), bf16[1024,2048]{1,0:T(8,128)(2,1)}) %all-gather.27.cloned.1.call-update) | async-done | bytes 4194320 | tf_op jit(solution)/shard_map/all_gather | solution.py:72
  949.1 124.3 %while.29 = (s32[]{:T(128)}, f32[1024,8,64]{0,2,1:T(8,128)}, f32[1024,8,64]{0,2,1:T(8,128)}, f32[2,512,8,64]{1,0,3,2:T(2,128)}, s32[2]{0:T(128)S(1)}, /*index=5*...) while((s32[]{:T(128)}, f32[1024,8,64]{0,2,1:T(8,128)}, ...), condition=%wide.region_12.13_spmd.clone, body=%wide.region_10.12_spmd.clone.sunk | while | flops 2726556672 | bytes 180840752 | solution.py:145
  989.6 19.6 %dynamic_update_slice.26 = f32[2,512,8,64]{1,0,3,2:T(2,128)} dynamic-update-slice(f32[2,512,8,64]{1,0,3,2:T(2,128)} %get-tuple-element.466, f32[1,512,8,64]{1,0,3,2:T(1,128)S(1)} %copy.67, s32[]{:T(128)S(6)} %copy.84, s32[]{:T(128)} %constant.62.clone.1..sunk.1, s32[]{:T(128)} %constant.62.clone.1..sunk.1, s32[]{:T(128)} %constant.62.clone.1..sunk.1) | dynamic-update-slice | bytes 2097156 | tf_op jit(solution)/shard_map/while/body/jit(dynamic_update_index_in_dim)/dynamic_update_slice | solution.py:145
  1030.5 10.7 multiply_convert_fusion.6
  1053.7 19.6 %dynamic_update_slice.26 = f32[2,512,8,64]{1,0,3,2:T(2,128)} dynamic-update-slice(f32[2,512,8,64]{1,0,3,2:T(2,128)} %get-tuple-element.466, f32[1,512,8,64]{1,0,3,2:T(1,128)S(1)} %copy.67, s32[]{:T(128)S(6)} %copy.84, s32[]{:T(128)} %constant.62.clone.1..sunk.1, s32[]{:T(128)} %constant.62.clone.1..sunk.1, s32[]{:T(128)} %constant.62.clone.1..sunk.1) | dynamic-update-slice | bytes 2097156 | tf_op jit(solution)/shard_map/while/body/jit(dynamic_update_index_in_dim)/dynamic_update_slice | solution.py:145
  1169.4 117.0 %reduce-scatter.23.cloned.1.call-done = f32[2,64,256]{2,1,0:T(8,128)} async-done(((f32[2,2048,256]{2,1,0:T(8,128)}), f32[2,64,256]{2,1,0:T(8,128)}) %reduce-scatter.23.cloned.1.call-update) | async-done | bytes 131088 | tf_op jit(solution)/shard_map/reduce_scatter | solution.py:284
  1288.1 146.1 %reduce-scatter.27.cloned.1.call-done = f32[2,256,1408]{2,1,0:T(8,128)} async-done(((f32[2,2048,1408]{2,1,0:T(8,128)}), f32[2,256,1408]{2,1,0:T(8,128)}) %reduce-scatter.27.cloned.1.call-update) | async-done | bytes 2883600 | tf_op jit(solution)/shard_map/reduce_scatter | solution.py:280
  1441.9 139.0 %reduce-scatter.19.cloned.1.call-done = f32[256,2048]{1,0:T(8,128)} async-done(((f32[1024,2048]{1,0:T(8,128)}), f32[256,2048]{1,0:T(8,128)}) %reduce-scatter.19.cloned.1.call-update) | async-done | bytes 2097168 | tf_op jit(solution)/shard_map/reduce_scatter | solution.py:76
  1584.6 143.8 %reduce-scatter.15.cloned.1.call-done = f32[256,2048]{1,0:T(8,128)} async-done(((f32[1024,2048]{1,0:T(8,128)}), f32[256,2048]{1,0:T(8,128)}) %reduce-scatter.15.cloned.1.call-update) | async-done | bytes 2097168 | tf_op jit(solution)/shard_map/reduce_scatter | solution.py:76
  1734.7 132.4 %reduce-scatter.31.cloned.1.call-done = f32[64,2]{1,0:T(8,128)} async-done(((f32[2048,2]{1,0:T(8,128)}), f32[64,2]{1,0:T(8,128)}) %reduce-scatter.31.cloned.1.call-update) | async-done | bytes 528
  (287 shorter events, 301.5 us)
Async XLA Ops:
  7.2 79.1 %all-gather.15.cloned.1.call-start = ((), (), s32[]{:S(2)}) async-start(), calls=%async_computation.12 | async-start | bytes 2162688 | tf_op jit(solution)/shard_map/all_gather | solution.py:191
  8.9 152.0 %all-gather.11.cloned.1.call-start = ((), (), s32[]{:S(2)}) async-start(), calls=%async_computation.10 | async-start | bytes 5242880 | tf_op jit(solution)/shard_map/all_gather | solution.py:68
  83.7 106.1 %all-gather.13.cloned.1.call-start = ((), (), s32[]{:S(2)}) async-start(), calls=%async_computation.11 | async-start | bytes 2359296 | tf_op jit(solution)/shard_map/all_gather | solution.py:185
  84.6 149.1 %all-gather.17.cloned.1.call-start = ((), (), s32[]{:S(2)}) async-start(), calls=%async_computation.13 | async-start | bytes 2359296 | tf_op jit(solution)/shard_map/all_gather | solution.py:186
  85.4 300.5 %reduce-scatter.13.cloned.1.call-start = ((), (), s32[]{:S(2)}) async-start(), calls=%async_computation.14 | async-start | bytes 10485760 | tf_op jit(solution)/shard_map/reduce_scatter | solution.py:76
  241.3 215.4 %all-gather.21.cloned.1.call-start = ((), (), s32[]{:S(2)}) async-start(), calls=%async_computation.16 | async-start | bytes 12976128 | tf_op jit(solution)/shard_map/all_gather | solution.py:187
  244.4 295.2 %all-gather.19.cloned.1.call-start = ((), (), s32[]{:S(2)}) async-start(), calls=%async_computation.15 | async-start | bytes 5242880 | tf_op jit(solution)/shard_map/all_gather | solution.py:68
  388.1 462.6 %copy-start.5 = (f32[256,2048]{1,0:T(8,128)}, f32[256,2048]{1,0:T(8,128)S(1)}, u32[]{:S(2)}) copy-start(f32[256,2048]{1,0:T(8,128)S(1)} %get-tuple-element.251) | copy-start | bytes 6291460
  388.1 462.6 %copy-start.45 = (f32[256]{0:T(256)}, f32[256]{0:T(256)S(1)}, u32[]{:S(2)}) copy-start(f32[256]{0:T(256)S(1)} %add_rsqrt_fusion) | copy-start | bytes 3076
  389.6 230.9 %all-gather.25.cloned.1.call-start = ((), (), s32[]{:S(2)}) async-start(), calls=%async_computation.19 | async-start | bytes 5242880 | tf_op jit(solution)/shard_map/all_gather | solution.py:72
  390.4 275.5 %all-gather.23.cloned.1.call-start = ((), (), s32[]{:S(2)}) async-start(), calls=%async_computation.17 | async-start | bytes 6488064 | tf_op jit(solution)/shard_map/all_gather | solution.py:188
  392.7 455.1 %reduce-scatter.17.cloned.1.call-start = ((), (), s32[]{:S(2)}) async-start(), calls=%async_computation.20 | async-start | bytes 10485760 | tf_op jit(solution)/shard_map/reduce_scatter | solution.py:76
  703.2 230.9 %all-gather.27.cloned.1.call-start = ((), (), s32[]{:S(2)}) async-start(), calls=%async_computation.21 | async-start | bytes 5242880 | tf_op jit(solution)/shard_map/all_gather | solution.py:72
  852.4 305.6 %reduce-scatter.29.cloned.1.call-start = ((), (), s32[]{:S(2)}) async-start(), calls=%async_computation.27 | async-start | bytes 12976128 | tf_op jit(solution)/shard_map/reduce_scatter | solution.py:281
  863.7 300.3 %reduce-scatter.25.cloned.1.call-start = ((), (), s32[]{:S(2)}) async-start(), calls=%async_computation.25 | async-start | bytes 4718592 | tf_op jit(solution)/shard_map/reduce_scatter | solution.py:279
  940.5 226.4 %reduce-scatter.21.cloned.1.call-start = ((), (), s32[]{:S(2)}) async-start(), calls=%async_computation.23 | async-start | bytes 4718592 | tf_op jit(solution)/shard_map/reduce_scatter | solution.py:278
  1086.9 199.6 %reduce-scatter.23.cloned.1.call-start = ((), (), s32[]{:S(2)}) async-start(), calls=%async_computation.24 | async-start | bytes 4325376 | tf_op jit(solution)/shard_map/reduce_scatter | solution.py:284
  1109.6 324.6 %reduce-scatter.27.cloned.1.call-start = ((), (), s32[]{:S(2)}) async-start(), calls=%async_computation.26 | async-start | bytes 25952256 | tf_op jit(solution)/shard_map/reduce_scatter | solution.py:280
  1134.9 446.0 %reduce-scatter.19.cloned.1.call-start = ((), (), s32[]{:S(2)}) async-start(), calls=%async_computation.22 | async-start | bytes 10485760 | tf_op jit(solution)/shard_map/reduce_scatter | solution.py:76
  1145.3 583.1 %reduce-scatter.15.cloned.1.call-start = ((), (), s32[]{:S(2)}) async-start(), calls=%async_computation.18 | async-start | bytes 10485760 | tf_op jit(solution)/shard_map/reduce_scatter | solution.py:76
  1157.7 709.4 %reduce-scatter.31.cloned.1.call-start = ((), (), s32[]{:S(2)}) async-start(), calls=%async_computation.28 | async-start | bytes 1081344
  1288.1 292.8 %copy-start.8 = (bf16[256,2048]{1,0:T(8,128)(2,1)S(1)}, bf16[256,2048]{1,0:T(8,128)(2,1)}, u32[]{:S(2)}) copy-start(bf16[256,2048]{1,0:T(8,128)(2,1)} %param.25) | copy-start | bytes 3145732
  1288.1 292.8 %copy-start.41 = (f32[1,2048]{1,0:T(1,128)S(1)}, f32[1,2048]{1,0:T(1,128)}, u32[]{:S(2)}) copy-start(f32[1,2048]{1,0:T(1,128)} %copy-done.40) | copy-start | bytes 24580
  1288.1 292.8 %copy-start.48 = (f32[256]{0:T(256)S(1)}, f32[256]{0:T(256)}, u32[]{:S(2)}) copy-start(f32[256]{0:T(256)} %copy-done.47) | copy-start | bytes 3076
  (60 other events, 3334.6 us)
Sparse Core Ops, SparseCore 0:
  11.7 59.2 all-gather.14
  83.9 77.0 all-gather.10
  163.4 26.4 all-gather.12
  192.2 28.1 all-gather.16
  241.4 144.4 reduce-scatter.12
  388.2 68.4 all-gather.20
  458.8 80.7 all-gather.18
  541.2 79.2 all-gather.24
  623.0 42.8 all-gather.22
  703.3 144.4 reduce-scatter.16
  852.5 81.4 all-gather.26
  937.4 85.3 reduce-scatter.28
  1026.1 51.2 reduce-scatter.24
  1087.0 49.2 reduce-scatter.20
  1138.4 147.9 reduce-scatter.22
  1289.9 144.2 reduce-scatter.26
  1436.4 144.4 reduce-scatter.18
  1583.1 145.1 reduce-scatter.14
  1730.6 136.4 reduce-scatter.30
where the time goes:
time: 1880 us
  waiting for transfers between devices  1390 us (74%)
  matrix products  219 us (12%)
  other arithmetic  99 us (5%)
  local copies, waits for them, and re-layouts  80.3 us (4%)
  blocking collectives  69.3 us (4%)
    reduce_scatter x4, waiting for transfers between devices, share_rows(): lax.psum_scatter(partial_value, 'tensor', scatter_dimension=0, tiled=True)  568 us
    all_gather x2, waiting for transfers between devices, collect_norm_rows(): return lax.all_gather(rows_low, 'tensor', axis=0, tiled=True)  158 us
    reduce_scatter x1, waiting for transfers between devices, on_device(): lax.psum_scatter(grad_gateup, 'dp', scatter_dimension=1, tiled=True)  146 us
    unnamed x20, waiting for transfers between devices  133 us
    all_gather x2, waiting for transfers between devices, gather_back(): return lax.all_gather(rows_low, 'tensor', axis=0, tiled=True)  131 us
    reduce_scatter x1, waiting for transfers between devices, on_device(): lax.psum_scatter(grad_keyval, ('dp', 'tensor'), scatter_dimension=1, tile...  117 us
    all_gather x1, blocking collectives, on_device(): lax.all_gather(gains.astype(jnp.bfloat16), ('dp', 'tensor'), axis=1, tile...  69.3 us
    all_gather x1, waiting for transfers between devices, on_device(): lax.all_gather(gateup_weight.astype(jnp.bfloat16), 'dp', axis=1, tiled=True)  63.9 us
  transfers between devices with their start and end apart: 19, of which 14 were waited for; matrix products, arithmetic and copies ran while one was open for 18% of the time, Pallas kernels for 0%

commit v1 on v0

v1 whole, which is shorter than its diff:
```python
import functools

import jax
import jax.numpy as jnp
from jax import lax
from jax.experimental import pallas as pl
from jax.experimental.pallas import tpu as pltpu
from jax.sharding import PartitionSpec as P

H = 32
KVH = 4
HD = 64
GROUP = 8
KVD = KVH * HD
STEP = 10
EPS = 1e-05
BETA_ONE = 0.9
BETA_TWO = 0.999
ADAM_EPS = 1e-08
DECAY = 0.1
RATE_QUERY = 0.06
RATE_KEYVAL = 0.06
RATE_OUTPUT = 0.5
RATE_GATEUP = 0.06
RATE_DOWN = 0.04
RATE_GAINS = 1.5
LOW = jnp.bfloat16
F32 = jnp.float32
TALL = 128
VMEM_LIMIT = 56 * 1024 * 1024
LONG = pl.CostEstimate(flops=2 * 10**14, bytes_accessed=10**6, transcendentals=0)


def lasting(us):
    return pl.CostEstimate(flops=int(us * 1.15e9), bytes_accessed=10**6, transcendentals=0)


def contract(left, right, dim_left, dim_right):
    return lax.dot_general(
        left, right, (((dim_left,), (dim_right,)), ((), ())), preferred_element_type=F32
    )


def ring_offsets(n):
    return [0] + [-k for k in range(1, n // 2 + 1)] + [k for k in range(1, (n - 1) // 2 + 1)]


def shift(x, n, by):
    return lax.ppermute(x, "tensor", [(i, (i + by) % n) for i in range(n)])


def ring_gather(x, n, steps=None, known=None):
    slots, used = [x], 1
    for by, hops in ((1, n // 2), (-1, (n - 1) // 2)):
        held = x
        for hop in range(hops):
            if steps is not None and hop >= steps:
                slots.append(None)
                continue
            if known is not None and known[used + hop] is not None:
                held = known[used + hop]
            else:
                held = shift(held, n, by)
            slots.append(held)
        used += hops
    return slots


def after(late, early):
    return lax.optimization_barrier((late, early))


def ring_way(slots, n, by, passed=None, hold=None):
    first, hops = (1, n // 2) if by < 0 else (1 + n // 2, (n - 1) // 2)
    held = None
    for k in range(hops, 0, -1):
        part = slots[first + k - 1]
        if held is not None:
            part = (part.astype(F32) + held.astype(F32)).astype(LOW)
            if hold is not None and k == 1:
                part, _ = after(part, hold)
            if passed is not None:
                passed.append(part)
        held = shift(part.astype(LOW), n, by)
    return held


def ring_most(slots, n):
    held = None
    for k in range(n // 2, 1, -1):
        part = slots[k] if held is None else ring_sum(slots[k], held)
        held = shift(part.astype(LOW), n, -1)
    return held


def ring_last(slots, n, held, hold=None):
    part = (slots[1] if held is None else ring_sum(slots[1], held)).astype(LOW)
    if hold is not None:
        part, _ = after(part, hold)
    return shift(part, n, -1)


def ring_sum(own, *arrived):
    total = own.astype(F32)
    for held in arrived:
        if held is not None:
            total = total + held.astype(F32)
    return total


def ring_scatter(slots, n):
    return ring_sum(slots[0], ring_way(slots, n, -1), ring_way(slots, n, 1))


def swap(x, size, bit):
    return lax.ppermute(x, "dp", [(i, i ^ bit) for i in range(size)])


def dp_plan(size, block):
    bits = [1 << i for i in range(1, size.bit_length() - 1)]
    return [bits, bits[::-1]] if block >= 256 else [bits]


def dp_order(size, block, odd):
    plan = dp_plan(size, block)
    me = lax.axis_index("dp")
    places = []
    for h, bits in enumerate(plan):
        partners = [odd]
        for bit in bits:
            partners += [p | bit for p in partners]
        places += [(me ^ p) * len(plan) + h for p in partners]
    return jnp.stack(places).astype(jnp.int32)


def dp_spread(x, size, hold):
    block = x.shape[0]
    plan = dp_plan(size, block)
    tall = block // len(plan)
    even = [x[h * tall : (h + 1) * tall] for h in range(len(plan))]
    for i in range(len(plan[0])):
        got = [swap(held, size, bits[i]) for held, bits in zip(even, plan)]
        even = [jnp.concatenate(pair, 0) for pair in zip(even, got)]
        if i == 0:
            even, _ = after(even, hold)
    return even


def dp_scatter(held, size, hold):
    plan = dp_plan(size, 2 * held.shape[0] // size)
    tall = held.shape[0] // len(plan)
    parts = [held[h * tall : (h + 1) * tall] for h in range(len(plan))]
    for i in reversed(range(len(plan[0]))):
        half = parts[0].shape[0] // 2
        got = [swap(part[half:], size, bits[i]) for part, bits in zip(parts, plan)]
        if i == len(plan[0]) - 1:
            got, _ = after(got, hold)
        parts = [ring_sum(part[:half], new).astype(LOW) for part, new in zip(parts, got)]
    return jnp.concatenate(parts, 0)


def norm_statistics(rows_in):
    inverse = lax.rsqrt(jnp.mean(rows_in * rows_in, -1, keepdims=True) + EPS)
    return rows_in * inverse, inverse


def norm_backward(grad, unit, inverse, gain):
    scaled = grad * gain
    return inverse * (scaled - unit * jnp.mean(scaled * unit, -1, keepdims=True))


def adamw(weight, first, second, grad, rate, decay):
    first_new = BETA_ONE * first + (1.0 - BETA_ONE) * grad
    second_new = BETA_TWO * second + (1.0 - BETA_TWO) * grad * grad
    fix_one = 1.0 - BETA_ONE**STEP
    fix_two = 1.0 - BETA_TWO**STEP
    direction = first_new / fix_one / (jnp.sqrt(second_new / fix_two) + ADAM_EPS)
    return first_new, second_new, weight - rate * (direction + decay * weight)


def turn(values, cosine, sine):
    upper, lower = values[: HD // 2], values[HD // 2 :]
    return jnp.concatenate([upper * cosine - lower * sine, lower * cosine + upper * sine], 0)


def begin_kernel(
    x_ref, gain_ref, weight_ref, cos_ref, sin_ref, out_ref, rows_ref, gains_ref, inverse_ref
):
    gains = gain_ref[...].astype(F32).T[: gains_ref.shape[0]]
    unit, inverse = norm_statistics(x_ref[...].astype(F32))
    rows = (unit * gains[:1]).astype(LOW)
    rows_ref[...], gains_ref[...], inverse_ref[...] = rows, gains, inverse
    wide = jnp.dot(rows, weight_ref[...], preferred_element_type=F32).T
    cosine, sine = cos_ref[...], sin_ref[...]
    for h in range(KVH):
        here = slice(h * HD, (h + 1) * HD)
        out_ref[here, :] = turn(wide[here], cosine, sine).astype(LOW)
    out_ref[KVD:, :] = wide[KVD:].astype(LOW)


def begin(x, weight, cosine, sine):
    tokens, width = x.shape
    cols = 2 * KVD
    return pl.pallas_call(
        begin_kernel,
        grid=(1,),
        in_specs=[
            pl.BlockSpec((tokens, width), lambda b: (0, 0)),
            pl.BlockSpec((width, TALL), lambda b: (0, (H * HD + cols) // TALL)),
            pl.BlockSpec((width, cols), lambda b: (0, H * HD // cols)),
            pl.BlockSpec(cosine.shape, lambda b: (0, 0)),
            pl.BlockSpec(sine.shape, lambda b: (0, 0)),
        ],
        out_specs=[
            pl.BlockSpec((cols, tokens), lambda b: (0, 0)),
            pl.BlockSpec((tokens, width), lambda b: (0, 0)),
            pl.BlockSpec((8, width), lambda b: (0, 0)),
            pl.BlockSpec((tokens, 1), lambda b: (0, 0)),
        ],
        out_shape=[
            jax.ShapeDtypeStruct((cols, tokens), LOW),
            jax.ShapeDtypeStruct((tokens, width), LOW),
            jax.ShapeDtypeStruct((8, width), F32),
            jax.ShapeDtypeStruct((tokens, 1), F32),
        ],
        compiler_params=pltpu.CompilerParams(vmem_limit_bytes=VMEM_LIMIT),
        cost_estimate=lasting(5.0),
        name="begin",
    )(x, weight, weight, cosine, sine)


def project_kernel(rows_ref, weight_ref, cos_ref, sin_ref, out_ref):
    wide = jnp.dot(rows_ref[...], weight_ref[...], preferred_element_type=F32).T
    cosine, sine = cos_ref[...], sin_ref[...]
    for h in range(wide.shape[0] // HD):
        here = slice(h * HD, (h + 1) * HD)
        out_ref[here, :] = (turn(wide[here], cosine, sine) * HD ** (-0.5)).astype(LOW)


def project(rows, weight, cosine, sine):
    tokens, width = rows.shape
    cols = 2 * KVD
    blocks = H * HD // cols
    return pl.pallas_call(
        project_kernel,
        grid=(blocks,),
        in_specs=[
            pl.BlockSpec((tokens, width), lambda b: (0, 0)),
            pl.BlockSpec((width, cols), lambda b: (0, b)),
            pl.BlockSpec(cosine.shape, lambda b: (0, 0)),
            pl.BlockSpec(sine.shape, lambda b: (0, 0)),
        ],
        out_specs=pl.BlockSpec((cols, tokens), lambda b: (b, 0)),
        out_shape=jax.ShapeDtypeStruct((blocks * cols, tokens), LOW),
        compiler_params=pltpu.CompilerParams(vmem_limit_bytes=VMEM_LIMIT),
        cost_estimate=lasting(8.0),
        name="project",
    )(rows, weight, cosine, sine)


def fill_bias(meta_ref, pos_ref, bias_ref, slots, tokens):
    query = meta_ref[2 * slots] + lax.broadcasted_iota(jnp.int32, (tokens, tokens), 1)
    least = query - pos_ref[...]
    row = lax.broadcasted_iota(jnp.int32, (tokens, tokens), 0)
    for c in range(slots):
        key = meta_ref[c] + row
        bias_ref[c] = jnp.where((key <= query) & (key >= least), 0.0, -1e30)


def attend_kernel(
    slots, heads, meta_ref, pos_ref, q_ref, kv_ref, out_ref, rows_ref, lse_ref, bias_ref
):
    tokens = q_ref.shape[1]
    block = pl.program_id(0)

    @pl.when(block == 0)
    def _():
        fill_bias(meta_ref, pos_ref, bias_ref, slots, tokens)

    start = pl.multiple_of(meta_ref[slots + block] * HD, HD)
    keys = [kv_ref[c, pl.ds(start, HD), :].T for c in range(slots)]
    values = [kv_ref[c, pl.ds(KVD + start, HD), :] for c in range(slots)]
    for h in range(heads):
        query = q_ref[h * HD : (h + 1) * HD, :]
        scores = [
            jnp.dot(keys[c], query, preferred_element_type=F32) + bias_ref[c] for c in range(slots)
        ]
        peak = functools.reduce(jnp.maximum, [jnp.max(s, 0, keepdims=True) for s in scores])
        total = jnp.zeros_like(peak)
        mixed = jnp.zeros((HD, tokens), F32)
        for c in range(slots):
            expo = jnp.exp(scores[c] - peak)
            total = total + jnp.sum(expo, 0, keepdims=True)
            mixed = mixed + jnp.dot(values[c], expo.astype(LOW), preferred_element_type=F32)
        out_ref[h * HD : (h + 1) * HD, :] = (mixed / total).astype(LOW)
        lse_ref[0, h : h + 1, :] = peak + jnp.log(total)
    rows_ref[...] = out_ref[...].T


def attend(meta, pos_row, q_t, kv_slots, slots):
    tokens = q_t.shape[1]
    heads = H // slots
    rows = heads * HD
    return pl.pallas_call(
        functools.partial(attend_kernel, slots, heads),
        grid_spec=pltpu.PrefetchScalarGridSpec(
            num_scalar_prefetch=1,
            grid=(slots,),
            in_specs=[
                pl.BlockSpec((1, tokens), lambda b, m: (0, 0)),
                pl.BlockSpec((rows, tokens), lambda b, m: (b, 0)),
                pl.BlockSpec((slots, 2 * KVD, tokens), lambda b, m: (0, 0, 0)),
            ],
            out_specs=[
                pl.BlockSpec((rows, tokens), lambda b, m: (b, 0)),
                pl.BlockSpec((tokens, rows), lambda b, m: (0, b)),
                pl.BlockSpec((1, heads, tokens), lambda b, m: (b, 0, 0)),
            ],
            scratch_shapes=[pltpu.VMEM((slots, tokens, tokens), F32)],
        ),
        out_shape=[
            jax.ShapeDtypeStruct((H * HD, tokens), LOW),
            jax.ShapeDtypeStruct((tokens, H * HD), LOW),
            jax.ShapeDtypeStruct((slots, heads, tokens), F32),
        ],
        compiler_params=pltpu.CompilerParams(vmem_limit_bytes=VMEM_LIMIT),
        cost_estimate=pl.CostEstimate(
            flops=16 * H * HD * tokens * tokens * slots,
            bytes_accessed=4 * H * HD * tokens,
            transcendentals=H * tokens * tokens * slots,
        ),
        name="attend",
    )(meta, pos_row, q_t, kv_slots)


def attend_back_kernel(slots, heads, count, meta_ref, pos_ref, q_ref, kv_ref, back_ref, *refs):
    weights, refs = refs[:count], refs[count:]
    o_ref, lse_ref, cos_ref, sin_ref, dq_ref, dkv_out_ref = refs[:6]
    bias_ref, dkv_ref, do_ref, moved_ref = refs[6:]
    tokens = q_ref.shape[1]
    block = pl.program_id(0)

    @pl.when(block == 0)
    def _():
        fill_bias(meta_ref, pos_ref, bias_ref, slots, tokens)
        dkv_ref[...] = jnp.zeros_like(dkv_ref)
        for i in range(back_ref.shape[1] // TALL):
            at = pl.multiple_of(meta_ref[2 * slots + 1 + i] * TALL, TALL)
            moved_ref[:, i * TALL : (i + 1) * TALL] = back_ref[:, pl.ds(at, TALL)]

    grad_mixed, at = 0.0, 0
    for weight in weights:
        here = slice(at, at + weight.shape[0])
        grad_mixed += jnp.dot(moved_ref[:, here], weight[...], preferred_element_type=F32)
        at += weight.shape[0]
    do_ref[...] = grad_mixed.T.astype(LOW)
    start = pl.multiple_of(meta_ref[slots + block] * HD, HD)
    keys_t = [kv_ref[c, pl.ds(start, HD), :] for c in range(slots)]
    keys = [k.T for k in keys_t]
    values = [kv_ref[c, pl.ds(KVD + start, HD), :].T for c in range(slots)]
    cosine, sine = cos_ref[...], -sin_ref[...]
    grad_keys = [jnp.zeros((HD, tokens), F32) for _ in range(slots)]
    grad_values = [jnp.zeros((HD, tokens), F32) for _ in range(slots)]
    for h in range(heads):
        here = slice(h * HD, (h + 1) * HD)
        query, grad = q_ref[here, :], do_ref[here, :]
        delta = jnp.sum(grad.astype(F32) * o_ref[here, :].astype(F32), 0, keepdims=True)
        log_total = lse_ref[0, h : h + 1, :]
        grad_query = jnp.zeros((HD, tokens), F32)
        for c in range(slots):
            scores = jnp.dot(keys[c], query, preferred_element_type=F32) + bias_ref[c]
            prob = jnp.exp(scores - log_total)
            grad_prob = jnp.dot(values[c], grad, preferred_element_type=F32)
            grad_score = (prob * (grad_prob - delta)).astype(LOW)
            grad_values[c] = grad_values[c] + contract(grad, prob.astype(LOW), 1, 1)
            grad_keys[c] = grad_keys[c] + contract(query, grad_score, 1, 1)
            grad_query = grad_query + jnp.dot(keys_t[c], grad_score, preferred_element_type=F32)
        dq_ref[here, :] = (turn(grad_query, cosine, sine) * HD ** (-0.5)).astype(LOW)
    for c in range(slots):
        dkv_ref[c, pl.ds(start, HD), :] += grad_keys[c]
        dkv_ref[c, pl.ds(KVD + start, HD), :] += grad_values[c]

    @pl.when(block == pl.num_programs(0) - 1)
    def _():
        dkv_out_ref[...] = dkv_ref[...].astype(LOW)


def attend_back(meta, pos_row, q_t, kv_slots, back, weights, o_t, lse, cosine, sine, slots):
    tokens = q_t.shape[1]
    heads = H // slots
    rows = heads * HD
    head_block = pl.BlockSpec((rows, tokens), lambda b, m: (b, 0))
    table = pl.BlockSpec(cosine.shape, lambda b, m: (0, 0))
    whole = pl.BlockSpec((slots, 2 * KVD, tokens), lambda b, m: (0, 0, 0))
    return pl.pallas_call(
        functools.partial(attend_back_kernel, slots, heads, len(weights)),
        grid_spec=pltpu.PrefetchScalarGridSpec(
            num_scalar_prefetch=1,
            grid=(slots,),
            in_specs=[
                pl.BlockSpec((1, tokens), lambda b, m: (0, 0)),
                head_block,
                whole,
                pl.BlockSpec(back.shape, lambda b, m: (0, 0)),
                *[pl.BlockSpec((w.shape[0], rows), lambda b, m: (0, b)) for w in weights],
                head_block,
                pl.BlockSpec((1, heads, tokens), lambda b, m: (b, 0, 0)),
                table,
                table,
            ],
            out_specs=[head_block, whole],
            scratch_shapes=[
                pltpu.VMEM((slots, tokens, tokens), F32),
                pltpu.VMEM((slots, 2 * KVD, tokens), F32),
                pltpu.VMEM((rows, tokens), LOW),
                pltpu.VMEM(back.shape, LOW),
            ],
        ),
        out_shape=[
            jax.ShapeDtypeStruct((H * HD, tokens), LOW),
            jax.ShapeDtypeStruct((slots, 2 * KVD, tokens), LOW),
        ],
        compiler_params=pltpu.CompilerParams(vmem_limit_bytes=VMEM_LIMIT),
        cost_estimate=LONG,
        name="attend_back",
    )(meta, pos_row, q_t, kv_slots, back, *weights, o_t, lse, cosine, sine)


def mix_kernel(count, order_ref, o_ref, x_ref, gain_ref, *refs):
    weights, (h_ref, n_ref, inverse_ref) = refs[:count], refs[count : count + 3]
    held, sems = refs[count + 3 : -1], refs[-1]
    copies = [
        pltpu.make_async_copy(src, dst, sems.at[i]) for i, (src, dst) in enumerate(zip(weights, held))
    ]
    for copy in copies:
        copy.start()
    at = 0
    for copy, weight in zip(copies, held):
        copy.wait()
        mixed = contract(o_ref[...], weight[...], 1, 1)
        for i in range(weight.shape[0] // TALL):
            here = pl.ds(pl.multiple_of(order_ref[at] * TALL, TALL), TALL)
            h_ref[:, here] = x_ref[:, here].astype(F32) + mixed[:, i * TALL : (i + 1) * TALL]
            at += 1
    unit, inverse = norm_statistics(h_ref[...])
    n_ref[...] = (unit * gain_ref[...]).astype(LOW)
    inverse_ref[...] = inverse


def mix(order, o, x, gain, weights):
    tokens, width = x.shape
    count = len(weights)
    full = pl.BlockSpec((tokens, width), lambda i, o: (0, 0))
    return pl.pallas_call(
        functools.partial(mix_kernel, count),
        grid_spec=pltpu.PrefetchScalarGridSpec(
            num_scalar_prefetch=1,
            grid=(1,),
            in_specs=[
                pl.BlockSpec(o.shape, lambda i, o: (0, 0)),
                full,
                pl.BlockSpec((1, width), lambda i, o: (0, 0)),
            ]
            + [pl.BlockSpec(memory_space=pl.ANY)] * count,
            out_specs=[full, full, pl.BlockSpec((tokens, 1), lambda i, o: (0, 0))],
            scratch_shapes=[pltpu.VMEM(weight.shape, LOW) for weight in weights]
            + [pltpu.SemaphoreType.DMA((count,))],
        ),
        out_shape=[
            jax.ShapeDtypeStruct((tokens, width), F32),
            jax.ShapeDtypeStruct((tokens, width), LOW),
            jax.ShapeDtypeStruct((tokens, 1), F32),
        ],
        compiler_params=pltpu.CompilerParams(vmem_limit_bytes=VMEM_LIMIT),
        cost_estimate=lasting(6.0),
        name="mix",
    )(order, o, x, gain, *weights)


def tail_pack_kernel(n, piece, cols, ids_ref, owned_ref, *outs):
    block, start = owned_ref.shape[0], H * HD
    span = start + 2 * KVD
    for s, out_ref in enumerate(outs):
        at = pl.multiple_of(ids_ref[s] * piece, piece)
        out_ref[:block, :] = owned_ref[:, s * cols : (s + 1) * cols]
        row = block
        for lo in range(start, span, cols):
            out_ref[row : row + piece, :] = owned_ref[pl.ds(at, piece), lo : lo + cols]
            row += piece
        gains = owned_ref[pl.ds(at, piece), span : span + 128].astype(F32).T.astype(LOW)
        out_ref[row:, :] = jnp.zeros((16, cols), LOW)
        out_ref[row : row + 16, :piece] = gains[:16]


def tail_pack(ids, owned, piece, cols):
    n, block = ids.shape[0], owned.shape[0]
    height = block + piece * (2 * KVD // cols) + 16
    return pl.pallas_call(
        functools.partial(tail_pack_kernel, n, piece, cols),
        grid_spec=pltpu.PrefetchScalarGridSpec(
            num_scalar_prefetch=1,
            grid=(1,),
            in_specs=[pl.BlockSpec(owned.shape, lambda i, o: (0, 0))],
            out_specs=[pl.BlockSpec((height, cols), lambda i, o: (0, 0))] * n,
        ),
        out_shape=[jax.ShapeDtypeStruct((height, cols), LOW)] * n,
        compiler_params=pltpu.CompilerParams(vmem_limit_bytes=VMEM_LIMIT),
        cost_estimate=lasting(2.0),
        name="tail_pack",
    )(ids, owned)


def tail_adamw_kernel(block, piece, parts, *refs):
    total = ring_sum(*[ref[...] for ref in refs[:parts]])
    states, outs = refs[parts : parts + 9], refs[parts + 9 :]
    groups = 2 * KVD // total.shape[1]
    keyval = [total[block + g * piece : block + (g + 1) * piece] for g in range(groups)]
    weight, first, second = states[:3]
    outs[0][...], outs[1][...], outs[2][...] = adamw(
        weight[...], first[...], second[...], total[:block].T, RATE_OUTPUT, DECAY
    )
    weight, first, second = states[3:6]
    for j in range(2):
        if groups == 1:
            grad = keyval[0][:, j * KVD : (j + 1) * KVD]
        else:
            grad = jnp.concatenate(keyval[j * groups // 2 : (j + 1) * groups // 2], 1)
        outs[3][j], outs[4][j], outs[5][j] = adamw(
            weight[j], first[j], second[j], grad, RATE_KEYVAL, DECAY
        )
    weight, first, second = states[6:]
    outs[6][...], outs[7][...], outs[8][...] = adamw(
        weight[...], first[...], second[...], total[-16:, :piece][:2], RATE_GAINS, 0.0
    )


def tail_adamw(parts, states, block, piece):
    vmem = pl.BlockSpec(memory_space=pltpu.VMEM)
    shapes = [states[3 * i].shape for i in range(3) for _ in range(3)]
    return pl.pallas_call(
        functools.partial(tail_adamw_kernel, block, piece, len(parts)),
        in_specs=[vmem] * (len(parts) + 9),
        out_specs=[vmem] * 9,
        out_shape=[jax.ShapeDtypeStruct(shape, F32) for shape in shapes],
        compiler_params=pltpu.CompilerParams(vmem_limit_bytes=VMEM_LIMIT),
        cost_estimate=lasting(3.0),
        name="tail_adamw",
    )(*parts, *states)


def weight_grad_kernel(count, summed, order_ref, rows_ref, x_ref, *rest):
    out_ref, left = rest[-2:]
    tall = left.shape[0] // count

    @pl.when(pl.program_id(0) == 0)
    def _():
        for i in range(count):
            start = pl.multiple_of(order_ref[i] * tall, tall)
            left[i * tall : (i + 1) * tall, :] = rows_ref[:, pl.ds(start, tall)].T

    grad = contract(left[...], x_ref[...], 1, 1)
    if summed:
        grad = grad + rest[0][...].astype(F32)
    out_ref[...] = grad.astype(LOW)


def weight_grad(
    rows, x_t, total, wide, steps, source, target, order=None, base=None, add=None, place=None
):
    tokens, width = rows.shape
    if order is None:
        order = jnp.arange(width // TALL, dtype=jnp.int32)
    count = order.shape[0]
    out_spec = pl.BlockSpec((count * TALL, wide), lambda i, o: (0, target(i)))
    in_specs = [
        pl.BlockSpec((tokens, width), lambda i, o: (0, 0)),
        pl.BlockSpec((wide, tokens), lambda i, o: (source(i), 0)),
    ]
    args, aliases = [order, rows, x_t], {}
    if add is not None:
        in_specs.append(pl.BlockSpec((count * TALL, wide), lambda i, o: (0, place(i))))
        args.append(add)
    if base is not None:
        in_specs.append(pl.BlockSpec(memory_space=pl.ANY))
        aliases = {len(args): 0}
        args.append(base)
    return pl.pallas_call(
        functools.partial(weight_grad_kernel, count, add is not None),
        grid_spec=pltpu.PrefetchScalarGridSpec(
            num_scalar_prefetch=1,
            grid=(steps,),
            in_specs=in_specs,
            out_specs=out_spec,
            scratch_shapes=[pltpu.VMEM((count * TALL, tokens), LOW)],
        ),
        out_shape=jax.ShapeDtypeStruct((count * TALL, total), LOW),
        input_output_aliases=aliases,
        compiler_params=pltpu.CompilerParams(vmem_limit_bytes=VMEM_LIMIT),
        cost_estimate=lasting(steps * wide * count / 4800),
        name="weight_grad",
    )(*args)


def gain_kernel(gain_ref, base_ref, out_ref):
    out_ref[...] = gain_ref[...].T.astype(LOW)


def put_gains(gain_grads, base, first):
    height = base.shape[0]
    return pl.pallas_call(
        gain_kernel,
        grid=(1,),
        in_specs=[
            pl.BlockSpec((128, height), lambda i: (0, 0)),
            pl.BlockSpec(memory_space=pl.ANY),
        ],
        out_specs=pl.BlockSpec((height, 128), lambda i: (0, first)),
        out_shape=jax.ShapeDtypeStruct(base.shape, LOW),
        input_output_aliases={1: 0},
        compiler_params=pltpu.CompilerParams(vmem_limit_bytes=VMEM_LIMIT),
        cost_estimate=lasting(2.0),
        name="put_gains",
    )(jnp.pad(gain_grads, ((0, 126), (0, 0))), base)


def turned_kernel(x_ref, out_ref):
    out_ref[...] = x_ref[...].T


def turned(x):
    vmem = pl.BlockSpec(memory_space=pltpu.VMEM)
    return pl.pallas_call(
        turned_kernel,
        in_specs=[vmem],
        out_specs=vmem,
        out_shape=jax.ShapeDtypeStruct(x.shape[::-1], x.dtype),
        compiler_params=pltpu.CompilerParams(vmem_limit_bytes=VMEM_LIMIT),
        cost_estimate=lasting(1.5),
        name="turned",
    )(x)


def feed_kernel(pieces, count, *refs):
    rows_refs, grad_refs = refs[:count], refs[count : 2 * count]
    weight_ref, acts_ref, back_ref = refs[2 * count : 2 * count + 3]
    gate_v, up_v, down_v, rows_v, grad_v, sems = refs[2 * count + 3 :]
    copies = []
    for i, here in enumerate(pieces):
        copies.append(
            [
                pltpu.make_async_copy(weight_ref.at[j, :, here], held.at[:, here], sems.at[j, i])
                for j, held in enumerate((gate_v, up_v, down_v))
            ]
        )
        for copy in copies[-1]:
            copy.start()
    tokens = rows_refs[0].shape[0]
    for s in range(count):
        rows_v[s * tokens : (s + 1) * tokens, :] = rows_refs[s][...]
        grad_v[s * tokens : (s + 1) * tokens, :] = grad_refs[s][...]
    for here, (gate_copy, up_copy, down_copy) in zip(pieces, copies):
        gate_copy.wait()
        gate = jnp.dot(rows_v[...], gate_v[:, here], preferred_element_type=F32)
        up_copy.wait()
        up = jnp.dot(rows_v[...], up_v[:, here], preferred_element_type=F32)
        down_copy.wait()
        grad_hidden = jnp.dot(grad_v[...], down_v[:, here], preferred_element_type=F32)
        sigmoid = jax.nn.sigmoid(gate)
        silu = gate * sigmoid
        acts_ref[2, :, here] = (silu * up).astype(LOW)
        acts_ref[1, :, here] = (grad_hidden * silu).astype(LOW)
        acts_ref[0, :, here] = (
            grad_hidden * up * sigmoid * (1.0 + gate * (1.0 - sigmoid))
        ).astype(LOW)
    width = rows_v.shape[1]
    tall = 1024
    for lo in range(0, width, tall):
        some = slice(lo, lo + tall)
        back_ref[:, some] = (
            contract(acts_ref[0], gate_v[some, :], 1, 1)
            + contract(acts_ref[1], up_v[some, :], 1, 1)
        ).astype(LOW)


def feed(rows, grads, weight):
    count = len(rows)
    tokens, width = rows[0].shape
    units = weight.shape[2]
    half = units // 256 * 128 + 128
    pieces = [slice(0, half), slice(half, units)] if units % 128 == 0 else [slice(0, units)]
    vmem = pl.BlockSpec(memory_space=pltpu.VMEM)
    anywhere = pl.BlockSpec(memory_space=pl.ANY)
    total = count * tokens
    return pl.pallas_call(
        functools.partial(feed_kernel, pieces, count),
        in_specs=[vmem] * (2 * count) + [anywhere],
        out_specs=[vmem, vmem],
        out_shape=[
            jax.ShapeDtypeStruct((3, total, units), LOW),
            jax.ShapeDtypeStruct((total, width), LOW),
        ],
        scratch_shapes=[
            pltpu.VMEM((width, units), LOW),
            pltpu.VMEM((width, units), LOW),
            pltpu.VMEM((width, units), LOW),
            pltpu.VMEM((total, width), LOW),
            pltpu.VMEM((total, width), LOW),
            pltpu.SemaphoreType.DMA((3, len(pieces))),
        ],
        compiler_params=pltpu.CompilerParams(vmem_limit_bytes=VMEM_LIMIT),
        cost_estimate=lasting(1.0),
        name="feed",
    )(*rows, *grads, weight)


def feed_grad_kernel(halves, n, *refs):
    acts, rows = refs[:halves], refs[halves : halves + n]
    out_ref, left, right = refs[-3:]
    tokens = rows[0].shape[1]

    @pl.when(pl.program_id(1) == 0)
    def _():
        at = 0
        for act in acts:
            right[at : at + act.shape[1], :] = act[0]
            at += act.shape[1]

    for s in range(n):
        left[:, s * tokens : (s + 1) * tokens] = rows[s][...]
    out_ref[0] = jnp.dot(left[...], right[...], preferred_element_type=F32).astype(LOW)


def feed_grad(acts, rows_t, first, parts, base=None):
    n, halves = len(rows_t), len(acts)
    width, tokens = rows_t[0].shape
    units = acts[0].shape[2]
    tall = 1024
    in_specs = [
        pl.BlockSpec((1, act.shape[1], units), lambda p, r: (first + p, 0, 0)) for act in acts
    ]
    in_specs += [pl.BlockSpec((tall, tokens), lambda p, r: (r, 0))] * n
    args, aliases = list(acts) + list(rows_t), {}
    if base is not None:
        in_specs.append(pl.BlockSpec(memory_space=pl.ANY))
        aliases = {len(args): 0}
        args.append(base)
    return pl.pallas_call(
        functools.partial(feed_grad_kernel, halves, n),
        grid=(parts, width // tall),
        in_specs=in_specs,
        out_specs=pl.BlockSpec((1, tall, units), lambda p, r: (first + p, r, 0)),
        out_shape=jax.ShapeDtypeStruct((3, width, units), LOW),
        scratch_shapes=[
            pltpu.VMEM((tall, n * tokens), LOW),
            pltpu.VMEM((n * tokens, units), LOW),
        ],
        input_output_aliases=aliases,
        compiler_params=pltpu.CompilerParams(vmem_limit_bytes=VMEM_LIMIT),
        cost_estimate=lasting(1.0),
        name="feed_grad",
    )(*args)


def adamw_turned_kernel(rate, weight, first, second, grad, first_out, second_out, weight_out):
    first_out[...], second_out[...], weight_out[...] = adamw(
        weight[...], first[...], second[...], grad[...].astype(F32).T, rate, DECAY
    )


def adamw_turned(weight, first, second, grad, rate):
    rows, cols = weight.shape
    tall = 128 if rows % 128 == 0 else rows
    block = pl.BlockSpec((tall, cols), lambda i: (i, 0))
    return tuple(
        pl.pallas_call(
            functools.partial(adamw_turned_kernel, rate),
            grid=(rows // tall,),
            in_specs=[block] * 3 + [pl.BlockSpec((cols, tall), lambda i: (0, i))],
            out_specs=[block] * 3,
            out_shape=[jax.ShapeDtypeStruct(weight.shape, F32)] * 3,
            compiler_params=pltpu.CompilerParams(vmem_limit_bytes=VMEM_LIMIT),
            cost_estimate=pl.CostEstimate(
                flops=12 * rows * cols, bytes_accessed=28 * rows * cols, transcendentals=0
            ),
            name="adamw_turned",
        )(weight, first, second, grad)
    )


def on_device(
    sizes,
    tokens,
    positions,
    cotangent,
    query_weight,
    query_first,
    query_second,
    keyval_weight,
    keyval_first,
    keyval_second,
    output_weight,
    output_first,
    output_second,
    gateup_weight,
    gateup_first,
    gateup_second,
    down_weight,
    down_first,
    down_second,
    gains,
    gains_first,
    gains_second,
):
    n = sizes["tensor"]
    rank = lax.axis_index("tensor")
    offsets = ring_offsets(n)
    chunk_ids = [(rank + off + n) % n for off in offsets]
    rows, width = tokens.shape
    piece = keyval_weight.shape[1]
    block, cols = query_weight.shape

    keyval_piece = jnp.concatenate(
        [
            keyval_weight[0].astype(LOW),
            keyval_weight[1].astype(LOW),
            jnp.pad(gains.T.astype(LOW), ((0, 0), (0, 126))),
        ],
        1,
    )
    keyval_slots = ring_gather(keyval_piece, n)
    query_slots = ring_gather(query_weight.astype(LOW), n)
    keyval_rows = jnp.zeros((n, piece, keyval_piece.shape[1]), LOW)
    for chunk, held in zip(chunk_ids, keyval_slots):
        keyval_rows = lax.dynamic_update_slice(keyval_rows, held[None], (chunk, 0, 0))
    keyval_rows = keyval_rows.reshape(n * piece, -1)
    attn_in = jnp.concatenate(query_slots + [keyval_rows], 1)
    feed_in = jnp.concatenate(
        [gateup_weight.astype(LOW), down_weight.T.astype(LOW)[None]], 0
    )
    attn_in, feed_in = after(attn_in, feed_in)
    attn_low = lax.all_gather(attn_in, "dp", axis=0, tiled=True)
    output_piece, _ = after(output_weight.T.astype(LOW), (query_slots, keyval_slots))
    output_slots = ring_gather(output_piece, n)
    grad_start, _ = after(cotangent, output_slots)
    grad_slots = ring_gather(grad_start, n, 1)
    feed_in, _ = after(feed_in, output_slots)
    feed_low = lax.all_gather(feed_in, "dp", axis=1, tiled=True)
    out_halves = dp_spread(
        jnp.concatenate(output_slots, 1), sizes["dp"], (attn_low, grad_slots)
    )
    out_order = jnp.concatenate([dp_order(sizes["dp"], block, odd) for odd in (0, 1)])

    span = H * HD + 2 * KVD
    own_positions = lax.dynamic_slice_in_dim(positions, rank * rows, rows, 0)
    freqs = 10000.0 ** (-jnp.arange(0, HD, 2, dtype=F32) / HD)
    angles = freqs[:, None] * own_positions.astype(F32)[None, :]
    cosine, sine = lax.optimization_barrier((jnp.cos(angles), jnp.sin(angles)))
    x = tokens.astype(F32)
    kv_t, first_normalized, gain_rows, first_inverse = begin(tokens, attn_low, cosine, sine)
    first_gain, second_gain = gain_rows[:1], gain_rows[1:2]
    q_t = project(first_normalized, attn_low, cosine, sine)
    kv_slots = jnp.stack(ring_gather(kv_t, n))
    grad_slots, kv_slots = after(grad_slots, kv_slots)
    grad_slots = ring_gather(grad_start, n, n, grad_slots)
    per_block = H // n
    meta = jnp.stack(
        [c * rows for c in chunk_ids]
        + [(c * per_block) // GROUP for c in chunk_ids]
        + [rank * rows]
    ).astype(jnp.int32)
    meta = jnp.concatenate([meta, out_order])
    pos_row = own_positions[None, :]
    mixed_t, mixed, lse = attend(meta, pos_row, q_t, kv_slots, n)
    out_halves, _ = after(out_halves, (mixed, grad_slots))
    out_pieces = out_halves + [swap(held, sizes["dp"], 1) for held in out_halves]
    residual, second_normalized, second_inverse = mix(
        out_order, mixed, tokens, second_gain, out_pieces
    )
    second_normalized, grad_slots = after(second_normalized, grad_slots)

    rows_slots = ring_gather(second_normalized, n, 1)
    grads_t = [turned(x) for x in grad_slots]
    groups = [[s for s in range(n) if abs(offsets[s]) == k] for k in range(n // 2 + 1)]
    order = sum(groups, [])
    rows_t, acts, part_slots, last = [None] * n, [], [None] * n, [grads_t]
    for k, group in enumerate(groups):
        if k == 2:
            rows_slots = ring_gather(second_normalized, n, n, rows_slots)
        chunks, _ = after([rows_slots[s] for s in group], last)
        for i, s in enumerate(group):
            rows_t[s] = turned(chunks[i])
        if k + 1 < len(groups):
            chunks, _ = after(chunks, [rows_t[s] for s in group])
        act, part = feed(chunks, [grad_slots[s] for s in group], feed_low)
        acts.append(act)
        last = part
        for i, s in enumerate(group):
            part_slots[s] = part[i * rows : (i + 1) * rows]
        if k == 0:
            for s in groups[1]:
                rows_slots[s], _ = after(rows_slots[s], part)
    acts, _ = after(acts, last)
    grad_mlp = feed_grad(acts, [rows_t[s] for s in order], 0, 2)
    from_left = ring_way(part_slots, n, 1)
    from_right = ring_way(part_slots, n, -1, None, grad_mlp[0, :8, :128])
    grad_mlp = feed_grad(acts, [grads_t[s] for s in order], 2, 1, grad_mlp)
    second_grad = ring_sum(part_slots[0], from_left, from_right)
    mlp_parts = [contract(act[2], feed_low[2], 1, 1).astype(LOW) for act in acts]
    second_grad, (_, mlp_parts) = after(second_grad, (grad_mlp, mlp_parts))
    owned_mlp = lax.psum_scatter(grad_mlp, "dp", scatter_dimension=1, tiled=True)

    second_unit = residual * second_inverse
    residual_grad = cotangent.astype(F32) + norm_backward(
        second_grad, second_unit, second_inverse, second_gain
    )
    second_gain_grad = jnp.sum(second_grad * second_unit, 0)
    back = residual_grad.astype(LOW)
    mlp_slots = [None] * n
    for group, part in zip(groups, mlp_parts):
        for i, s in enumerate(group):
            mlp_slots[s] = part[i * rows : (i + 1) * rows]
    block_far, block_left = ring_most(mlp_slots, n), ring_way(mlp_slots, n, 1)
    grad_q_t, grad_kv = attend_back(
        meta, pos_row, q_t, kv_slots, back, out_pieces, mixed_t, lse, cosine, sine, n
    )
    (grad_q_t, grad_kv), _ = after((grad_q_t, grad_kv), (block_far, block_left))

    places = [dp_order(sizes["dp"], block, odd) for odd in (0, 1)]
    partner = swap(
        weight_grad(
            first_normalized, grad_q_t, n * cols, cols, n, lambda i: i, lambda i: i, places[1]
        ),
        sizes["dp"],
        1,
    )
    kv_parts = [grad_kv[s] for s in range(n)]
    own_kv = ring_scatter(kv_parts, n)
    out_rows, _ = after(back, grad_q_t)
    held_cols, heads_cols = attn_low.shape[1], H * HD // (2 * KVD)
    grad_pack = weight_grad(
        out_rows, mixed_t, held_cols, 2 * KVD, heads_cols, lambda i: i, lambda i: i
    )
    own_kv, _ = after(own_kv, partner)
    grad_k = own_kv[:KVD].reshape(KVH, 2, HD // 2, rows)
    upper, lower = grad_k[:, 0], grad_k[:, 1]
    grad_k = jnp.stack([upper * cosine + lower * sine, lower * cosine - upper * sine], 1)
    grad_kv_t = jnp.concatenate(
        [grad_k.reshape(KVD, rows).astype(LOW), own_kv[KVD:].astype(LOW)], 0
    )
    grad_pack = weight_grad(
        first_normalized, grad_kv_t, held_cols, 2 * KVD, 1, lambda i: 0, lambda i: heads_cols,
        None, grad_pack,
    )
    grad_qkv_t = jnp.concatenate(
        [grad_q_t, grad_kv_t, jnp.zeros((held_cols - span, rows), LOW)], 0
    )
    first_grad = contract(grad_qkv_t, attn_low, 0, 1)
    first_unit = x * first_inverse
    first_gain_grad = jnp.sum(first_grad * first_unit, 0)
    grad_pack = put_gains(
        jnp.stack([first_gain_grad, second_gain_grad]), grad_pack, span // 128
    )
    grad_pack, owned_mlp = after(grad_pack, owned_mlp)
    owned_pack = lax.psum_scatter(grad_pack, "dp", scatter_dimension=0, tiled=True)
    layer_input_gradient = residual_grad + norm_backward(
        first_grad, first_unit, first_inverse, first_gain
    )

    query_slots, last = [None] * n, grad_pack
    for s in order[::-1]:
        query_rows, _ = after(first_normalized, last)
        last = query_slots[s] = weight_grad(
            query_rows, grad_q_t, cols, cols, 1, lambda i, s=s: s, lambda i: 0, places[0], None,
            partner, lambda i, s=s: s,
        )
    query_far, query_left = ring_most(query_slots, n), ring_way(query_slots, n, 1)
    query_right = ring_last(query_slots, n, query_far)
    query_sum = ring_sum(query_slots[0], query_left, query_right).astype(LOW)
    block_right = ring_last(mlp_slots, n, block_far, query_right)
    block_out = residual + ring_sum(mlp_slots[0], block_left, block_right)

    owned_gateup, owned_down = owned_mlp[:2], owned_mlp[2]
    gateup_up = adamw(
        gateup_weight, gateup_first, gateup_second, owned_gateup.astype(F32), RATE_GATEUP, DECAY
    )
    down_up = adamw_turned(down_weight, down_first, down_second, owned_down, RATE_DOWN)
    own_query = dp_scatter(query_sum, sizes["dp"], (gateup_up, down_up)).astype(F32)
    query_up = adamw(query_weight, query_first, query_second, own_query, RATE_QUERY, DECAY)

    slots = tail_pack(jnp.stack(chunk_ids).astype(jnp.int32), owned_pack, piece, cols)
    parts = [slots[0], ring_way(slots, n, -1), ring_way(slots, n, 1)]
    states = [output_weight, output_first, output_second, keyval_weight, keyval_first]
    states += [keyval_second, gains, gains_first, gains_second]
    parts = [part for part in parts if part is not None]
    last = tail_adamw(parts, states, block, piece)
    output_up, keyval_up, gains_up = tuple(last[:3]), tuple(last[3:6]), tuple(last[6:])
    return (
        (block_out, layer_input_gradient)
        + query_up
        + keyval_up
        + output_up
        + gateup_up
        + down_up
        + gains_up
    )


def solution(mesh):
    rows = P(("dp", "tensor"), None)
    grid = P("dp", "tensor")
    cross = P("tensor", "dp")
    pair = P(None, ("dp", "tensor"), None)
    stacked = P(None, "dp", "tensor")
    narrow = P(None, ("dp", "tensor"))
    states = (grid,) * 3 + (pair,) * 3 + (cross,) * 3 + (stacked,) * 3 + (cross,) * 3 + (narrow,) * 3
    return jax.shard_map(
        functools.partial(on_device, dict(mesh.shape)),
        mesh=mesh,
        in_specs=(rows, P("dp"), rows) + states,
        out_specs=(rows, rows) + states,
        check_vma=False,
    )
```

time: 1880 us -> 618 us (0.33)
  waiting for transfers between devices: 1390 us -> 193 us
  Pallas kernels: 0 us -> 242 us
  matrix products: 219 us -> 28.5 us
  blocking collectives: 69.3 us -> 0 us
  starting transfers between devices: 1.58 us -> 69.2 us
  local copies, waits for them, and re-layouts: 80.3 us -> 20.2 us
  other arithmetic: 99 us -> 43.7 us
    reduce_scatter x9 -> x2, waiting for transfers between devices: 831 us -> 0.02 us  [the longest x1 0.02 us: on_device(): lax.psum_scatter(grad_pack, 'dp', scatter_dimension=0, tiled=True)]
    all_gather x9 -> x2, waiting for transfers between devices: 423 us -> 57.3 us  [the longest x1 40.1 us: on_device(): attn_low = lax.all_gather(attn_in, 'dp', axis=0, tiled=True)]
    pallas_call x0 -> x29, Pallas kernels: none -> 242 us  [the longest x3 56 us: feed(): pl.pallas_call(functools.partial(feed_kernel, pieces, count), in_specs=[v...]
    dot_general x35 -> x4, matrix products: 219 us -> 28.5 us  [contract(): lax.dot_general(left, right, (((dim_left,), (dim_right,)), ((), ())), pre...]
    ppermute x0 -> x44, waiting for transfers between devices: none -> 136 us  [the longest x33 119 us: shift(): return lax.ppermute(x, 'tensor', [(i, (i + by) % n) for i in range(n)])]
    unnamed x20 -> x4, waiting for transfers between devices: 133 us -> 0.07 us
    all_gather x1 -> x0, blocking collectives: 69.3 us -> none  [on_device(): lax.all_gather(gains.astype(jnp.bfloat16), ('dp', 'tensor'), axis=1, tile...]
    ppermute x0 -> x44, starting transfers between devices: none -> 69.1 us  [the longest x33 58.9 us: shift(): return lax.ppermute(x, 'tensor', [(i, (i + by) % n) for i in range(n)])]
  transfers between devices with their start and end apart: 19 -> 48, of which waited for: 14 -> 22; matrix products, arithmetic and copies ran while one was open for 18% -> 14% of each run, Pallas kernels for 0% -> 37%
where the time goes in v1:
time: 618 us; the launch traced here: 611 us
  Pallas kernels  242 us (39%)
  waiting for transfers between devices  193 us (31%)
  starting transfers between devices  69.2 us (11%)
  other arithmetic  43.7 us (7%)
  matrix products  28.5 us (5%)
  local copies, waits for them, and re-layouts  20.2 us (3%)
  between operations  15 us (2%)
    ppermute x33, waiting for transfers between devices, shift(): return lax.ppermute(x, 'tensor', [(i, (i + by) % n) for i in range(n)])  119 us
    ppermute x33, starting transfers between devices, shift(): return lax.ppermute(x, 'tensor', [(i, (i + by) % n) for i in range(n)])  58.9 us
    pallas_call x3, Pallas kernels, feed(): pl.pallas_call(functools.partial(feed_kernel, pieces, count), in_specs=[v...  56 us
    pallas_call x1, Pallas kernels, attend_back(): pl.pallas_call(functools.partial(attend_back_kernel, slots, heads, len(we...  40.4 us
    all_gather x1, waiting for transfers between devices, on_device(): attn_low = lax.all_gather(attn_in, 'dp', axis=0, tiled=True)  40.1 us
    pallas_call x7, Pallas kernels, weight_grad(): pl.pallas_call(functools.partial(weight_grad_kernel, count, add is not No...  34.6 us
    pallas_call x2, Pallas kernels, feed_grad(): pl.pallas_call(functools.partial(feed_grad_kernel, halves, n), grid=(part...  29.5 us
    dot_general x4, matrix products, contract(): lax.dot_general(left, right, (((dim_left,), (dim_right,)), ((), ())), pre...  28.5 us
  transfers between devices with their start and end apart: 48, of which 22 were waited for; matrix products, arithmetic and copies ran while one was open for 14% of the time, Pallas kernels for 37%

profile of v1, /device:TPU:0, one launch (start us, length us, event | category | flops | bytes accessed | tf_op | source)
XLA Modules:
  0.0 611.1 jit_solution(5132094686377208394)
XLA Ops:
  50.0 7.2 %collective-permute-done.6 = bf16[256,512]{1,0:T(8,128)(2,1)S(1)} collective-permute-done((bf16[256,512]{1,0:T(8,128)(2,1)S(1)}, bf16[256,512]{1,0:T(8,128)(2,1)S(1)}, u32[]{:S(2)}, u32[]{:S(2)}) %collective-permute-start.6) | collective-permute-done | bytes 262176 | tf_op jit(solution)/shard_map/ppermute | solution.py:49
  74.2 40.1 %all-gather.3.cloned.1.call-done.gain_ref.weight_ref = bf16[2048,2688]{1,0:T(8,128)(2,1)} async-done(((bf16[256,2688]{1,0:T(8,128)(2,1)}), bf16[2048,2688]{1,0:T(8,128)(2,1)}) %all-gather.3.cloned.1.call-update) | async-done | bytes 11010064 | tf_op jit(solution)/shard_map/all_gather | solution.py:841
  129.4 7.0 %project.1.q_ref = bf16[2048,256]{1,0:T(8,128)(2,1)} custom-call(bf16[256,2048]{1,0:T(8,128)(2,1)} %get-tuple-element.164.rows_ref, bf16[2048,2688]{1,0:T(8,128)(2,1)} %all-gather.3.cloned.1.call-done.gain_ref.weight_ref, f32[32,256]{1,0:T(8,128)} %get-tuple-element.103.cos_ref.refs_6_, f32[32,256]{1,0:T(8,128)} %get-tuple-element.104.sin_ref.refs_7_), custom_call_target="tpu_custom_call" | custom-call | flops 9200000000 | bytes 1000000 | tf_op jit(solution)/shard_map/project/pallas_call | solution.py:244
  141.2 22.0 %attend.1 = (bf16[2048,256]{1,0:T(8,128)(2,1)}, bf16[256,2048]{1,0:T(8,128)(2,1)}, f32[4,8,256]{2,1,0:T(8,128)}) custom-call(s32[25]{0:T(128)} %concatenate.42.meta_ref, s32[1,256]{1,0:T(1,128)} %bitcast.115, bf16[2048,256]{1,0:T(8,128)(2,1)} %project.1.q_ref, bf16[4,512,256]{2,1,0:T(8,128)(2,1)} %pad_maximum_fusion.3.kv_ref), custom_call_target="tpu_custom_call" | custom-call | flops 8589934592 | bytes 2097152 | tf_op jit(solution)/shard_map/attend/pallas_call | solution.py:304
  163.3 8.3 %collective-permute-done.16 = bf16[256,2048]{1,0:T(8,128)(2,1)S(1)} collective-permute-done((bf16[256,2048]{1,0:T(8,128)(2,1)S(1)}, bf16[256,2048]{1,0:T(8,128)(2,1)S(1)}, u32[]{:S(2)}, u32[]{:S(2)}) %collective-permute-start.16) | collective-permute-done | bytes 1048608 | tf_op jit(solution)/shard_map/ppermute | solution.py:116
  184.4 8.9 %mix.1 = (f32[256,2048]{1,0:T(8,128)}, bf16[256,2048]{1,0:T(8,128)(2,1)}, f32[256,1]{1,0:T(8,128)}) custom-call(s32[16]{0:T(128)} %concatenate.41.order_ref, bf16[256,2048]{1,0:T(8,128)(2,1)} %get-tuple-element.110.o_ref, bf16[256,2048]{1,0:T(8,128)(2,1)} %x_ref.3, f32[1,2048]{1,0:T(1,128)} %get-tuple-element.211.gain_ref, bf16[512,2048]{1,0:T(8,128)(2,1)} %copy-done.17, ...), custom_call_target="tpu_custom_call" | custom-call | flops 6899999744 | bytes 1000000 | tf_op jit(solution)/shard_map/mix/pallas_call | solution.py:454
  210.2 17.2 %all-gather.5.cloned.1.call-done.refs_2_.refs_4_ = bf16[3,2048,1408]{2,1,0:T(8,128)(2,1)} async-done(((bf16[3,256,1408]{2,1,0:T(8,128)(2,1)}), bf16[3,2048,1408]{2,1,0:T(8,128)(2,1)}) %all-gather.5.cloned.1.call-update) | async-done | bytes 17301520 | tf_op jit(solution)/shard_map/all_gather | solution.py:847
  227.5 14.8 %feed.3 = (bf16[3,256,1408]{2,1,0:T(8,128)(2,1)}, bf16[256,2048]{1,0:T(8,128)(2,1)}) custom-call(bf16[256,2048]{1,0:T(8,128)(2,1)} %get-tuple-element.126.x_ref.refs_0_, bf16[256,2048]{1,0:T(8,128)(2,1)} %refs_1_, bf16[3,2048,1408]{2,1,0:T(8,128)(2,1)} %all-gather.5.cloned.1.call-done.refs_2_.refs_4_), custom_call_target="tpu_custom_call" | custom-call | flops 1150000000 | bytes 1000000 | tf_op jit(solution)/shard_map/feed/pallas_call | solution.py:694
  249.7 26.3 %feed.4 = (bf16[3,512,1408]{2,1,0:T(8,128)(2,1)}, bf16[512,2048]{1,0:T(8,128)(2,1)}) custom-call(bf16[256,2048]{1,0:T(8,128)(2,1)} %copy-done.27, bf16[256,2048]{1,0:T(8,128)(2,1)} %copy-done.28, bf16[256,2048]{1,0:T(8,128)(2,1)} %collective-permute-done.9.x_ref.refs_2_, bf16[256,2048]{1,0:T(8,128)(2,1)} %copy-done.26, ...), custom_call_target="tpu_custom_call" | custom-call | flops 1150000000 | bytes 1000000 | tf_op jit(solution)/shard_map/feed/pallas_call | solution.py:694
  277.1 14.9 %feed.5 = (bf16[3,256,1408]{2,1,0:T(8,128)(2,1)}, bf16[256,2048]{1,0:T(8,128)(2,1)}) custom-call(bf16[256,2048]{1,0:T(8,128)(2,1)} %copy-done.24, bf16[256,2048]{1,0:T(8,128)(2,1)} %copy-done.23, bf16[3,2048,1408]{2,1,0:T(8,128)(2,1)} %all-gather.5.cloned.1.call-done.refs_2_.refs_4_), custom_call_target="tpu_custom_call" | custom-call | flops 1150000000 | bytes 1000000 | tf_op jit(solution)/shard_map/feed/pallas_call | solution.py:694
  298.9 18.3 %feed_grad.2.refs_7_ = bf16[3,2048,1408]{2,1,0:T(8,128)(2,1)} custom-call(bf16[3,256,1408]{2,1,0:T(8,128)(2,1)} %get-tuple-element.142.refs_0_, bf16[3,512,1408]{2,1,0:T(8,128)(2,1)} %get-tuple-element.143.refs_1_, bf16[3,256,1408]{2,1,0:T(8,128)(2,1)} %get-tuple-element.144.refs_2_, bf16[2048,256]{1,0:T(8,128)(2,1)} %turned.12.refs_3_, ...), custom_call_target="tpu_custom_call" | custom-call | flops 1150000000 | bytes 1000000 | tf_op jit(solution)/shard_map/feed_grad/pallas_call | solution.py:747
  317.2 11.2 %feed_grad.3 = bf16[3,2048,1408]{2,1,0:T(8,128)(2,1)} custom-call(bf16[3,256,1408]{2,1,0:T(8,128)(2,1)} %get-tuple-element.142.refs_0_, bf16[3,512,1408]{2,1,0:T(8,128)(2,1)} %get-tuple-element.143.refs_1_, bf16[3,256,1408]{2,1,0:T(8,128)(2,1)} %get-tuple-element.144.refs_2_, bf16[2048,256]{1,0:T(8,128)(2,1)} %turned.8.refs_3_, ...), custom_call_target="tpu_custom_call", output_to_operand_aliasing={{}: (7, {})} | custom-call | flops 1150000000 | bytes 1000000 | tf_op jit(solution)/shard_map/feed_grad/pallas_call | solution.py:747
  339.7 6.8 %fusion.7 = bf16[256,2048]{1,0:T(8,128)(2,1)} fusion(bf16[3,2048,1408]{2,1,0:T(8,128)(2,1)} %all-gather.5.cloned.1.call-done.refs_2_.refs_4_, bf16[3,256,1408]{2,1,0:T(8,128)(2,1)} %get-tuple-element.144.refs_2_), kind=kOutput, calls=%fused_computation.11 | convolution fusion | flops 1476919296 | bytes 7536640 | tf_op jit(solution)/shard_map/dot_general | solution.py:39
  346.6 7.9 %fusion.3 = bf16[512,2048]{1,0:T(8,128)(2,1)S(1)} fusion(bf16[3,2048,1408]{2,1,0:T(8,128)(2,1)} %all-gather.5.cloned.1.call-done.refs_2_.refs_4_, bf16[3,512,1408]{2,1,0:T(8,128)(2,1)} %get-tuple-element.143.refs_1_), kind=kOutput, calls=%fused_computation.6 | convolution fusion | flops 2953838592 | bytes 9306112 | tf_op jit(solution)/shard_map/dot_general | solution.py:39
  354.5 9.6 %collective-permute-done.26 = bf16[256,2048]{1,0:T(8,128)(2,1)S(1)} collective-permute-done((bf16[256,2048]{1,0:T(8,128)(2,1)S(1)}, bf16[256,2048]{1,0:T(8,128)(2,1)S(1)}, u32[]{:S(2)}, u32[]{:S(2)}) %collective-permute-start.26) | collective-permute-done | bytes 1048608 | tf_op jit(solution)/shard_map/ppermute | solution.py:49
  373.6 40.4 %attend_back.1 = (bf16[2048,256]{1,0:T(8,128)(2,1)}, bf16[4,512,256]{2,1,0:T(8,128)(2,1)}) custom-call(s32[25]{0:T(128)} %concatenate.42.meta_ref, s32[1,256]{1,0:T(1,128)} %bitcast.116, bf16[2048,256]{1,0:T(8,128)(2,1)} %project.1.q_ref, bf16[4,512,256]{2,1,0:T(8,128)(2,1)} %pad_maximum_fusion.3.kv_ref, bf16[256,2048]{1,0:T(8,128)(2,1)} %fusion.29.back_ref.rows_ref, ...), custom_call_target="tpu_custom_call" | custom-call | flops 200000000753664 | bytes 1000000 | tf_op jit(solution)/shard_map/attend_back/pallas_call | solution.py:395
  426.4 6.5 %collective-permute-done.29 = bf16[512,256]{1,0:T(8,128)(2,1)S(1)} collective-permute-done((bf16[512,256]{1,0:T(8,128)(2,1)S(1)}, bf16[512,256]{1,0:T(8,128)(2,1)S(1)}, u32[]{:S(2)}, u32[]{:S(2)}) %collective-permute-start.29) | collective-permute-done | bytes 262176 | tf_op jit(solution)/shard_map/ppermute | solution.py:49
  437.6 7.8 %weight_grad.8.rest_0_ = bf16[2048,2688]{1,0:T(8,128)(2,1)} custom-call(s32[16]{0:T(128)} %iota.13.order_ref, bf16[256,2048]{1,0:T(8,128)(2,1)} %fusion.29.back_ref.rows_ref, bf16[2048,256]{1,0:T(8,128)(2,1)} %get-tuple-element.150.refs_4_.x_ref), custom_call_target="tpu_custom_call" | custom-call | flops 7850666496 | bytes 1000000 | tf_op jit(solution)/shard_map/weight_grad/pallas_call | solution.py:587
  451.9 8.2 %multiply_reduce_fusion = (f32[256]{0:T(256)S(1)}, f32[2048]{0:T(1024)S(1)}, f32[256,2048]{1,0:T(8,128)S(1)}) fusion(bf16[256,2048]{1,0:T(8,128)(2,1)S(1)} %copy-done.10, f32[2048]{0:T(1024)S(1)} %bitcast.111, f32[256]{0:T(256)S(1)} %reduce.1, bf16[2048,2688]{1,0:T(8,128)(2,1)} %all-gather.3.cloned.1.call-done.gain_ref.weight_ref, ...), kind=kOutput, calls=%fused_computation.17 | convolution fusion | flops 2827745024 | bytes 15490304 | tf_op jit(solution)/shard_map/dot_general | solution.py:39
  485.6 8.5 %collective-permute-done.33 = bf16[1024,512]{1,0:T(8,128)(2,1)} collective-permute-done((bf16[1024,512]{1,0:T(8,128)(2,1)}, bf16[1024,512]{1,0:T(8,128)(2,1)}, u32[]{:S(2)}, u32[]{:S(2)}) %collective-permute-start.33) | collective-permute-done | bytes 1048608 | tf_op jit(solution)/shard_map/ppermute | solution.py:49
  505.7 10.8 %collective-permute-done.36 = bf16[1024,512]{1,0:T(8,128)(2,1)} collective-permute-done((bf16[1024,512]{1,0:T(8,128)(2,1)}, bf16[1024,512]{1,0:T(8,128)(2,1)}, u32[]{:S(2)}, u32[]{:S(2)}) %collective-permute-start.36) | collective-permute-done | bytes 1048608 | tf_op jit(solution)/shard_map/ppermute | solution.py:49
  516.5 21.3 %collective-permute-done.34 = bf16[1024,512]{1,0:T(8,128)(2,1)S(1)} collective-permute-done((bf16[1024,512]{1,0:T(8,128)(2,1)S(1)}, bf16[1024,512]{1,0:T(8,128)(2,1)S(1)}, u32[]{:S(2)}, u32[]{:S(2)}) %collective-permute-start.34) | collective-permute-done | bytes 1048608 | tf_op jit(solution)/shard_map/ppermute | solution.py:49
  542.5 8.9 %adamw_turned.1 = (f32[1408,256]{1,0:T(8,128)}, f32[1408,256]{1,0:T(8,128)}, f32[1408,256]{1,0:T(8,128)}) custom-call(f32[1408,256]{1,0:T(8,128)} %weight.1, f32[1408,256]{1,0:T(8,128)} %first.1, f32[1408,256]{1,0:T(8,128)} %second.1, bf16[256,1408]{1,0:T(8,128)(2,1)} %slice_bitcast_fusion.10.grad), custom_call_target="tpu_custom_call" | custom-call | flops 4325376 | bytes 10092544 | tf_op jit(solution)/shard_map/adamw_turned/pallas_call | solution.py:775
  566.3 22.1 %collective-permute-done.41 = bf16[336,512]{1,0:T(8,128)(2,1)S(1)} collective-permute-done((bf16[336,512]{1,0:T(8,128)(2,1)}, bf16[336,512]{1,0:T(8,128)(2,1)S(1)}, u32[]{:S(2)}, u32[]{:S(2)}) %collective-permute-start.41) | collective-permute-done | bytes 344096 | tf_op jit(solution)/shard_map/ppermute | solution.py:49
  (280 shorter events, 241.0 us)
Async XLA Ops:
  7.2 107.0 %all-gather.3.cloned.1.call-start = ((), (), s32[]{:S(2)}) async-start(), calls=%async_computation.2 | async-start | bytes 12386304 | tf_op jit(solution)/shard_map/all_gather | solution.py:841
  16.7 27.1 %collective-permute-start.2 = (bf16[256,512]{1,0:T(8,128)(2,1)}, bf16[256,512]{1,0:T(8,128)(2,1)}, u32[]{:S(2)}, u32[]{:S(2)}) collective-permute-start(bf16[256,512]{1,0:T(8,128)(2,1)} %get-tuple-element.197), channel_id=1, source_target_pairs={{0,3},{1,0},{2,1},{3,2},{4,7},{5,4},{6,5},{7,6},{8,11},{9,8},{10,9... | collective-permute-start | bytes 786440 | tf_op jit(solution)/shard_map/ppermute | solution.py:49
  45.9 181.6 %all-gather.5.cloned.1.call-start = ((), (), s32[]{:S(2)}) async-start(), calls=%async_computation.3 | async-start | bytes 19464192 | tf_op jit(solution)/shard_map/all_gather | solution.py:847
  65.7 397.8 %reduce-scatter.3.cloned.1.call-start = ((), (), s32[]{:S(2)}) async-start(), calls=%async_computation.4 | async-start | bytes 19464192 | tf_op jit(solution)/shard_map/reduce_scatter | solution.py:910
  68.8 55.5 %collective-permute-start.10 = (bf16[256,2048]{1,0:T(8,128)(2,1)S(1)}, bf16[256,2048]{1,0:T(8,128)(2,1)S(1)}, u32[]{:S(2)}, u32[]{:S(2)}) collective-permute-start(bf16[256,2048]{1,0:T(8,128)(2,1)S(1)} %copy-done.7), channel_id=1, source_target_pairs={{0,3},{1,0},{2,1},{3,2},{4,7},{5,4},{6,5},{7,6},{8,11},{9,8},{10,9... | collective-permute-start | bytes 3145736 | tf_op jit(solution)/shard_map/ppermute | solution.py:49
  68.9 55.5 %collective-permute-start.9 = (bf16[256,2048]{1,0:T(8,128)(2,1)S(1)}, bf16[256,2048]{1,0:T(8,128)(2,1)}, u32[]{:S(2)}, u32[]{:S(2)}) collective-permute-start(bf16[256,2048]{1,0:T(8,128)(2,1)S(1)} %copy-done.7), channel_id=1, source_target_pairs={{0,1},{1,2},{2,3},{3,0},{4,5},{5,6},{6,7},{7,4},{8,9},{9,10},{10,1... | collective-permute-start | bytes 3145736 | tf_op jit(solution)/shard_map/ppermute | solution.py:49
  71.1 47.7 %collective-permute-start.15 = (bf16[128,2048]{1,0:T(8,128)(2,1)S(1)}, bf16[128,2048]{1,0:T(8,128)(2,1)}, u32[]{:S(2)}, u32[]{:S(2)}) collective-permute-start(bf16[128,2048]{1,0:T(8,128)(2,1)S(1)} %get-tuple-element.206), channel_id=1, source_target_pairs={{0,16},{4,20},{8,24},{12,28},{16,0},{20,4},{24,8},{28,12},{1,17},{... | collective-permute-start | bytes 1572872 | tf_op jit(solution)/shard_map/ppermute | solution.py:116
  72.7 47.3 %collective-permute-start.14 = (bf16[128,2048]{1,0:T(8,128)(2,1)S(1)}, bf16[128,2048]{1,0:T(8,128)(2,1)}, u32[]{:S(2)}, u32[]{:S(2)}) collective-permute-start(bf16[128,2048]{1,0:T(8,128)(2,1)S(1)} %get-tuple-element.207), channel_id=1, source_target_pairs={{0,8},{4,12},{8,0},{12,4},{16,24},{20,28},{24,16},{28,20},{1,9},{5... | collective-permute-start | bytes 1572872 | tf_op jit(solution)/shard_map/ppermute | solution.py:116
  124.4 47.2 %collective-permute-start.16 = (bf16[256,2048]{1,0:T(8,128)(2,1)S(1)}, bf16[256,2048]{1,0:T(8,128)(2,1)S(1)}, u32[]{:S(2)}, u32[]{:S(2)}) collective-permute-start(bf16[256,2048]{1,0:T(8,128)(2,1)S(1)} %pad_maximum_fusion.4), channel_id=1, source_target_pairs={{0,16},{4,20},{8,24},{12,28},{16,0},{20,4},{24,8},{28,12},{1,17},{... | collective-permute-start | bytes 3145736 | tf_op jit(solution)/shard_map/ppermute | solution.py:116
  125.2 47.4 %collective-permute-start.17 = (bf16[256,2048]{1,0:T(8,128)(2,1)S(1)}, bf16[256,2048]{1,0:T(8,128)(2,1)S(1)}, u32[]{:S(2)}, u32[]{:S(2)}) collective-permute-start(bf16[256,2048]{1,0:T(8,128)(2,1)S(1)} %pad_maximum_fusion.5), channel_id=1, source_target_pairs={{0,8},{4,12},{8,0},{12,4},{16,24},{20,28},{24,16},{28,20},{1,9},{5... | collective-permute-start | bytes 3145736 | tf_op jit(solution)/shard_map/ppermute | solution.py:116
  141.0 33.2 %collective-permute-start.18 = (bf16[256,2048]{1,0:T(8,128)(2,1)}, bf16[256,2048]{1,0:T(8,128)(2,1)S(1)}, u32[]{:S(2)}, u32[]{:S(2)}) collective-permute-start(bf16[256,2048]{1,0:T(8,128)(2,1)} %collective-permute-done.9.x_ref.refs_2_), channel_id=1, source_target_pairs={{0,1},{1,2},{2,3},{3,0},{4,5},{5,6},{6,7},{7,4},{8,9},{9,10},{10,1... | collective-permute-start | bytes 3145736 | tf_op jit(solution)/shard_map/ppermute | solution.py:49
  193.3 49.0 %collective-permute-start.21 = (bf16[256,2048]{1,0:T(8,128)(2,1)}, bf16[256,2048]{1,0:T(8,128)(2,1)S(1)}, u32[]{:S(2)}, u32[]{:S(2)}) collective-permute-start(bf16[256,2048]{1,0:T(8,128)(2,1)} %get-tuple-element.126.x_ref.refs_0_), channel_id=1, source_target_pairs={{0,1},{1,2},{2,3},{3,0},{4,5},{5,6},{6,7},{7,4},{8,9},{9,10},{10,1... | collective-permute-start | bytes 3145736 | tf_op jit(solution)/shard_map/ppermute | solution.py:49
  193.4 50.9 %collective-permute-start.22 = (bf16[256,2048]{1,0:T(8,128)(2,1)}, bf16[256,2048]{1,0:T(8,128)(2,1)S(1)}, u32[]{:S(2)}, u32[]{:S(2)}) collective-permute-start(bf16[256,2048]{1,0:T(8,128)(2,1)} %get-tuple-element.126.x_ref.refs_0_), channel_id=1, source_target_pairs={{0,3},{1,0},{2,1},{3,2},{4,7},{5,4},{6,5},{7,6},{8,11},{9,8},{10,9... | collective-permute-start | bytes 3145736 | tf_op jit(solution)/shard_map/ppermute | solution.py:49
  242.3 33.8 %collective-permute-start.24 = (bf16[256,2048]{1,0:T(8,128)(2,1)S(1)}, bf16[256,2048]{1,0:T(8,128)(2,1)S(1)}, u32[]{:S(2)}, u32[]{:S(2)}) collective-permute-start(bf16[256,2048]{1,0:T(8,128)(2,1)S(1)} %collective-permute-done.21.x_ref.refs_0_), channel_id=1, source_target_pairs={{0,1},{1,2},{2,3},{3,0},{4,5},{5,6},{6,7},{7,4},{8,9},{9,10},{10,1... | collective-permute-start | bytes 3145736 | tf_op jit(solution)/shard_map/ppermute | solution.py:49
  292.0 42.2 %collective-permute-start.25 = (bf16[256,2048]{1,0:T(8,128)(2,1)}, bf16[256,2048]{1,0:T(8,128)(2,1)}, u32[]{:S(2)}, u32[]{:S(2)}) collective-permute-start(bf16[256,2048]{1,0:T(8,128)(2,1)} %get-tuple-element.138), channel_id=1, source_target_pairs={{0,3},{1,0},{2,1},{3,2},{4,7},{5,4},{6,5},{7,6},{8,11},{9,8},{10,9... | collective-permute-start | bytes 3145736 | tf_op jit(solution)/shard_map/ppermute | solution.py:49
  296.2 58.3 %collective-permute-start.23 = (bf16[256,2048]{1,0:T(8,128)(2,1)}, bf16[256,2048]{1,0:T(8,128)(2,1)S(1)}, u32[]{:S(2)}, u32[]{:S(2)}) collective-permute-start(bf16[256,2048]{1,0:T(8,128)(2,1)} %slice.113), channel_id=1, source_target_pairs={{0,1},{1,2},{2,3},{3,0},{4,5},{5,6},{6,7},{7,4},{8,9},{9,10},{10,1... | collective-permute-start | bytes 3145736 | tf_op jit(solution)/shard_map/ppermute | solution.py:49
  328.4 229.8 %reduce-scatter.5.cloned.1.call-start = ((), (), s32[]{:S(2)}) async-start(), calls=%async_computation.5 | async-start | bytes 12386304 | tf_op jit(solution)/shard_map/reduce_scatter | solution.py:964
  335.9 28.2 %collective-permute-start.26 = (bf16[256,2048]{1,0:T(8,128)(2,1)S(1)}, bf16[256,2048]{1,0:T(8,128)(2,1)S(1)}, u32[]{:S(2)}, u32[]{:S(2)}) collective-permute-start(bf16[256,2048]{1,0:T(8,128)(2,1)S(1)} %add_convert_fusion.3), channel_id=1, source_target_pairs={{0,3},{1,0},{2,1},{3,2},{4,7},{5,4},{6,5},{7,6},{8,11},{9,8},{10,9... | collective-permute-start | bytes 3145736 | tf_op jit(solution)/shard_map/ppermute | solution.py:49
  369.4 44.7 %collective-permute-start.27 = (bf16[256,2048]{1,0:T(8,128)(2,1)}, bf16[256,2048]{1,0:T(8,128)(2,1)}, u32[]{:S(2)}, u32[]{:S(2)}) collective-permute-start(bf16[256,2048]{1,0:T(8,128)(2,1)} %slice.119), channel_id=1, source_target_pairs={{0,1},{1,2},{2,3},{3,0},{4,5},{5,6},{6,7},{7,4},{8,9},{9,10},{10,1... | collective-permute-start | bytes 3145736 | tf_op jit(solution)/shard_map/ppermute | solution.py:49
  369.9 48.0 %collective-permute-start.28 = (bf16[256,2048]{1,0:T(8,128)(2,1)}, bf16[256,2048]{1,0:T(8,128)(2,1)}, u32[]{:S(2)}, u32[]{:S(2)}) collective-permute-start(bf16[256,2048]{1,0:T(8,128)(2,1)} %fusion.7), channel_id=1, source_target_pairs={{0,3},{1,0},{2,1},{3,2},{4,7},{5,4},{6,5},{7,6},{8,11},{9,8},{10,9... | collective-permute-start | bytes 3145736 | tf_op jit(solution)/shard_map/ppermute | solution.py:49
  477.5 39.1 %collective-permute-start.36 = (bf16[1024,512]{1,0:T(8,128)(2,1)}, bf16[1024,512]{1,0:T(8,128)(2,1)}, u32[]{:S(2)}, u32[]{:S(2)}) collective-permute-start(bf16[1024,512]{1,0:T(8,128)(2,1)} %weight_grad.11), channel_id=1, source_target_pairs={{0,1},{1,2},{2,3},{3,0},{4,5},{5,6},{6,7},{7,4},{8,9},{9,10},{10,1... | collective-permute-start | bytes 3145736 | tf_op jit(solution)/shard_map/ppermute | solution.py:49
  495.6 42.2 %collective-permute-start.34 = (bf16[1024,512]{1,0:T(8,128)(2,1)S(1)}, bf16[1024,512]{1,0:T(8,128)(2,1)S(1)}, u32[]{:S(2)}, u32[]{:S(2)}) collective-permute-start(bf16[1024,512]{1,0:T(8,128)(2,1)S(1)} %add_convert_fusion.1), channel_id=1, source_target_pairs={{0,3},{1,0},{2,1},{3,2},{4,7},{5,4},{6,5},{7,6},{8,11},{9,8},{10,9... | collective-permute-start | bytes 3145736 | tf_op jit(solution)/shard_map/ppermute | solution.py:49
  553.3 39.4 %collective-permute-start.35 = (bf16[256,2048]{1,0:T(8,128)(2,1)}, bf16[256,2048]{1,0:T(8,128)(2,1)}, u32[]{:S(2)}, u32[]{:S(2)}) collective-permute-start(bf16[256,2048]{1,0:T(8,128)(2,1)} %add_convert_fusion.2), channel_id=1, source_target_pairs={{0,3},{1,0},{2,1},{3,2},{4,7},{5,4},{6,5},{7,6},{8,11},{9,8},{10,9... | collective-permute-start | bytes 3145736 | tf_op jit(solution)/shard_map/ppermute | solution.py:49
  566.3 31.4 %collective-permute-start.43 = (bf16[336,512]{1,0:T(8,128)(2,1)}, bf16[336,512]{1,0:T(8,128)(2,1)S(1)}, u32[]{:S(2)}, u32[]{:S(2)}) collective-permute-start(bf16[336,512]{1,0:T(8,128)(2,1)} %get-tuple-element.174), channel_id=1, source_target_pairs={{0,1},{1,2},{2,3},{3,0},{4,5},{5,6},{6,7},{7,4},{8,9},{9,10},{10,1... | collective-permute-start | bytes 1032200 | tf_op jit(solution)/shard_map/ppermute | solution.py:49
  (72 other events, 989.6 us)
Sparse Core Ops, SparseCore 0:
  46.0 68.1 all-gather.2
  116.7 110.7 all-gather.4
  328.6 119.0 reduce-scatter.2
  463.6 84.3 reduce-scatter.4

commit v2 on v1

--- a/solution.py
+++ b/solution.py
@@ -181,6 +181,70 @@
 def turn(values, cosine, sine):
     upper, lower = values[: HD // 2], values[HD // 2 :]
     return jnp.concatenate([upper * cosine - lower * sine, lower * cosine + upper * sine], 0)
+
+
+def first_pack_kernel(cols, query_ref, keyval_ref, gains_ref, out_ref):
+    block, piece = query_ref.shape[0], keyval_ref.shape[1]
+    out_ref[block:, :] = jnp.zeros((out_ref.shape[0] - block, cols), LOW)
+    out_ref[:block, :] = query_ref[...].astype(LOW)
+    row = block
+    for lo in range(0, 2 * KVD, cols):
+        for j in range(0, cols, KVD):
+            at = (lo + j) // KVD
+            out_ref[row : row + piece, j : j + KVD] = keyval_ref[at].astype(LOW)
+        row += piece
+    out_ref[row : row + 2, :piece] = gains_ref[...].astype(LOW)
+
+
+def first_pack(query, keyval, gains):
+    block, cols = query.shape
+    piece = keyval.shape[1]
+    vmem = pl.BlockSpec(memory_space=pltpu.VMEM)
+    height = block + piece * (2 * KVD // cols) + 16
+    return pl.pallas_call(
+        functools.partial(first_pack_kernel, cols),
+        in_specs=[vmem] * 3,
+        out_specs=vmem,
+        out_shape=jax.ShapeDtypeStruct((height, cols), LOW),
+        compiler_params=pltpu.CompilerParams(vmem_limit_bytes=VMEM_LIMIT),
+        cost_estimate=lasting(2.0),
+        name="first_pack",
+    )(query, keyval, gains)
+
+
+def first_join_kernel(n, piece, ids_ref, *refs):
+    slots, out_ref = refs[:n], refs[n]
+    block, cols = out_ref.shape[0], slots[0].shape[1]
+    span = n * cols + 2 * KVD
+    out_ref[:, span:] = jnp.zeros((block, out_ref.shape[1] - span), LOW)
+    for s, slot in enumerate(slots):
+        at = pl.multiple_of(ids_ref[s] * piece, piece)
+        out_ref[:, s * cols : (s + 1) * cols] = slot[:block, :]
+        row = block
+        for lo in range(n * cols, span, cols):
+            out_ref[pl.ds(at, piece), lo : lo + cols] = slot[row : row + piece, :]
+            row += piece
+        gains = slot[row : row + 16, :128].astype(F32).T.astype(LOW)
+        out_ref[pl.ds(at, piece), span : span + 16] = gains[:piece]
+
+
+def first_join(ids, slots, block, piece):
+    n = len(slots)
+    cols = slots[0].shape[1]
+    width = n * cols + 2 * KVD + 128
+    return pl.pallas_call(
+        functools.partial(first_join_kernel, n, piece),
+        grid_spec=pltpu.PrefetchScalarGridSpec(
+            num_scalar_prefetch=1,
+            grid=(1,),
+            in_specs=[pl.BlockSpec(slots[0].shape, lambda i, o: (0, 0))] * n,
+            out_specs=pl.BlockSpec((block, width), lambda i, o: (0, 0)),
+        ),
+        out_shape=jax.ShapeDtypeStruct((block, width), LOW),
+        compiler_params=pltpu.CompilerParams(vmem_limit_bytes=VMEM_LIMIT),
+        cost_estimate=lasting(2.0),
+        name="first_join",
+    )(ids, *slots)
 
 
 def begin_kernel(
@@ -477,7 +541,7 @@
     )(order, o, x, gain, *weights)
 
 
-def tail_pack_kernel(n, piece, cols, ids_ref, owned_ref, *outs):
+def tail_pack_kernel(n, piece, cols, ids_ref, owned_ref, gain_ref, *outs):
     block, start = owned_ref.shape[0], H * HD
     span = start + 2 * KVD
     for s, out_ref in enumerate(outs):
@@ -487,12 +551,12 @@
         for lo in range(start, span, cols):
             out_ref[row : row + piece, :] = owned_ref[pl.ds(at, piece), lo : lo + cols]
             row += piece
-        gains = owned_ref[pl.ds(at, piece), span : span + 128].astype(F32).T.astype(LOW)
+        gains = gain_ref[pl.ds(at, piece), :].T.astype(LOW)
         out_ref[row:, :] = jnp.zeros((16, cols), LOW)
         out_ref[row : row + 16, :piece] = gains[:16]
 
 
-def tail_pack(ids, owned, piece, cols):
+def tail_pack(ids, owned, gain_cols, piece, cols):
     n, block = ids.shape[0], owned.shape[0]
     height = block + piece * (2 * KVD // cols) + 16
     return pl.pallas_call(
@@ -500,14 +564,17 @@
         grid_spec=pltpu.PrefetchScalarGridSpec(
             num_scalar_prefetch=1,
             grid=(1,),
-            in_specs=[pl.BlockSpec(owned.shape, lambda i, o: (0, 0))],
+            in_specs=[
+                pl.BlockSpec(owned.shape, lambda i, o: (0, 0)),
+                pl.BlockSpec(gain_cols.shape, lambda i, o: (0, 0)),
+            ],
             out_specs=[pl.BlockSpec((height, cols), lambda i, o: (0, 0))] * n,
         ),
         out_shape=[jax.ShapeDtypeStruct((height, cols), LOW)] * n,
         compiler_params=pltpu.CompilerParams(vmem_limit_bytes=VMEM_LIMIT),
         cost_estimate=lasting(2.0),
         name="tail_pack",
-    )(ids, owned)
+    )(ids, owned, gain_cols)
 
 
 def tail_adamw_kernel(block, piece, parts, *refs):
@@ -599,28 +666,6 @@
         cost_estimate=lasting(steps * wide * count / 4800),
         name="weight_grad",
     )(*args)
-
-
-def gain_kernel(gain_ref, base_ref, out_ref):
-    out_ref[...] = gain_ref[...].T.astype(LOW)
-
-
-def put_gains(gain_grads, base, first):
-    height = base.shape[0]
-    return pl.pallas_call(
-        gain_kernel,
-        grid=(1,),
-        in_specs=[
-            pl.BlockSpec((128, height), lambda i: (0, 0)),
-            pl.BlockSpec(memory_space=pl.ANY),
-        ],
-        out_specs=pl.BlockSpec((height, 128), lambda i: (0, first)),
-        out_shape=jax.ShapeDtypeStruct(base.shape, LOW),
-        input_output_aliases={1: 0},
-        compiler_params=pltpu.CompilerParams(vmem_limit_bytes=VMEM_LIMIT),
-        cost_estimate=lasting(2.0),
-        name="put_gains",
-    )(jnp.pad(gain_grads, ((0, 126), (0, 0))), base)
 
 
 def turned_kernel(x_ref, out_ref):
@@ -819,27 +864,15 @@
     piece = keyval_weight.shape[1]
     block, cols = query_weight.shape
 
-    keyval_piece = jnp.concatenate(
-        [
-            keyval_weight[0].astype(LOW),
-            keyval_weight[1].astype(LOW),
-            jnp.pad(gains.T.astype(LOW), ((0, 0), (0, 126))),
-        ],
-        1,
-    )
-    keyval_slots = ring_gather(keyval_piece, n)
-    query_slots = ring_gather(query_weight.astype(LOW), n)
-    keyval_rows = jnp.zeros((n, piece, keyval_piece.shape[1]), LOW)
-    for chunk, held in zip(chunk_ids, keyval_slots):
-        keyval_rows = lax.dynamic_update_slice(keyval_rows, held[None], (chunk, 0, 0))
-    keyval_rows = keyval_rows.reshape(n * piece, -1)
-    attn_in = jnp.concatenate(query_slots + [keyval_rows], 1)
+    ids = jnp.stack(chunk_ids).astype(jnp.int32)
+    first_slots = ring_gather(first_pack(query_weight, keyval_weight, gains), n)
+    attn_in = first_join(ids, first_slots, block, piece)
     feed_in = jnp.concatenate(
         [gateup_weight.astype(LOW), down_weight.T.astype(LOW)[None]], 0
     )
     attn_in, feed_in = after(attn_in, feed_in)
     attn_low = lax.all_gather(attn_in, "dp", axis=0, tiled=True)
-    output_piece, _ = after(output_weight.T.astype(LOW), (query_slots, keyval_slots))
+    output_piece, _ = after(output_weight.T.astype(LOW), first_slots)
     output_slots = ring_gather(output_piece, n)
     grad_start, _ = after(cotangent, output_slots)
     grad_slots = ring_gather(grad_start, n, 1)
@@ -902,7 +935,9 @@
     acts, _ = after(acts, last)
     grad_mlp = feed_grad(acts, [rows_t[s] for s in order], 0, 2)
     from_left = ring_way(part_slots, n, 1)
-    from_right = ring_way(part_slots, n, -1, None, grad_mlp[0, :8, :128])
+    passed = []
+    from_right = ring_way(part_slots, n, -1, passed, grad_mlp[0, :8, :128])
+    acts, _ = after(acts, passed)
     grad_mlp = feed_grad(acts, [grads_t[s] for s in order], 2, 1, grad_mlp)
     second_grad = ring_sum(part_slots[0], from_left, from_right)
     mlp_parts = [contract(act[2], feed_low[2], 1, 1).astype(LOW) for act in acts]
@@ -926,19 +961,18 @@
     (grad_q_t, grad_kv), _ = after((grad_q_t, grad_kv), (block_far, block_left))
 
     places = [dp_order(sizes["dp"], block, odd) for odd in (0, 1)]
-    partner = swap(
-        weight_grad(
-            first_normalized, grad_q_t, n * cols, cols, n, lambda i: i, lambda i: i, places[1]
-        ),
-        sizes["dp"],
-        1,
-    )
     kv_parts = [grad_kv[s] for s in range(n)]
-    own_kv = ring_scatter(kv_parts, n)
+    kv_left, passed = ring_way(kv_parts, n, 1), []
+    own_kv = ring_sum(kv_parts[0], ring_way(kv_parts, n, -1, passed), kv_left)
+    query_rows, _ = after(first_normalized, (passed, kv_left))
+    partner = weight_grad(
+        query_rows, grad_q_t, n * cols, cols, n, lambda i: i, lambda i: i, places[1]
+    )
+    partner = swap(partner, sizes["dp"], 1)
     out_rows, _ = after(back, grad_q_t)
-    held_cols, heads_cols = attn_low.shape[1], H * HD // (2 * KVD)
+    heads_cols = H * HD // (2 * KVD)
     grad_pack = weight_grad(
-        out_rows, mixed_t, held_cols, 2 * KVD, heads_cols, lambda i: i, lambda i: i
+        out_rows, mixed_t, span, 2 * KVD, heads_cols, lambda i: i, lambda i: i
     )
     own_kv, _ = after(own_kv, partner)
     grad_k = own_kv[:KVD].reshape(KVH, 2, HD // 2, rows)
@@ -948,23 +982,11 @@
         [grad_k.reshape(KVD, rows).astype(LOW), own_kv[KVD:].astype(LOW)], 0
     )
     grad_pack = weight_grad(
-        first_normalized, grad_kv_t, held_cols, 2 * KVD, 1, lambda i: 0, lambda i: heads_cols,
+        first_normalized, grad_kv_t, span, 2 * KVD, 1, lambda i: 0, lambda i: heads_cols,
         None, grad_pack,
-    )
-    grad_qkv_t = jnp.concatenate(
-        [grad_q_t, grad_kv_t, jnp.zeros((held_cols - span, rows), LOW)], 0
-    )
-    first_grad = contract(grad_qkv_t, attn_low, 0, 1)
-    first_unit = x * first_inverse
-    first_gain_grad = jnp.sum(first_grad * first_unit, 0)
-    grad_pack = put_gains(
-        jnp.stack([first_gain_grad, second_gain_grad]), grad_pack, span // 128
     )
     grad_pack, owned_mlp = after(grad_pack, owned_mlp)
     owned_pack = lax.psum_scatter(grad_pack, "dp", scatter_dimension=0, tiled=True)
-    layer_input_gradient = residual_grad + norm_backward(
-        first_grad, first_unit, first_inverse, first_gain
-    )
 
     query_slots, last = [None] * n, grad_pack
     for s in order[::-1]:
@@ -974,20 +996,36 @@
             partner, lambda i, s=s: s,
         )
     query_far, query_left = ring_most(query_slots, n), ring_way(query_slots, n, 1)
-    query_right = ring_last(query_slots, n, query_far)
+    owned_gateup, owned_down = owned_mlp[:2], owned_mlp[2]
+    gateup_up = adamw(
+        gateup_weight, gateup_first, gateup_second, owned_gateup.astype(F32), RATE_GATEUP, DECAY
+    )
+    down_up = adamw_turned(down_weight, down_first, down_second, owned_down, RATE_DOWN)
+    query_right = ring_last(query_slots, n, query_far, (gateup_up, down_up))
     query_sum = ring_sum(query_slots[0], query_left, query_right).astype(LOW)
     block_right = ring_last(mlp_slots, n, block_far, query_right)
     block_out = residual + ring_sum(mlp_slots[0], block_left, block_right)
-
-    owned_gateup, owned_down = owned_mlp[:2], owned_mlp[2]
-    gateup_up = adamw(
-        gateup_weight, gateup_first, gateup_second, owned_gateup.astype(F32), RATE_GATEUP, DECAY
-    )
-    down_up = adamw_turned(down_weight, down_first, down_second, owned_down, RATE_DOWN)
-    own_query = dp_scatter(query_sum, sizes["dp"], (gateup_up, down_up)).astype(F32)
+    own_query = dp_scatter(query_sum, sizes["dp"], ()).astype(F32)
     query_up = adamw(query_weight, query_first, query_second, own_query, RATE_QUERY, DECAY)
 
-    slots = tail_pack(jnp.stack(chunk_ids).astype(jnp.int32), owned_pack, piece, cols)
+    (back_q_t, back_kv_t), _ = after((grad_q_t, grad_kv_t), query_slots)
+    grad_qkv_t = jnp.concatenate(
+        [back_q_t, back_kv_t, jnp.zeros((attn_low.shape[1] - span, rows), LOW)], 0
+    )
+    first_grad = contract(grad_qkv_t, attn_low, 0, 1)
+    first_unit = x * first_inverse
+    first_gain_grad = jnp.sum(first_grad * first_unit, 0)
+    layer_input_gradient = residual_grad + norm_backward(
+        first_grad, first_unit, first_inverse, first_gain
+    )
+    gain_grads, bit = jnp.stack([first_gain_grad, second_gain_grad]), 1
+    while bit < sizes["dp"]:
+        gain_grads = gain_grads + swap(gain_grads, sizes["dp"], bit)
+        bit *= 2
+    gain_grads = lax.dynamic_slice_in_dim(gain_grads, lax.axis_index("dp") * block, block, 1)
+    gain_cols = jnp.pad(gain_grads.T, ((0, 0), (0, 126)))
+
+    slots = tail_pack(ids, owned_pack, gain_cols, piece, cols)
     parts = [slots[0], ring_way(slots, n, -1), ring_way(slots, n, 1)]
     states = [output_weight, output_first, output_second, keyval_weight, keyval_first]
     states += [keyval_second, gains, gains_first, gains_second]

time: 618 us -> 614 us (level)
    ppermute x33 -> x30, waiting for transfers between devices: 119 us -> 107 us  [shift(): return lax.ppermute(x, 'tensor', [(i, (i + by) % n) for i in range(n)])]
    ppermute x33 -> x30, starting transfers between devices: 58.9 us -> 52.5 us  [shift(): return lax.ppermute(x, 'tensor', [(i, (i + by) % n) for i in range(n)])]
    ppermute x11 -> x14, waiting for transfers between devices: 16.7 us -> 19.9 us  [swap(): return lax.ppermute(x, 'dp', [(i, i ^ bit) for i in range(size)])]
    ppermute x11 -> x14, starting transfers between devices: 10.1 us -> 12.6 us  [swap(): return lax.ppermute(x, 'dp', [(i, i ^ bit) for i in range(size)])]
  transfers between devices with their start and end apart: 48 -> 48, of which waited for: 22 -> 26; matrix products, arithmetic and copies ran while one was open for 14% -> 15% of each run, Pallas kernels for 37% -> 36%
where the time goes in v2:
time: 614 us; the launch traced here: 608 us
  Pallas kernels  245 us (40%)
  waiting for transfers between devices  188 us (31%)
  starting transfers between devices  65.2 us (11%)
  other arithmetic  43.3 us (7%)
  matrix products  30.5 us (5%)
  local copies, waits for them, and re-layouts  21 us (3%)
  between operations  14.9 us (2%)
    ppermute x30, waiting for transfers between devices, shift(): return lax.ppermute(x, 'tensor', [(i, (i + by) % n) for i in range(n)])  107 us
    pallas_call x3, Pallas kernels, feed(): pl.pallas_call(functools.partial(feed_kernel, pieces, count), in_specs=[v...  56 us
    ppermute x30, starting transfers between devices, shift(): return lax.ppermute(x, 'tensor', [(i, (i + by) % n) for i in range(n)])  52.5 us
    all_gather x1, waiting for transfers between devices, on_device(): attn_low = lax.all_gather(attn_in, 'dp', axis=0, tiled=True)  40.5 us
    pallas_call x1, Pallas kernels, attend_back(): pl.pallas_call(functools.partial(attend_back_kernel, slots, heads, len(we...  40.2 us
    pallas_call x7, Pallas kernels, weight_grad(): pl.pallas_call(functools.partial(weight_grad_kernel, count, add is not No...  35.3 us
    dot_general x4, matrix products, contract(): lax.dot_general(left, right, (((dim_left,), (dim_right,)), ((), ())), pre...  30.5 us
    pallas_call x2, Pallas kernels, feed_grad(): pl.pallas_call(functools.partial(feed_grad_kernel, halves, n), grid=(part...  29.5 us
  transfers between devices with their start and end apart: 48, of which 26 were waited for; matrix products, arithmetic and copies ran while one was open for 15% of the time, Pallas kernels for 36%

profile of v2, /device:TPU:0, one launch (start us, length us, event | category | flops | bytes accessed | tf_op | source)
XLA Modules:
  0.0 608.3 jit_solution(19822124247525855)
XLA Ops:
  14.3 9.1 %collective-permute-done.refs_1_ = bf16[336,512]{1,0:T(8,128)(2,1)S(1)} collective-permute-done((bf16[336,512]{1,0:T(8,128)(2,1)}, bf16[336,512]{1,0:T(8,128)(2,1)S(1)}, u32[]{:S(2)}, u32[]{:S(2)}) %collective-permute-start) | collective-permute-done | bytes 344096 | tf_op jit(solution)/shard_map/ppermute | solution.py:49
  29.7 7.8 %collective-permute-done.1.refs_2_ = bf16[336,512]{1,0:T(8,128)(2,1)} collective-permute-done((bf16[336,512]{1,0:T(8,128)(2,1)S(1)}, bf16[336,512]{1,0:T(8,128)(2,1)}, u32[]{:S(2)}, u32[]{:S(2)}) %collective-permute-start.1) | collective-permute-done | bytes 344096 | tf_op jit(solution)/shard_map/ppermute | solution.py:49
  44.8 7.3 %collective-permute-done.3 = bf16[256,512]{1,0:T(8,128)(2,1)S(1)} collective-permute-done((bf16[256,512]{1,0:T(8,128)(2,1)S(1)}, bf16[256,512]{1,0:T(8,128)(2,1)S(1)}, u32[]{:S(2)}, u32[]{:S(2)}) %collective-permute-start.3) | collective-permute-done | bytes 262176 | tf_op jit(solution)/shard_map/ppermute | solution.py:49
  68.8 40.5 %all-gather.3.cloned.1.call-done.gain_ref.weight_ref = bf16[2048,2688]{1,0:T(8,128)(2,1)} async-done(((bf16[256,2688]{1,0:T(8,128)(2,1)}), bf16[2048,2688]{1,0:T(8,128)(2,1)}) %all-gather.3.cloned.1.call-update) | async-done | bytes 11010064 | tf_op jit(solution)/shard_map/all_gather | solution.py:874
  124.4 7.1 %project.1.q_ref = bf16[2048,256]{1,0:T(8,128)(2,1)} custom-call(bf16[256,2048]{1,0:T(8,128)(2,1)} %get-tuple-element.180.rows_ref, bf16[2048,2688]{1,0:T(8,128)(2,1)} %all-gather.3.cloned.1.call-done.gain_ref.weight_ref, f32[32,256]{1,0:T(8,128)} %get-tuple-element.110.cos_ref.refs_6_, f32[32,256]{1,0:T(8,128)} %get-tuple-element.111.sin_ref.refs_7_), custom_call_target="tpu_custom_call" | custom-call | flops 9200000000 | bytes 1000000 | tf_op jit(solution)/shard_map/project/pallas_call | solution.py:308
  136.3 22.0 %attend.1 = (bf16[2048,256]{1,0:T(8,128)(2,1)}, bf16[256,2048]{1,0:T(8,128)(2,1)}, f32[4,8,256]{2,1,0:T(8,128)}) custom-call(s32[25]{0:T(128)} %concatenate.35.meta_ref, s32[1,256]{1,0:T(1,128)} %bitcast.102, bf16[2048,256]{1,0:T(8,128)(2,1)} %project.1.q_ref, bf16[4,512,256]{2,1,0:T(8,128)(2,1)} %pad_maximum_fusion.3.kv_ref), custom_call_target="tpu_custom_call" | custom-call | flops 8589934592 | bytes 2097152 | tf_op jit(solution)/shard_map/attend/pallas_call | solution.py:368
  158.3 7.4 %collective-permute-done.13 = bf16[256,2048]{1,0:T(8,128)(2,1)S(1)} collective-permute-done((bf16[256,2048]{1,0:T(8,128)(2,1)S(1)}, bf16[256,2048]{1,0:T(8,128)(2,1)S(1)}, u32[]{:S(2)}, u32[]{:S(2)}) %collective-permute-start.13) | collective-permute-done | bytes 1048608 | tf_op jit(solution)/shard_map/ppermute | solution.py:116
  176.8 8.8 %mix.1 = (f32[256,2048]{1,0:T(8,128)}, bf16[256,2048]{1,0:T(8,128)(2,1)}, f32[256,1]{1,0:T(8,128)}) custom-call(s32[16]{0:T(128)} %concatenate.34.order_ref, bf16[256,2048]{1,0:T(8,128)(2,1)} %get-tuple-element.117.o_ref, bf16[256,2048]{1,0:T(8,128)(2,1)} %x_ref.3, f32[1,2048]{1,0:T(1,128)} %get-tuple-element.223.gain_ref, bf16[512,2048]{1,0:T(8,128)(2,1)} %copy-done.19, ...), custom_call_target="tpu_custom_call" | custom-call | flops 6899999744 | bytes 1000000 | tf_op jit(solution)/shard_map/mix/pallas_call | solution.py:518
  202.4 21.1 %all-gather.5.cloned.1.call-done.refs_2_.refs_4_ = bf16[3,2048,1408]{2,1,0:T(8,128)(2,1)} async-done(((bf16[3,256,1408]{2,1,0:T(8,128)(2,1)}), bf16[3,2048,1408]{2,1,0:T(8,128)(2,1)}) %all-gather.5.cloned.1.call-update) | async-done | bytes 17301520 | tf_op jit(solution)/shard_map/all_gather | solution.py:880
  223.5 14.8 %feed.3 = (bf16[3,256,1408]{2,1,0:T(8,128)(2,1)}, bf16[256,2048]{1,0:T(8,128)(2,1)}) custom-call(bf16[256,2048]{1,0:T(8,128)(2,1)} %get-tuple-element.133.x_ref.refs_0_, bf16[256,2048]{1,0:T(8,128)(2,1)} %refs_1_, bf16[3,2048,1408]{2,1,0:T(8,128)(2,1)} %all-gather.5.cloned.1.call-done.refs_2_.refs_4_), custom_call_target="tpu_custom_call" | custom-call | flops 1150000000 | bytes 1000000 | tf_op jit(solution)/shard_map/feed/pallas_call | solution.py:739
  245.7 26.4 %feed.4 = (bf16[3,512,1408]{2,1,0:T(8,128)(2,1)}, bf16[512,2048]{1,0:T(8,128)(2,1)}) custom-call(bf16[256,2048]{1,0:T(8,128)(2,1)} %copy-done.26, bf16[256,2048]{1,0:T(8,128)(2,1)} %copy-done.27, bf16[256,2048]{1,0:T(8,128)(2,1)} %collective-permute-done.6.x_ref.refs_2_, bf16[256,2048]{1,0:T(8,128)(2,1)} %copy-done.25, ...), custom_call_target="tpu_custom_call" | custom-call | flops 1150000000 | bytes 1000000 | tf_op jit(solution)/shard_map/feed/pallas_call | solution.py:739
  273.0 14.9 %feed.5 = (bf16[3,256,1408]{2,1,0:T(8,128)(2,1)}, bf16[256,2048]{1,0:T(8,128)(2,1)}) custom-call(bf16[256,2048]{1,0:T(8,128)(2,1)} %copy-done.24, bf16[256,2048]{1,0:T(8,128)(2,1)} %copy-done.22, bf16[3,2048,1408]{2,1,0:T(8,128)(2,1)} %all-gather.5.cloned.1.call-done.refs_2_.refs_4_), custom_call_target="tpu_custom_call" | custom-call | flops 1150000000 | bytes 1000000 | tf_op jit(solution)/shard_map/feed/pallas_call | solution.py:739
  294.2 18.3 %feed_grad.2.refs_7_ = bf16[3,2048,1408]{2,1,0:T(8,128)(2,1)} custom-call(bf16[3,256,1408]{2,1,0:T(8,128)(2,1)} %get-tuple-element.152.refs_0_, bf16[3,512,1408]{2,1,0:T(8,128)(2,1)} %get-tuple-element.153.refs_1_, bf16[3,256,1408]{2,1,0:T(8,128)(2,1)} %get-tuple-element.154.refs_2_, bf16[2048,256]{1,0:T(8,128)(2,1)} %turned.12.refs_3_, ...), custom_call_target="tpu_custom_call" | custom-call | flops 1150000000 | bytes 1000000 | tf_op jit(solution)/shard_map/feed_grad/pallas_call | solution.py:792
  321.0 11.2 %feed_grad.3 = bf16[3,2048,1408]{2,1,0:T(8,128)(2,1)} custom-call(bf16[3,256,1408]{2,1,0:T(8,128)(2,1)} %get-tuple-element.152.refs_0_, bf16[3,512,1408]{2,1,0:T(8,128)(2,1)} %get-tuple-element.153.refs_1_, bf16[3,256,1408]{2,1,0:T(8,128)(2,1)} %get-tuple-element.154.refs_2_, bf16[2048,256]{1,0:T(8,128)(2,1)} %turned.8.refs_3_, ...), custom_call_target="tpu_custom_call", output_to_operand_aliasing={{}: (7, {})} | custom-call | flops 1150000000 | bytes 1000000 | tf_op jit(solution)/shard_map/feed_grad/pallas_call | solution.py:792
  338.1 7.0 %fusion.7 = bf16[256,2048]{1,0:T(8,128)(2,1)} fusion(bf16[3,2048,1408]{2,1,0:T(8,128)(2,1)} %all-gather.5.cloned.1.call-done.refs_2_.refs_4_, bf16[3,256,1408]{2,1,0:T(8,128)(2,1)} %get-tuple-element.154.refs_2_), kind=kOutput, calls=%fused_computation.11 | convolution fusion | flops 1476919296 | bytes 7536640 | tf_op jit(solution)/shard_map/dot_general | solution.py:39
  345.0 7.9 %fusion.3 = bf16[512,2048]{1,0:T(8,128)(2,1)S(1)} fusion(bf16[3,2048,1408]{2,1,0:T(8,128)(2,1)} %all-gather.5.cloned.1.call-done.refs_2_.refs_4_, bf16[3,512,1408]{2,1,0:T(8,128)(2,1)} %get-tuple-element.153.refs_1_), kind=kOutput, calls=%fused_computation.6 | convolution fusion | flops 2953838592 | bytes 9306112 | tf_op jit(solution)/shard_map/dot_general | solution.py:39
  353.0 7.0 %collective-permute-done.23 = bf16[256,2048]{1,0:T(8,128)(2,1)S(1)} collective-permute-done((bf16[256,2048]{1,0:T(8,128)(2,1)}, bf16[256,2048]{1,0:T(8,128)(2,1)S(1)}, u32[]{:S(2)}, u32[]{:S(2)}) %collective-permute-start.23) | collective-permute-done | bytes 1048608 | tf_op jit(solution)/shard_map/ppermute | solution.py:49
  369.5 40.2 %attend_back.1 = (bf16[2048,256]{1,0:T(8,128)(2,1)}, bf16[4,512,256]{2,1,0:T(8,128)(2,1)}) custom-call(s32[25]{0:T(128)} %concatenate.35.meta_ref, s32[1,256]{1,0:T(1,128)} %bitcast.103, bf16[2048,256]{1,0:T(8,128)(2,1)} %project.1.q_ref, bf16[4,512,256]{2,1,0:T(8,128)(2,1)} %pad_maximum_fusion.3.kv_ref, bf16[256,2048]{1,0:T(8,128)(2,1)} %fusion.27.back_ref.rows_ref, ...), custom_call_target="tpu_custom_call" | custom-call | flops 200000000753664 | bytes 1000000 | tf_op jit(solution)/shard_map/attend_back/pallas_call | solution.py:459
  437.5 7.7 %weight_grad.8.rest_0_ = bf16[2048,2560]{1,0:T(8,128)(2,1)} custom-call(s32[16]{0:T(128)} %iota.13.order_ref, bf16[256,2048]{1,0:T(8,128)(2,1)} %fusion.27.back_ref.rows_ref, bf16[2048,256]{1,0:T(8,128)(2,1)} %get-tuple-element.160.refs_4_.x_ref), custom_call_target="tpu_custom_call" | custom-call | flops 7850666496 | bytes 1000000 | tf_op jit(solution)/shard_map/weight_grad/pallas_call | solution.py:654
  480.5 9.1 %adamw_turned.1 = (f32[1408,256]{1,0:T(8,128)}, f32[1408,256]{1,0:T(8,128)}, f32[1408,256]{1,0:T(8,128)}) custom-call(f32[1408,256]{1,0:T(8,128)} %weight.1, f32[1408,256]{1,0:T(8,128)} %first.1, f32[1408,256]{1,0:T(8,128)} %second.1, bf16[256,1408]{1,0:T(8,128)(2,1)} %slice_bitcast_fusion.10.grad), custom_call_target="tpu_custom_call" | custom-call | flops 4325376 | bytes 10092544 | tf_op jit(solution)/shard_map/adamw_turned/pallas_call | solution.py:820
  489.6 9.8 %multiply_reduce_fusion.1 = (f32[2048]{0:T(1024)S(1)}, f32[256]{0:T(256)S(1)}, f32[256,2048]{1,0:T(8,128)}) fusion(bf16[256,2048]{1,0:T(8,128)(2,1)S(1)} %copy-done.10, f32[256]{0:T(256)S(1)} %reduce.1, f32[2048]{0:T(1024)S(1)} %bitcast.98, bf16[2048,2688]{1,0:T(8,128)(2,1)} %all-gather.3.cloned.1.call-done.gain_ref.weight_ref, ...), kind=kOutput, calls=%fused_computation.16 | convolution fusion | flops 2826368768 | bytes 15490304 | tf_op jit(solution)/shard_map/dot_general | solution.py:39
  499.4 9.3 %collective-permute-done.30 = bf16[1024,512]{1,0:T(8,128)(2,1)} collective-permute-done((bf16[1024,512]{1,0:T(8,128)(2,1)}, bf16[1024,512]{1,0:T(8,128)(2,1)}, u32[]{:S(2)}, u32[]{:S(2)}) %collective-permute-start.30) | collective-permute-done | bytes 1048608 | tf_op jit(solution)/shard_map/ppermute | solution.py:49
  523.0 13.1 %collective-permute-done.31 = bf16[1024,512]{1,0:T(8,128)(2,1)} collective-permute-done((bf16[1024,512]{1,0:T(8,128)(2,1)}, bf16[1024,512]{1,0:T(8,128)(2,1)}, u32[]{:S(2)}, u32[]{:S(2)}) %collective-permute-start.31) | collective-permute-done | bytes 1048608 | tf_op jit(solution)/shard_map/ppermute | solution.py:49
  565.9 20.1 %collective-permute-done.41 = bf16[336,512]{1,0:T(8,128)(2,1)S(1)} collective-permute-done((bf16[336,512]{1,0:T(8,128)(2,1)}, bf16[336,512]{1,0:T(8,128)(2,1)S(1)}, u32[]{:S(2)}, u32[]{:S(2)}) %collective-permute-start.41) | collective-permute-done | bytes 344096 | tf_op jit(solution)/shard_map/ppermute | solution.py:49
  (277 shorter events, 245.5 us)
Async XLA Ops:
  7.2 102.1 %all-gather.3.cloned.1.call-start = ((), (), s32[]{:S(2)}) async-start(), calls=%async_computation.2 | async-start | bytes 12386304 | tf_op jit(solution)/shard_map/all_gather | solution.py:874
  40.7 182.7 %all-gather.5.cloned.1.call-start = ((), (), s32[]{:S(2)}) async-start(), calls=%async_computation.3 | async-start | bytes 19464192 | tf_op jit(solution)/shard_map/all_gather | solution.py:880
  60.3 391.5 %reduce-scatter.3.cloned.1.call-start = ((), (), s32[]{:S(2)}) async-start(), calls=%async_computation.4 | async-start | bytes 19464192 | tf_op jit(solution)/shard_map/reduce_scatter | solution.py:945
  63.4 56.0 %collective-permute-start.7 = (bf16[256,2048]{1,0:T(8,128)(2,1)S(1)}, bf16[256,2048]{1,0:T(8,128)(2,1)S(1)}, u32[]{:S(2)}, u32[]{:S(2)}) collective-permute-start(bf16[256,2048]{1,0:T(8,128)(2,1)S(1)} %copy-done.7), channel_id=1, source_target_pairs={{0,3},{1,0},{2,1},{3,2},{4,7},{5,4},{6,5},{7,6},{8,11},{9,8},{10,9... | collective-permute-start | bytes 3145736 | tf_op jit(solution)/shard_map/ppermute | solution.py:49
  63.6 55.8 %collective-permute-start.6 = (bf16[256,2048]{1,0:T(8,128)(2,1)S(1)}, bf16[256,2048]{1,0:T(8,128)(2,1)}, u32[]{:S(2)}, u32[]{:S(2)}) collective-permute-start(bf16[256,2048]{1,0:T(8,128)(2,1)S(1)} %copy-done.7), channel_id=1, source_target_pairs={{0,1},{1,2},{2,3},{3,0},{4,5},{5,6},{6,7},{7,4},{8,9},{9,10},{10,1... | collective-permute-start | bytes 3145736 | tf_op jit(solution)/shard_map/ppermute | solution.py:49
  65.7 49.1 %collective-permute-start.12 = (bf16[128,2048]{1,0:T(8,128)(2,1)S(1)}, bf16[128,2048]{1,0:T(8,128)(2,1)}, u32[]{:S(2)}, u32[]{:S(2)}) collective-permute-start(bf16[128,2048]{1,0:T(8,128)(2,1)S(1)} %get-tuple-element.218), channel_id=1, source_target_pairs={{0,16},{4,20},{8,24},{12,28},{16,0},{20,4},{24,8},{28,12},{1,17},{... | collective-permute-start | bytes 1572872 | tf_op jit(solution)/shard_map/ppermute | solution.py:116
  67.3 48.6 %collective-permute-start.11 = (bf16[128,2048]{1,0:T(8,128)(2,1)S(1)}, bf16[128,2048]{1,0:T(8,128)(2,1)}, u32[]{:S(2)}, u32[]{:S(2)}) collective-permute-start(bf16[128,2048]{1,0:T(8,128)(2,1)S(1)} %get-tuple-element.219), channel_id=1, source_target_pairs={{0,8},{4,12},{8,0},{12,4},{16,24},{20,28},{24,16},{28,20},{1,9},{5... | collective-permute-start | bytes 1572872 | tf_op jit(solution)/shard_map/ppermute | solution.py:116
  119.4 46.3 %collective-permute-start.13 = (bf16[256,2048]{1,0:T(8,128)(2,1)S(1)}, bf16[256,2048]{1,0:T(8,128)(2,1)S(1)}, u32[]{:S(2)}, u32[]{:S(2)}) collective-permute-start(bf16[256,2048]{1,0:T(8,128)(2,1)S(1)} %pad_maximum_fusion.4), channel_id=1, source_target_pairs={{0,16},{4,20},{8,24},{12,28},{16,0},{20,4},{24,8},{28,12},{1,17},{... | collective-permute-start | bytes 3145736 | tf_op jit(solution)/shard_map/ppermute | solution.py:116
  119.9 46.9 %collective-permute-start.14 = (bf16[256,2048]{1,0:T(8,128)(2,1)S(1)}, bf16[256,2048]{1,0:T(8,128)(2,1)S(1)}, u32[]{:S(2)}, u32[]{:S(2)}) collective-permute-start(bf16[256,2048]{1,0:T(8,128)(2,1)S(1)} %pad_maximum_fusion.5), channel_id=1, source_target_pairs={{0,8},{4,12},{8,0},{12,4},{16,24},{20,28},{24,16},{28,20},{1,9},{5... | collective-permute-start | bytes 3145736 | tf_op jit(solution)/shard_map/ppermute | solution.py:116
  136.1 32.3 %collective-permute-start.15 = (bf16[256,2048]{1,0:T(8,128)(2,1)}, bf16[256,2048]{1,0:T(8,128)(2,1)S(1)}, u32[]{:S(2)}, u32[]{:S(2)}) collective-permute-start(bf16[256,2048]{1,0:T(8,128)(2,1)} %collective-permute-done.6.x_ref.refs_2_), channel_id=1, source_target_pairs={{0,1},{1,2},{2,3},{3,0},{4,5},{5,6},{6,7},{7,4},{8,9},{9,10},{10,1... | collective-permute-start | bytes 3145736 | tf_op jit(solution)/shard_map/ppermute | solution.py:49
  185.6 52.6 %collective-permute-start.18 = (bf16[256,2048]{1,0:T(8,128)(2,1)}, bf16[256,2048]{1,0:T(8,128)(2,1)S(1)}, u32[]{:S(2)}, u32[]{:S(2)}) collective-permute-start(bf16[256,2048]{1,0:T(8,128)(2,1)} %get-tuple-element.133.x_ref.refs_0_), channel_id=1, source_target_pairs={{0,1},{1,2},{2,3},{3,0},{4,5},{5,6},{6,7},{7,4},{8,9},{9,10},{10,1... | collective-permute-start | bytes 3145736 | tf_op jit(solution)/shard_map/ppermute | solution.py:49
  185.7 54.5 %collective-permute-start.19 = (bf16[256,2048]{1,0:T(8,128)(2,1)}, bf16[256,2048]{1,0:T(8,128)(2,1)S(1)}, u32[]{:S(2)}, u32[]{:S(2)}) collective-permute-start(bf16[256,2048]{1,0:T(8,128)(2,1)} %get-tuple-element.133.x_ref.refs_0_), channel_id=1, source_target_pairs={{0,3},{1,0},{2,1},{3,2},{4,7},{5,4},{6,5},{7,6},{8,11},{9,8},{10,9... | collective-permute-start | bytes 3145736 | tf_op jit(solution)/shard_map/ppermute | solution.py:49
  238.3 33.8 %collective-permute-start.21 = (bf16[256,2048]{1,0:T(8,128)(2,1)S(1)}, bf16[256,2048]{1,0:T(8,128)(2,1)S(1)}, u32[]{:S(2)}, u32[]{:S(2)}) collective-permute-start(bf16[256,2048]{1,0:T(8,128)(2,1)S(1)} %collective-permute-done.18.x_ref.refs_0_), channel_id=1, source_target_pairs={{0,1},{1,2},{2,3},{3,0},{4,5},{5,6},{6,7},{7,4},{8,9},{9,10},{10,1... | collective-permute-start | bytes 3145736 | tf_op jit(solution)/shard_map/ppermute | solution.py:49
  287.9 26.2 %collective-permute-start.22 = (bf16[256,2048]{1,0:T(8,128)(2,1)}, bf16[256,2048]{1,0:T(8,128)(2,1)}, u32[]{:S(2)}, u32[]{:S(2)}) collective-permute-start(bf16[256,2048]{1,0:T(8,128)(2,1)} %get-tuple-element.145), channel_id=1, source_target_pairs={{0,3},{1,0},{2,1},{3,2},{4,7},{5,4},{6,5},{7,6},{8,11},{9,8},{10,9... | collective-permute-start | bytes 3145736 | tf_op jit(solution)/shard_map/ppermute | solution.py:49
  291.5 61.5 %collective-permute-start.20 = (bf16[256,2048]{1,0:T(8,128)(2,1)}, bf16[256,2048]{1,0:T(8,128)(2,1)S(1)}, u32[]{:S(2)}, u32[]{:S(2)}) collective-permute-start(bf16[256,2048]{1,0:T(8,128)(2,1)} %slice.103), channel_id=1, source_target_pairs={{0,1},{1,2},{2,3},{3,0},{4,5},{5,6},{6,7},{7,4},{8,9},{9,10},{10,1... | collective-permute-start | bytes 3145736 | tf_op jit(solution)/shard_map/ppermute | solution.py:49
  316.8 43.2 %collective-permute-start.23 = (bf16[256,2048]{1,0:T(8,128)(2,1)}, bf16[256,2048]{1,0:T(8,128)(2,1)S(1)}, u32[]{:S(2)}, u32[]{:S(2)}) collective-permute-start(bf16[256,2048]{1,0:T(8,128)(2,1)} %add_convert_fusion.3), channel_id=1, source_target_pairs={{0,3},{1,0},{2,1},{3,2},{4,7},{5,4},{6,5},{7,6},{8,11},{9,8},{10,9... | collective-permute-start | bytes 3145736 | tf_op jit(solution)/shard_map/ppermute | solution.py:49
  332.3 224.1 %reduce-scatter.5.cloned.1.call-start = ((), (), s32[]{:S(2)}) async-start(), calls=%async_computation.5 | async-start | bytes 11796480 | tf_op jit(solution)/shard_map/reduce_scatter | solution.py:989
  365.3 44.4 %collective-permute-start.24 = (bf16[256,2048]{1,0:T(8,128)(2,1)}, bf16[256,2048]{1,0:T(8,128)(2,1)}, u32[]{:S(2)}, u32[]{:S(2)}) collective-permute-start(bf16[256,2048]{1,0:T(8,128)(2,1)} %slice.109), channel_id=1, source_target_pairs={{0,1},{1,2},{2,3},{3,0},{4,5},{5,6},{6,7},{7,4},{8,9},{9,10},{10,1... | collective-permute-start | bytes 3145736 | tf_op jit(solution)/shard_map/ppermute | solution.py:49
  365.8 48.0 %collective-permute-start.25 = (bf16[256,2048]{1,0:T(8,128)(2,1)}, bf16[256,2048]{1,0:T(8,128)(2,1)}, u32[]{:S(2)}, u32[]{:S(2)}) collective-permute-start(bf16[256,2048]{1,0:T(8,128)(2,1)} %fusion.7), channel_id=1, source_target_pairs={{0,3},{1,0},{2,1},{3,2},{4,7},{5,4},{6,5},{7,6},{8,11},{9,8},{10,9... | collective-permute-start | bytes 3145736 | tf_op jit(solution)/shard_map/ppermute | solution.py:49
  460.4 62.6 %collective-permute-start.33 = (bf16[1024,512]{1,0:T(8,128)(2,1)}, bf16[1024,512]{1,0:T(8,128)(2,1)}, u32[]{:S(2)}, u32[]{:S(2)}) collective-permute-start(bf16[1024,512]{1,0:T(8,128)(2,1)} %weight_grad.11), channel_id=1, source_target_pairs={{0,1},{1,2},{2,3},{3,0},{4,5},{5,6},{6,7},{7,4},{8,9},{9,10},{10,1... | collective-permute-start | bytes 3145736 | tf_op jit(solution)/shard_map/ppermute | solution.py:49
  460.5 48.3 %collective-permute-start.30 = (bf16[1024,512]{1,0:T(8,128)(2,1)}, bf16[1024,512]{1,0:T(8,128)(2,1)}, u32[]{:S(2)}, u32[]{:S(2)}) collective-permute-start(bf16[1024,512]{1,0:T(8,128)(2,1)} %weight_grad.10), channel_id=1, source_target_pairs={{0,3},{1,0},{2,1},{3,2},{4,7},{5,4},{6,5},{7,6},{8,11},{9,8},{10,9... | collective-permute-start | bytes 3145736 | tf_op jit(solution)/shard_map/ppermute | solution.py:49
  550.5 40.0 %collective-permute-start.32 = (bf16[256,2048]{1,0:T(8,128)(2,1)}, bf16[256,2048]{1,0:T(8,128)(2,1)}, u32[]{:S(2)}, u32[]{:S(2)}) collective-permute-start(bf16[256,2048]{1,0:T(8,128)(2,1)} %add_convert_fusion.2), channel_id=1, source_target_pairs={{0,3},{1,0},{2,1},{3,2},{4,7},{5,4},{6,5},{7,6},{8,11},{9,8},{10,9... | collective-permute-start | bytes 3145736 | tf_op jit(solution)/shard_map/ppermute | solution.py:49
  560.1 25.9 %collective-permute-start.41 = (bf16[336,512]{1,0:T(8,128)(2,1)}, bf16[336,512]{1,0:T(8,128)(2,1)S(1)}, u32[]{:S(2)}, u32[]{:S(2)}) collective-permute-start(bf16[336,512]{1,0:T(8,128)(2,1)} %get-tuple-element.187), channel_id=1, source_target_pairs={{0,3},{1,0},{2,1},{3,2},{4,7},{5,4},{6,5},{7,6},{8,11},{9,8},{10,9... | collective-permute-start | bytes 1032200 | tf_op jit(solution)/shard_map/ppermute | solution.py:49
  565.7 29.8 %collective-permute-start.43 = (bf16[336,512]{1,0:T(8,128)(2,1)}, bf16[336,512]{1,0:T(8,128)(2,1)S(1)}, u32[]{:S(2)}, u32[]{:S(2)}) collective-permute-start(bf16[336,512]{1,0:T(8,128)(2,1)} %get-tuple-element.188), channel_id=1, source_target_pairs={{0,1},{1,2},{2,3},{3,0},{4,5},{5,6},{6,7},{7,4},{8,9},{9,10},{10,1... | collective-permute-start | bytes 1032200 | tf_op jit(solution)/shard_map/ppermute | solution.py:49
  (73 other events, 931.2 us)
Sparse Core Ops, SparseCore 0:
  40.8 68.4 all-gather.2
  111.8 111.6 all-gather.4
  332.4 115.8 reduce-scatter.2
  452.1 81.7 reduce-scatter.4

commit v3 on v2

--- a/solution.py
+++ b/solution.py
@@ -940,7 +940,7 @@
     acts, _ = after(acts, passed)
     grad_mlp = feed_grad(acts, [grads_t[s] for s in order], 2, 1, grad_mlp)
     second_grad = ring_sum(part_slots[0], from_left, from_right)
-    mlp_parts = [contract(act[2], feed_low[2], 1, 1).astype(LOW) for act in acts]
+    mlp_parts = [contract(act[2], feed_low[2], 1, 1).astype(LOW) for act in acts[1:]]
     second_grad, (_, mlp_parts) = after(second_grad, (grad_mlp, mlp_parts))
     owned_mlp = lax.psum_scatter(grad_mlp, "dp", scatter_dimension=1, tiled=True)
 
@@ -951,7 +951,7 @@
     second_gain_grad = jnp.sum(second_grad * second_unit, 0)
     back = residual_grad.astype(LOW)
     mlp_slots = [None] * n
-    for group, part in zip(groups, mlp_parts):
+    for group, part in zip(groups[1:], mlp_parts):
         for i, s in enumerate(group):
             mlp_slots[s] = part[i * rows : (i + 1) * rows]
     block_far, block_left = ring_most(mlp_slots, n), ring_way(mlp_slots, n, 1)
@@ -985,29 +985,29 @@
         first_normalized, grad_kv_t, span, 2 * KVD, 1, lambda i: 0, lambda i: heads_cols,
         None, grad_pack,
     )
-    grad_pack, owned_mlp = after(grad_pack, owned_mlp)
-    owned_pack = lax.psum_scatter(grad_pack, "dp", scatter_dimension=0, tiled=True)
-
-    query_slots, last = [None] * n, grad_pack
+    query_slots, last, own_act = [None] * n, grad_pack, acts[0][2]
     for s in order[::-1]:
+        if s == order[n // 2 - 1]:
+            own_act, _ = after(own_act, last)
+            mlp_slots[0] = contract(own_act, feed_low[2], 1, 1).astype(LOW)
+            grad_pack, (owned_mlp, _, _) = after(grad_pack, (owned_mlp, last, mlp_slots[0]))
+            owned_pack = lax.psum_scatter(grad_pack, "dp", scatter_dimension=0, tiled=True)
+            owned_gateup, owned_down = owned_mlp[:2], owned_mlp[2]
+            gateup_up = adamw(
+                gateup_weight, gateup_first, gateup_second, owned_gateup.astype(F32), RATE_GATEUP,
+                DECAY,
+            )
+            down_up = adamw_turned(down_weight, down_first, down_second, owned_down, RATE_DOWN)
+            last = (last, gateup_up, down_up)
         query_rows, _ = after(first_normalized, last)
         last = query_slots[s] = weight_grad(
             query_rows, grad_q_t, cols, cols, 1, lambda i, s=s: s, lambda i: 0, places[0], None,
             partner, lambda i, s=s: s,
         )
     query_far, query_left = ring_most(query_slots, n), ring_way(query_slots, n, 1)
-    owned_gateup, owned_down = owned_mlp[:2], owned_mlp[2]
-    gateup_up = adamw(
-        gateup_weight, gateup_first, gateup_second, owned_gateup.astype(F32), RATE_GATEUP, DECAY
-    )
-    down_up = adamw_turned(down_weight, down_first, down_second, owned_down, RATE_DOWN)
-    query_right = ring_last(query_slots, n, query_far, (gateup_up, down_up))
+    query_right = ring_last(query_slots, n, query_far)
     query_sum = ring_sum(query_slots[0], query_left, query_right).astype(LOW)
     block_right = ring_last(mlp_slots, n, block_far, query_right)
-    block_out = residual + ring_sum(mlp_slots[0], block_left, block_right)
-    own_query = dp_scatter(query_sum, sizes["dp"], ()).astype(F32)
-    query_up = adamw(query_weight, query_first, query_second, own_query, RATE_QUERY, DECAY)
-
     (back_q_t, back_kv_t), _ = after((grad_q_t, grad_kv_t), query_slots)
     grad_qkv_t = jnp.concatenate(
         [back_q_t, back_kv_t, jnp.zeros((attn_low.shape[1] - span, rows), LOW)], 0
@@ -1026,7 +1026,12 @@
     gain_cols = jnp.pad(gain_grads.T, ((0, 0), (0, 126)))
 
     slots = tail_pack(ids, owned_pack, gain_cols, piece, cols)
+    query_sum, _ = after(query_sum, slots[0])
+    own_query = dp_scatter(query_sum, sizes["dp"], ()).astype(F32)
+    query_up = adamw(query_weight, query_first, query_second, own_query, RATE_QUERY, DECAY)
     parts = [slots[0], ring_way(slots, n, -1), ring_way(slots, n, 1)]
+    block_right, _ = after(block_right, parts[1])
+    block_out = residual + ring_sum(mlp_slots[0], block_left, block_right)
     states = [output_weight, output_first, output_second, keyval_weight, keyval_first]
     states += [keyval_second, gains, gains_first, gains_second]
     parts = [part for part in parts if part is not None]

time: 614 us -> 625 us (1.018)
  waiting for transfers between devices: 188 us -> 204 us
    ppermute x30, waiting for transfers between devices: 107 us -> 117 us  [shift(): return lax.ppermute(x, 'tensor', [(i, (i + by) % n) for i in range(n)])]
    reduce_scatter x1, waiting for transfers between devices: 0.02 us -> 7.25 us  [on_device(): lax.psum_scatter(grad_pack, 'dp', scatter_dimension=0, tiled=True)]
  transfers between devices with their start and end apart: 48 -> 48, of which waited for: 26 -> 27; matrix products, arithmetic and copies ran while one was open for 15% -> 14% of each run, Pallas kernels for 36% -> 35%
where the time goes in v3:
time: 625 us; the launch traced here: 619 us
  Pallas kernels  245 us (39%)
  waiting for transfers between devices  204 us (33%)
  starting transfers between devices  66.9 us (11%)
  other arithmetic  38.4 us (6%)
  matrix products  28.9 us (5%)
  local copies, waits for them, and re-layouts  20.8 us (3%)
  between operations  14.8 us (2%)
    ppermute x30, waiting for transfers between devices, shift(): return lax.ppermute(x, 'tensor', [(i, (i + by) % n) for i in range(n)])  117 us
    pallas_call x3, Pallas kernels, feed(): pl.pallas_call(functools.partial(feed_kernel, pieces, count), in_specs=[v...  56 us
    ppermute x30, starting transfers between devices, shift(): return lax.ppermute(x, 'tensor', [(i, (i + by) % n) for i in range(n)])  53.8 us
    pallas_call x1, Pallas kernels, attend_back(): pl.pallas_call(functools.partial(attend_back_kernel, slots, heads, len(we...  40.2 us
    all_gather x1, waiting for transfers between devices, on_device(): attn_low = lax.all_gather(attn_in, 'dp', axis=0, tiled=True)  39.5 us
    pallas_call x7, Pallas kernels, weight_grad(): pl.pallas_call(functools.partial(weight_grad_kernel, count, add is not No...  33.7 us
    pallas_call x2, Pallas kernels, feed_grad(): pl.pallas_call(functools.partial(feed_grad_kernel, halves, n), grid=(part...  29.5 us
    dot_general x4, matrix products, contract(): lax.dot_general(left, right, (((dim_left,), (dim_right,)), ((), ())), pre...  28.9 us
  transfers between devices with their start and end apart: 48, of which 27 were waited for; matrix products, arithmetic and copies ran while one was open for 14% of the time, Pallas kernels for 35%

profile of v3, /device:TPU:0, one launch (start us, length us, event | category | flops | bytes accessed | tf_op | source)
XLA Modules:
  0.0 618.9 jit_solution(2001185441936308643)
XLA Ops:
  14.3 9.1 %collective-permute-done.refs_1_ = bf16[336,512]{1,0:T(8,128)(2,1)S(1)} collective-permute-done((bf16[336,512]{1,0:T(8,128)(2,1)}, bf16[336,512]{1,0:T(8,128)(2,1)S(1)}, u32[]{:S(2)}, u32[]{:S(2)}) %collective-permute-start) | collective-permute-done | bytes 344096 | tf_op jit(solution)/shard_map/ppermute | solution.py:49
  29.7 7.8 %collective-permute-done.1.refs_2_ = bf16[336,512]{1,0:T(8,128)(2,1)} collective-permute-done((bf16[336,512]{1,0:T(8,128)(2,1)S(1)}, bf16[336,512]{1,0:T(8,128)(2,1)}, u32[]{:S(2)}, u32[]{:S(2)}) %collective-permute-start.1) | collective-permute-done | bytes 344096 | tf_op jit(solution)/shard_map/ppermute | solution.py:49
  44.8 7.3 %collective-permute-done.3 = bf16[256,512]{1,0:T(8,128)(2,1)S(1)} collective-permute-done((bf16[256,512]{1,0:T(8,128)(2,1)S(1)}, bf16[256,512]{1,0:T(8,128)(2,1)S(1)}, u32[]{:S(2)}, u32[]{:S(2)}) %collective-permute-start.3) | collective-permute-done | bytes 262176 | tf_op jit(solution)/shard_map/ppermute | solution.py:49
  70.5 39.5 %all-gather.3.cloned.1.call-done.gain_ref.weight_ref = bf16[2048,2688]{1,0:T(8,128)(2,1)} async-done(((bf16[256,2688]{1,0:T(8,128)(2,1)}), bf16[2048,2688]{1,0:T(8,128)(2,1)}) %all-gather.3.cloned.1.call-update) | async-done | bytes 11010064 | tf_op jit(solution)/shard_map/all_gather | solution.py:874
  125.1 7.0 %project.1.q_ref = bf16[2048,256]{1,0:T(8,128)(2,1)} custom-call(bf16[256,2048]{1,0:T(8,128)(2,1)} %get-tuple-element.179.rows_ref, bf16[2048,2688]{1,0:T(8,128)(2,1)} %all-gather.3.cloned.1.call-done.gain_ref.weight_ref, f32[32,256]{1,0:T(8,128)} %get-tuple-element.111.cos_ref.refs_6_, f32[32,256]{1,0:T(8,128)} %get-tuple-element.112.sin_ref.refs_7_), custom_call_target="tpu_custom_call" | custom-call | flops 9200000000 | bytes 1000000 | tf_op jit(solution)/shard_map/project/pallas_call | solution.py:308
  137.0 22.0 %attend.1 = (bf16[2048,256]{1,0:T(8,128)(2,1)}, bf16[256,2048]{1,0:T(8,128)(2,1)}, f32[4,8,256]{2,1,0:T(8,128)}) custom-call(s32[25]{0:T(128)} %concatenate.35.meta_ref, s32[1,256]{1,0:T(1,128)} %bitcast.102, bf16[2048,256]{1,0:T(8,128)(2,1)} %project.1.q_ref, bf16[4,512,256]{2,1,0:T(8,128)(2,1)} %pad_maximum_fusion.3.kv_ref), custom_call_target="tpu_custom_call" | custom-call | flops 8589934592 | bytes 2097152 | tf_op jit(solution)/shard_map/attend/pallas_call | solution.py:368
  159.0 8.1 %collective-permute-done.13 = bf16[256,2048]{1,0:T(8,128)(2,1)S(1)} collective-permute-done((bf16[256,2048]{1,0:T(8,128)(2,1)S(1)}, bf16[256,2048]{1,0:T(8,128)(2,1)S(1)}, u32[]{:S(2)}, u32[]{:S(2)}) %collective-permute-start.13) | collective-permute-done | bytes 1048608 | tf_op jit(solution)/shard_map/ppermute | solution.py:116
  181.0 8.8 %mix.1 = (f32[256,2048]{1,0:T(8,128)}, bf16[256,2048]{1,0:T(8,128)(2,1)}, f32[256,1]{1,0:T(8,128)}) custom-call(s32[16]{0:T(128)} %concatenate.34.order_ref, bf16[256,2048]{1,0:T(8,128)(2,1)} %get-tuple-element.118.o_ref, bf16[256,2048]{1,0:T(8,128)(2,1)} %x_ref.3, f32[1,2048]{1,0:T(1,128)} %get-tuple-element.225.gain_ref, bf16[512,2048]{1,0:T(8,128)(2,1)} %copy-done.20, ...), custom_call_target="tpu_custom_call" | custom-call | flops 6899999744 | bytes 1000000 | tf_op jit(solution)/shard_map/mix/pallas_call | solution.py:518
  206.7 16.7 %all-gather.5.cloned.1.call-done.refs_2_.refs_4_ = bf16[3,2048,1408]{2,1,0:T(8,128)(2,1)} async-done(((bf16[3,256,1408]{2,1,0:T(8,128)(2,1)}), bf16[3,2048,1408]{2,1,0:T(8,128)(2,1)}) %all-gather.5.cloned.1.call-update) | async-done | bytes 17301520 | tf_op jit(solution)/shard_map/all_gather | solution.py:880
  223.5 14.8 %feed.3 = (bf16[3,256,1408]{2,1,0:T(8,128)(2,1)}, bf16[256,2048]{1,0:T(8,128)(2,1)}) custom-call(bf16[256,2048]{1,0:T(8,128)(2,1)} %get-tuple-element.134.x_ref.refs_0_, bf16[256,2048]{1,0:T(8,128)(2,1)} %refs_1_, bf16[3,2048,1408]{2,1,0:T(8,128)(2,1)} %all-gather.5.cloned.1.call-done.refs_2_.refs_4_), custom_call_target="tpu_custom_call" | custom-call | flops 1150000000 | bytes 1000000 | tf_op jit(solution)/shard_map/feed/pallas_call | solution.py:739
  245.6 26.3 %feed.4 = (bf16[3,512,1408]{2,1,0:T(8,128)(2,1)}, bf16[512,2048]{1,0:T(8,128)(2,1)}) custom-call(bf16[256,2048]{1,0:T(8,128)(2,1)} %copy-done.27, bf16[256,2048]{1,0:T(8,128)(2,1)} %copy-done.28, bf16[256,2048]{1,0:T(8,128)(2,1)} %collective-permute-done.6.x_ref.refs_2_, bf16[256,2048]{1,0:T(8,128)(2,1)} %copy-done.26, ...), custom_call_target="tpu_custom_call" | custom-call | flops 1150000000 | bytes 1000000 | tf_op jit(solution)/shard_map/feed/pallas_call | solution.py:739
  273.0 14.9 %feed.5 = (bf16[3,256,1408]{2,1,0:T(8,128)(2,1)}, bf16[256,2048]{1,0:T(8,128)(2,1)}) custom-call(bf16[256,2048]{1,0:T(8,128)(2,1)} %copy-done.25, bf16[256,2048]{1,0:T(8,128)(2,1)} %copy-done.23, bf16[3,2048,1408]{2,1,0:T(8,128)(2,1)} %all-gather.5.cloned.1.call-done.refs_2_.refs_4_), custom_call_target="tpu_custom_call" | custom-call | flops 1150000000 | bytes 1000000 | tf_op jit(solution)/shard_map/feed/pallas_call | solution.py:739
  294.2 18.3 %feed_grad.2.refs_7_ = bf16[3,2048,1408]{2,1,0:T(8,128)(2,1)} custom-call(bf16[3,256,1408]{2,1,0:T(8,128)(2,1)} %get-tuple-element.153.refs_0_, bf16[3,512,1408]{2,1,0:T(8,128)(2,1)} %get-tuple-element.155.refs_1_, bf16[3,256,1408]{2,1,0:T(8,128)(2,1)} %get-tuple-element.156.refs_2_, bf16[2048,256]{1,0:T(8,128)(2,1)} %turned.12.refs_3_, ...), custom_call_target="tpu_custom_call" | custom-call | flops 1150000000 | bytes 1000000 | tf_op jit(solution)/shard_map/feed_grad/pallas_call | solution.py:792
  321.0 11.2 %feed_grad.3 = bf16[3,2048,1408]{2,1,0:T(8,128)(2,1)} custom-call(bf16[3,256,1408]{2,1,0:T(8,128)(2,1)} %get-tuple-element.153.refs_0_, bf16[3,512,1408]{2,1,0:T(8,128)(2,1)} %get-tuple-element.155.refs_1_, bf16[3,256,1408]{2,1,0:T(8,128)(2,1)} %get-tuple-element.156.refs_2_, bf16[2048,256]{1,0:T(8,128)(2,1)} %turned.8.refs_3_, ...), custom_call_target="tpu_custom_call", output_to_operand_aliasing={{}: (7, {})} | custom-call | flops 1150000000 | bytes 1000000 | tf_op jit(solution)/shard_map/feed_grad/pallas_call | solution.py:792
  338.1 8.0 %fusion.3 = bf16[512,2048]{1,0:T(8,128)(2,1)S(1)} fusion(bf16[3,2048,1408]{2,1,0:T(8,128)(2,1)} %all-gather.5.cloned.1.call-done.refs_2_.refs_4_, bf16[3,512,1408]{2,1,0:T(8,128)(2,1)} %get-tuple-element.155.refs_1_), kind=kOutput, calls=%fused_computation.6 | convolution fusion | flops 2953838592 | bytes 9306112 | tf_op jit(solution)/shard_map/dot_general | solution.py:39
  346.2 13.9 %collective-permute-done.23 = bf16[256,2048]{1,0:T(8,128)(2,1)S(1)} collective-permute-done((bf16[256,2048]{1,0:T(8,128)(2,1)}, bf16[256,2048]{1,0:T(8,128)(2,1)S(1)}, u32[]{:S(2)}, u32[]{:S(2)}) %collective-permute-start.23) | collective-permute-done | bytes 1048608 | tf_op jit(solution)/shard_map/ppermute | solution.py:49
  368.2 40.2 %attend_back.1 = (bf16[2048,256]{1,0:T(8,128)(2,1)}, bf16[4,512,256]{2,1,0:T(8,128)(2,1)}) custom-call(s32[25]{0:T(128)} %concatenate.35.meta_ref, s32[1,256]{1,0:T(1,128)} %bitcast.103, bf16[2048,256]{1,0:T(8,128)(2,1)} %project.1.q_ref, bf16[4,512,256]{2,1,0:T(8,128)(2,1)} %pad_maximum_fusion.3.kv_ref, bf16[256,2048]{1,0:T(8,128)(2,1)} %fusion.25.back_ref.rows_ref, ...), custom_call_target="tpu_custom_call" | custom-call | flops 200000000753664 | bytes 1000000 | tf_op jit(solution)/shard_map/attend_back/pallas_call | solution.py:459
  440.2 7.7 %weight_grad.8.rest_0_ = bf16[2048,2560]{1,0:T(8,128)(2,1)} custom-call(s32[16]{0:T(128)} %iota.13.order_ref, bf16[256,2048]{1,0:T(8,128)(2,1)} %fusion.25.back_ref.rows_ref, bf16[2048,256]{1,0:T(8,128)(2,1)} %get-tuple-element.158.refs_4_.x_ref), custom_call_target="tpu_custom_call" | custom-call | flops 7850666496 | bytes 1000000 | tf_op jit(solution)/shard_map/weight_grad/pallas_call | solution.py:654
  471.7 11.1 %adamw_turned.1 = (f32[1408,256]{1,0:T(8,128)}, f32[1408,256]{1,0:T(8,128)}, f32[1408,256]{1,0:T(8,128)}) custom-call(f32[1408,256]{1,0:T(8,128)} %weight.1, f32[1408,256]{1,0:T(8,128)} %first.1, f32[1408,256]{1,0:T(8,128)} %second.1, bf16[256,1408]{1,0:T(8,128)(2,1)} %slice_bitcast_fusion.10.grad), custom_call_target="tpu_custom_call" | custom-call | flops 4325376 | bytes 10092544 | tf_op jit(solution)/shard_map/adamw_turned/pallas_call | solution.py:820
  502.8 9.7 %multiply_reduce_fusion = (f32[256]{0:T(256)S(1)}, f32[2048]{0:T(1024)S(1)}, f32[256,2048]{1,0:T(8,128)}) fusion(bf16[256,2048]{1,0:T(8,128)(2,1)S(1)} %copy-done.10, f32[2048]{0:T(1024)S(1)} %bitcast.98, f32[256]{0:T(256)S(1)} %reduce.1, bf16[2048,2688]{1,0:T(8,128)(2,1)} %all-gather.3.cloned.1.call-done.gain_ref.weight_ref, ...), kind=kOutput, calls=%fused_computation.17 | convolution fusion | flops 2826368768 | bytes 15490304 | tf_op jit(solution)/shard_map/dot_general | solution.py:39
  525.7 13.5 %collective-permute-done.31 = bf16[1024,512]{1,0:T(8,128)(2,1)} collective-permute-done((bf16[1024,512]{1,0:T(8,128)(2,1)}, bf16[1024,512]{1,0:T(8,128)(2,1)}, u32[]{:S(2)}, u32[]{:S(2)}) %collective-permute-start.31) | collective-permute-done | bytes 1048608 | tf_op jit(solution)/shard_map/ppermute | solution.py:49
  541.1 7.2 %reduce-scatter.5.cloned.1.call-done.owned_ref = bf16[256,2560]{1,0:T(8,128)(2,1)} async-done(((bf16[2048,2560]{1,0:T(8,128)(2,1)}), bf16[256,2560]{1,0:T(8,128)(2,1)}) %reduce-scatter.5.cloned.1.call-update) | async-done | bytes 1310736 | tf_op jit(solution)/shard_map/reduce_scatter | solution.py:994
  573.7 17.1 %collective-permute-done.32 = bf16[256,2048]{1,0:T(8,128)(2,1)S(1)} collective-permute-done((bf16[256,2048]{1,0:T(8,128)(2,1)S(1)}, bf16[256,2048]{1,0:T(8,128)(2,1)S(1)}, u32[]{:S(2)}, u32[]{:S(2)}) %collective-permute-start.32) | collective-permute-done | bytes 1048608 | tf_op jit(solution)/shard_map/ppermute | solution.py:49
  590.8 12.2 %collective-permute-done.37.refs_1_ = bf16[336,512]{1,0:T(8,128)(2,1)S(1)} collective-permute-done((bf16[336,512]{1,0:T(8,128)(2,1)S(1)}, bf16[336,512]{1,0:T(8,128)(2,1)S(1)}, u32[]{:S(2)}, u32[]{:S(2)}) %collective-permute-start.37) | collective-permute-done | bytes 344096 | tf_op jit(solution)/shard_map/ppermute | solution.py:49
  (284 shorter events, 251.5 us)
Async XLA Ops:
  7.2 102.8 %all-gather.3.cloned.1.call-start = ((), (), s32[]{:S(2)}) async-start(), calls=%async_computation.2 | async-start | bytes 12386304 | tf_op jit(solution)/shard_map/all_gather | solution.py:874
  40.7 182.7 %all-gather.5.cloned.1.call-start = ((), (), s32[]{:S(2)}) async-start(), calls=%async_computation.3 | async-start | bytes 19464192 | tf_op jit(solution)/shard_map/all_gather | solution.py:880
  60.3 407.1 %reduce-scatter.3.cloned.1.call-start = ((), (), s32[]{:S(2)}) async-start(), calls=%async_computation.4 | async-start | bytes 19464192 | tf_op jit(solution)/shard_map/reduce_scatter | solution.py:945
  63.4 56.8 %collective-permute-start.6 = (bf16[256,2048]{1,0:T(8,128)(2,1)S(1)}, bf16[256,2048]{1,0:T(8,128)(2,1)}, u32[]{:S(2)}, u32[]{:S(2)}) collective-permute-start(bf16[256,2048]{1,0:T(8,128)(2,1)S(1)} %copy-done.7), channel_id=1, source_target_pairs={{0,1},{1,2},{2,3},{3,0},{4,5},{5,6},{6,7},{7,4},{8,9},{9,10},{10,1... | collective-permute-start | bytes 3145736 | tf_op jit(solution)/shard_map/ppermute | solution.py:49
  63.4 56.7 %collective-permute-start.7 = (bf16[256,2048]{1,0:T(8,128)(2,1)S(1)}, bf16[256,2048]{1,0:T(8,128)(2,1)S(1)}, u32[]{:S(2)}, u32[]{:S(2)}) collective-permute-start(bf16[256,2048]{1,0:T(8,128)(2,1)S(1)} %copy-done.7), channel_id=1, source_target_pairs={{0,3},{1,0},{2,1},{3,2},{4,7},{5,4},{6,5},{7,6},{8,11},{9,8},{10,9... | collective-permute-start | bytes 3145736 | tf_op jit(solution)/shard_map/ppermute | solution.py:49
  67.4 47.3 %collective-permute-start.11 = (bf16[128,2048]{1,0:T(8,128)(2,1)S(1)}, bf16[128,2048]{1,0:T(8,128)(2,1)}, u32[]{:S(2)}, u32[]{:S(2)}) collective-permute-start(bf16[128,2048]{1,0:T(8,128)(2,1)S(1)} %get-tuple-element.221), channel_id=1, source_target_pairs={{0,8},{4,12},{8,0},{12,4},{16,24},{20,28},{24,16},{28,20},{1,9},{5... | collective-permute-start | bytes 1572872 | tf_op jit(solution)/shard_map/ppermute | solution.py:116
  69.0 46.9 %collective-permute-start.12 = (bf16[128,2048]{1,0:T(8,128)(2,1)S(1)}, bf16[128,2048]{1,0:T(8,128)(2,1)}, u32[]{:S(2)}, u32[]{:S(2)}) collective-permute-start(bf16[128,2048]{1,0:T(8,128)(2,1)S(1)} %get-tuple-element.220), channel_id=1, source_target_pairs={{0,16},{4,20},{8,24},{12,28},{16,0},{20,4},{24,8},{28,12},{1,17},{... | collective-permute-start | bytes 1572872 | tf_op jit(solution)/shard_map/ppermute | solution.py:116
  120.1 47.0 %collective-permute-start.13 = (bf16[256,2048]{1,0:T(8,128)(2,1)S(1)}, bf16[256,2048]{1,0:T(8,128)(2,1)S(1)}, u32[]{:S(2)}, u32[]{:S(2)}) collective-permute-start(bf16[256,2048]{1,0:T(8,128)(2,1)S(1)} %pad_maximum_fusion.4), channel_id=1, source_target_pairs={{0,16},{4,20},{8,24},{12,28},{16,0},{20,4},{24,8},{28,12},{1,17},{... | collective-permute-start | bytes 3145736 | tf_op jit(solution)/shard_map/ppermute | solution.py:116
  121.7 47.5 %collective-permute-start.14 = (bf16[256,2048]{1,0:T(8,128)(2,1)S(1)}, bf16[256,2048]{1,0:T(8,128)(2,1)S(1)}, u32[]{:S(2)}, u32[]{:S(2)}) collective-permute-start(bf16[256,2048]{1,0:T(8,128)(2,1)S(1)} %pad_maximum_fusion.5), channel_id=1, source_target_pairs={{0,8},{4,12},{8,0},{12,4},{16,24},{20,28},{24,16},{28,20},{1,9},{5... | collective-permute-start | bytes 3145736 | tf_op jit(solution)/shard_map/ppermute | solution.py:116
  136.8 34.0 %collective-permute-start.15 = (bf16[256,2048]{1,0:T(8,128)(2,1)}, bf16[256,2048]{1,0:T(8,128)(2,1)S(1)}, u32[]{:S(2)}, u32[]{:S(2)}) collective-permute-start(bf16[256,2048]{1,0:T(8,128)(2,1)} %collective-permute-done.6.x_ref.refs_2_), channel_id=1, source_target_pairs={{0,1},{1,2},{2,3},{3,0},{4,5},{5,6},{6,7},{7,4},{8,9},{9,10},{10,1... | collective-permute-start | bytes 3145736 | tf_op jit(solution)/shard_map/ppermute | solution.py:49
  189.9 48.4 %collective-permute-start.18 = (bf16[256,2048]{1,0:T(8,128)(2,1)}, bf16[256,2048]{1,0:T(8,128)(2,1)S(1)}, u32[]{:S(2)}, u32[]{:S(2)}) collective-permute-start(bf16[256,2048]{1,0:T(8,128)(2,1)} %get-tuple-element.134.x_ref.refs_0_), channel_id=1, source_target_pairs={{0,1},{1,2},{2,3},{3,0},{4,5},{5,6},{6,7},{7,4},{8,9},{9,10},{10,1... | collective-permute-start | bytes 3145736 | tf_op jit(solution)/shard_map/ppermute | solution.py:49
  190.0 50.2 %collective-permute-start.19 = (bf16[256,2048]{1,0:T(8,128)(2,1)}, bf16[256,2048]{1,0:T(8,128)(2,1)S(1)}, u32[]{:S(2)}, u32[]{:S(2)}) collective-permute-start(bf16[256,2048]{1,0:T(8,128)(2,1)} %get-tuple-element.134.x_ref.refs_0_), channel_id=1, source_target_pairs={{0,3},{1,0},{2,1},{3,2},{4,7},{5,4},{6,5},{7,6},{8,11},{9,8},{10,9... | collective-permute-start | bytes 3145736 | tf_op jit(solution)/shard_map/ppermute | solution.py:49
  238.3 33.7 %collective-permute-start.20 = (bf16[256,2048]{1,0:T(8,128)(2,1)S(1)}, bf16[256,2048]{1,0:T(8,128)(2,1)S(1)}, u32[]{:S(2)}, u32[]{:S(2)}) collective-permute-start(bf16[256,2048]{1,0:T(8,128)(2,1)S(1)} %collective-permute-done.18.x_ref.refs_0_), channel_id=1, source_target_pairs={{0,1},{1,2},{2,3},{3,0},{4,5},{5,6},{6,7},{7,4},{8,9},{9,10},{10,1... | collective-permute-start | bytes 3145736 | tf_op jit(solution)/shard_map/ppermute | solution.py:49
  291.5 54.6 %collective-permute-start.22 = (bf16[256,2048]{1,0:T(8,128)(2,1)}, bf16[256,2048]{1,0:T(8,128)(2,1)S(1)}, u32[]{:S(2)}, u32[]{:S(2)}) collective-permute-start(bf16[256,2048]{1,0:T(8,128)(2,1)} %slice.105), channel_id=1, source_target_pairs={{0,1},{1,2},{2,3},{3,0},{4,5},{5,6},{6,7},{7,4},{8,9},{9,10},{10,1... | collective-permute-start | bytes 3145736 | tf_op jit(solution)/shard_map/ppermute | solution.py:49
  316.8 43.3 %collective-permute-start.23 = (bf16[256,2048]{1,0:T(8,128)(2,1)}, bf16[256,2048]{1,0:T(8,128)(2,1)S(1)}, u32[]{:S(2)}, u32[]{:S(2)}) collective-permute-start(bf16[256,2048]{1,0:T(8,128)(2,1)} %add_convert_fusion.3), channel_id=1, source_target_pairs={{0,3},{1,0},{2,1},{3,2},{4,7},{5,4},{6,5},{7,6},{8,11},{9,8},{10,9... | collective-permute-start | bytes 3145736 | tf_op jit(solution)/shard_map/ppermute | solution.py:49
  332.3 216.1 %reduce-scatter.5.cloned.1.call-start = ((), (), s32[]{:S(2)}) async-start(), calls=%async_computation.5 | async-start | bytes 11796480 | tf_op jit(solution)/shard_map/reduce_scatter | solution.py:994
  364.2 44.2 %collective-permute-start.24 = (bf16[256,2048]{1,0:T(8,128)(2,1)}, bf16[256,2048]{1,0:T(8,128)(2,1)}, u32[]{:S(2)}, u32[]{:S(2)}) collective-permute-start(bf16[256,2048]{1,0:T(8,128)(2,1)} %fusion.6), channel_id=1, source_target_pairs={{0,3},{1,0},{2,1},{3,2},{4,7},{5,4},{6,5},{7,6},{8,11},{9,8},{10,9... | collective-permute-start | bytes 3145736 | tf_op jit(solution)/shard_map/ppermute | solution.py:49
  367.9 44.5 %collective-permute-start.25 = (bf16[256,2048]{1,0:T(8,128)(2,1)}, bf16[256,2048]{1,0:T(8,128)(2,1)}, u32[]{:S(2)}, u32[]{:S(2)}) collective-permute-start(bf16[256,2048]{1,0:T(8,128)(2,1)} %slice.109), channel_id=1, source_target_pairs={{0,1},{1,2},{2,3},{3,0},{4,5},{5,6},{6,7},{7,4},{8,9},{9,10},{10,1... | collective-permute-start | bytes 3145736 | tf_op jit(solution)/shard_map/ppermute | solution.py:49
  468.4 27.9 %collective-permute-start.30 = (bf16[1024,512]{1,0:T(8,128)(2,1)}, bf16[1024,512]{1,0:T(8,128)(2,1)}, u32[]{:S(2)}, u32[]{:S(2)}) collective-permute-start(bf16[1024,512]{1,0:T(8,128)(2,1)} %weight_grad.10), channel_id=1, source_target_pairs={{0,3},{1,0},{2,1},{3,2},{4,7},{5,4},{6,5},{7,6},{8,11},{9,8},{10,9... | collective-permute-start | bytes 3145736 | tf_op jit(solution)/shard_map/ppermute | solution.py:49
  470.8 54.9 %collective-permute-start.38 = (bf16[1024,512]{1,0:T(8,128)(2,1)}, bf16[1024,512]{1,0:T(8,128)(2,1)}, u32[]{:S(2)}, u32[]{:S(2)}) collective-permute-start(bf16[1024,512]{1,0:T(8,128)(2,1)} %weight_grad.11), channel_id=1, source_target_pairs={{0,1},{1,2},{2,3},{3,0},{4,5},{5,6},{6,7},{7,4},{8,9},{9,10},{10,1... | collective-permute-start | bytes 3145736 | tf_op jit(solution)/shard_map/ppermute | solution.py:49
  499.0 40.2 %collective-permute-start.31 = (bf16[1024,512]{1,0:T(8,128)(2,1)}, bf16[1024,512]{1,0:T(8,128)(2,1)}, u32[]{:S(2)}, u32[]{:S(2)}) collective-permute-start(bf16[1024,512]{1,0:T(8,128)(2,1)} %add_convert_fusion.1), channel_id=1, source_target_pairs={{0,3},{1,0},{2,1},{3,2},{4,7},{5,4},{6,5},{7,6},{8,11},{9,8},{10,9... | collective-permute-start | bytes 3145736 | tf_op jit(solution)/shard_map/ppermute | solution.py:49
  559.0 31.8 %collective-permute-start.32 = (bf16[256,2048]{1,0:T(8,128)(2,1)S(1)}, bf16[256,2048]{1,0:T(8,128)(2,1)S(1)}, u32[]{:S(2)}, u32[]{:S(2)}) collective-permute-start(bf16[256,2048]{1,0:T(8,128)(2,1)S(1)} %add_convert_fusion.2), channel_id=1, source_target_pairs={{0,3},{1,0},{2,1},{3,2},{4,7},{5,4},{6,5},{7,6},{8,11},{9,8},{10,9... | collective-permute-start | bytes 3145736 | tf_op jit(solution)/shard_map/ppermute | solution.py:49
  559.6 48.3 %collective-permute-start.43 = (bf16[336,512]{1,0:T(8,128)(2,1)S(1)}, bf16[336,512]{1,0:T(8,128)(2,1)S(1)}, u32[]{:S(2)}, u32[]{:S(2)}) collective-permute-start(bf16[336,512]{1,0:T(8,128)(2,1)S(1)} %copy-done.48), channel_id=1, source_target_pairs={{0,1},{1,2},{2,3},{3,0},{4,5},{5,6},{6,7},{7,4},{8,9},{9,10},{10,1... | collective-permute-start | bytes 1032200 | tf_op jit(solution)/shard_map/ppermute | solution.py:49
  567.7 35.3 %collective-permute-start.37 = (bf16[336,512]{1,0:T(8,128)(2,1)S(1)}, bf16[336,512]{1,0:T(8,128)(2,1)S(1)}, u32[]{:S(2)}, u32[]{:S(2)}) collective-permute-start(bf16[336,512]{1,0:T(8,128)(2,1)S(1)} %add_convert_fusion.4), channel_id=1, source_target_pairs={{0,3},{1,0},{2,1},{3,2},{4,7},{5,4},{6,5},{7,6},{8,11},{9,8},{10,9... | collective-permute-start | bytes 1032200 | tf_op jit(solution)/shard_map/ppermute | solution.py:49
  (76 other events, 1040.9 us)
Sparse Core Ops, SparseCore 0:
  40.8 69.1 all-gather.2
  112.5 110.9 all-gather.4
  332.4 115.8 reduce-scatter.2
  467.6 80.7 reduce-scatter.4

commit v4 on v2

--- a/solution.py
+++ b/solution.py
@@ -962,9 +962,11 @@
 
     places = [dp_order(sizes["dp"], block, odd) for odd in (0, 1)]
     kv_parts = [grad_kv[s] for s in range(n)]
-    kv_left, passed = ring_way(kv_parts, n, 1), []
-    own_kv = ring_sum(kv_parts[0], ring_way(kv_parts, n, -1, passed), kv_left)
-    query_rows, _ = after(first_normalized, (passed, kv_left))
+    kv_left = ring_way(kv_parts, n, 1)
+    block_right = ring_last(mlp_slots, n, block_far, grad_kv)
+    kv_far = ring_most(kv_parts, n)
+    own_kv = ring_sum(kv_parts[0], ring_last(kv_parts, n, kv_far, block_right), kv_left)
+    query_rows, _ = after(first_normalized, kv_far)
     partner = weight_grad(
         query_rows, grad_q_t, n * cols, cols, n, lambda i: i, lambda i: i, places[1]
     )
@@ -974,7 +976,7 @@
     grad_pack = weight_grad(
         out_rows, mixed_t, span, 2 * KVD, heads_cols, lambda i: i, lambda i: i
     )
-    own_kv, _ = after(own_kv, partner)
+
     grad_k = own_kv[:KVD].reshape(KVH, 2, HD // 2, rows)
     upper, lower = grad_k[:, 0], grad_k[:, 1]
     grad_k = jnp.stack([upper * cosine + lower * sine, lower * cosine - upper * sine], 1)
@@ -1003,11 +1005,7 @@
     down_up = adamw_turned(down_weight, down_first, down_second, owned_down, RATE_DOWN)
     query_right = ring_last(query_slots, n, query_far, (gateup_up, down_up))
     query_sum = ring_sum(query_slots[0], query_left, query_right).astype(LOW)
-    block_right = ring_last(mlp_slots, n, block_far, query_right)
     block_out = residual + ring_sum(mlp_slots[0], block_left, block_right)
-    own_query = dp_scatter(query_sum, sizes["dp"], ()).astype(F32)
-    query_up = adamw(query_weight, query_first, query_second, own_query, RATE_QUERY, DECAY)
-
     (back_q_t, back_kv_t), _ = after((grad_q_t, grad_kv_t), query_slots)
     grad_qkv_t = jnp.concatenate(
         [back_q_t, back_kv_t, jnp.zeros((attn_low.shape[1] - span, rows), LOW)], 0
@@ -1026,6 +1024,9 @@
     gain_cols = jnp.pad(gain_grads.T, ((0, 0), (0, 126)))
 
     slots = tail_pack(ids, owned_pack, gain_cols, piece, cols)
+    query_sum, _ = after(query_sum, slots[0])
+    own_query = dp_scatter(query_sum, sizes["dp"], ()).astype(F32)
+    query_up = adamw(query_weight, query_first, query_second, own_query, RATE_QUERY, DECAY)
     parts = [slots[0], ring_way(slots, n, -1), ring_way(slots, n, 1)]
     states = [output_weight, output_first, output_second, keyval_weight, keyval_first]
     states += [keyval_second, gains, gains_first, gains_second]

time: 614 us -> 618 us (level)
  waiting for transfers between devices: 188 us -> 197 us
    ppermute x14, waiting for transfers between devices: 19.9 us -> 27.1 us  [swap(): return lax.ppermute(x, 'dp', [(i, i ^ bit) for i in range(size)])]
  transfers between devices with their start and end apart: 48 -> 48, of which waited for: 26 -> 26; matrix products, arithmetic and copies ran while one was open for 15% -> 13% of each run, Pallas kernels for 36% -> 35%
where the time goes in v4:
time: 618 us; the launch traced here: 612 us
  Pallas kernels  244 us (39%)
  waiting for transfers between devices  197 us (32%)
  starting transfers between devices  69 us (11%)
  other arithmetic  38 us (6%)
  matrix products  30.5 us (5%)
  local copies, waits for them, and re-layouts  18.2 us (3%)
  between operations  14.9 us (2%)
    ppermute x30, waiting for transfers between devices, shift(): return lax.ppermute(x, 'tensor', [(i, (i + by) % n) for i in range(n)])  109 us
    pallas_call x3, Pallas kernels, feed(): pl.pallas_call(functools.partial(feed_kernel, pieces, count), in_specs=[v...  56 us
    ppermute x30, starting transfers between devices, shift(): return lax.ppermute(x, 'tensor', [(i, (i + by) % n) for i in range(n)])  54 us
    all_gather x1, waiting for transfers between devices, on_device(): attn_low = lax.all_gather(attn_in, 'dp', axis=0, tiled=True)  40.5 us
    pallas_call x1, Pallas kernels, attend_back(): pl.pallas_call(functools.partial(attend_back_kernel, slots, heads, len(we...  40.4 us
    pallas_call x7, Pallas kernels, weight_grad(): pl.pallas_call(functools.partial(weight_grad_kernel, count, add is not No...  33.7 us
    dot_general x4, matrix products, contract(): lax.dot_general(left, right, (((dim_left,), (dim_right,)), ((), ())), pre...  30.5 us
    pallas_call x2, Pallas kernels, feed_grad(): pl.pallas_call(functools.partial(feed_grad_kernel, halves, n), grid=(part...  29.5 us
  transfers between devices with their start and end apart: 48, of which 26 were waited for; matrix products, arithmetic and copies ran while one was open for 13% of the time, Pallas kernels for 35%

profile of v4, /device:TPU:0, one launch (start us, length us, event | category | flops | bytes accessed | tf_op | source)
XLA Modules:
  0.0 611.5 jit_solution(3463618812233075691)
XLA Ops:
  14.3 9.1 %collective-permute-done.refs_1_ = bf16[336,512]{1,0:T(8,128)(2,1)S(1)} collective-permute-done((bf16[336,512]{1,0:T(8,128)(2,1)}, bf16[336,512]{1,0:T(8,128)(2,1)S(1)}, u32[]{:S(2)}, u32[]{:S(2)}) %collective-permute-start) | collective-permute-done | bytes 344096 | tf_op jit(solution)/shard_map/ppermute | solution.py:49
  29.7 7.8 %collective-permute-done.1.refs_2_ = bf16[336,512]{1,0:T(8,128)(2,1)} collective-permute-done((bf16[336,512]{1,0:T(8,128)(2,1)S(1)}, bf16[336,512]{1,0:T(8,128)(2,1)}, u32[]{:S(2)}, u32[]{:S(2)}) %collective-permute-start.1) | collective-permute-done | bytes 344096 | tf_op jit(solution)/shard_map/ppermute | solution.py:49
  44.8 7.3 %collective-permute-done.3 = bf16[256,512]{1,0:T(8,128)(2,1)S(1)} collective-permute-done((bf16[256,512]{1,0:T(8,128)(2,1)S(1)}, bf16[256,512]{1,0:T(8,128)(2,1)S(1)}, u32[]{:S(2)}, u32[]{:S(2)}) %collective-permute-start.3) | collective-permute-done | bytes 262176 | tf_op jit(solution)/shard_map/ppermute | solution.py:49
  68.7 40.5 %all-gather.3.cloned.1.call-done.gain_ref.weight_ref = bf16[2048,2688]{1,0:T(8,128)(2,1)} async-done(((bf16[256,2688]{1,0:T(8,128)(2,1)}), bf16[2048,2688]{1,0:T(8,128)(2,1)}) %all-gather.3.cloned.1.call-update) | async-done | bytes 11010064 | tf_op jit(solution)/shard_map/all_gather | solution.py:874
  124.4 7.0 %project.1.q_ref = bf16[2048,256]{1,0:T(8,128)(2,1)} custom-call(bf16[256,2048]{1,0:T(8,128)(2,1)} %get-tuple-element.176.rows_ref, bf16[2048,2688]{1,0:T(8,128)(2,1)} %all-gather.3.cloned.1.call-done.gain_ref.weight_ref, f32[32,256]{1,0:T(8,128)} %get-tuple-element.111.cos_ref.refs_6_, f32[32,256]{1,0:T(8,128)} %get-tuple-element.112.sin_ref.refs_7_), custom_call_target="tpu_custom_call" | custom-call | flops 9200000000 | bytes 1000000 | tf_op jit(solution)/shard_map/project/pallas_call | solution.py:308
  136.3 22.0 %attend.1 = (bf16[2048,256]{1,0:T(8,128)(2,1)}, bf16[256,2048]{1,0:T(8,128)(2,1)}, f32[4,8,256]{2,1,0:T(8,128)}) custom-call(s32[25]{0:T(128)} %concatenate.35.meta_ref, s32[1,256]{1,0:T(1,128)} %bitcast.102, bf16[2048,256]{1,0:T(8,128)(2,1)} %project.1.q_ref, bf16[4,512,256]{2,1,0:T(8,128)(2,1)} %pad_maximum_fusion.3.kv_ref), custom_call_target="tpu_custom_call" | custom-call | flops 8589934592 | bytes 2097152 | tf_op jit(solution)/shard_map/attend/pallas_call | solution.py:368
  158.3 7.4 %collective-permute-done.13 = bf16[256,2048]{1,0:T(8,128)(2,1)S(1)} collective-permute-done((bf16[256,2048]{1,0:T(8,128)(2,1)S(1)}, bf16[256,2048]{1,0:T(8,128)(2,1)S(1)}, u32[]{:S(2)}, u32[]{:S(2)}) %collective-permute-start.13) | collective-permute-done | bytes 1048608 | tf_op jit(solution)/shard_map/ppermute | solution.py:116
  176.8 8.8 %mix.1 = (f32[256,2048]{1,0:T(8,128)}, bf16[256,2048]{1,0:T(8,128)(2,1)}, f32[256,1]{1,0:T(8,128)}) custom-call(s32[16]{0:T(128)} %concatenate.34.order_ref, bf16[256,2048]{1,0:T(8,128)(2,1)} %get-tuple-element.118.o_ref, bf16[256,2048]{1,0:T(8,128)(2,1)} %x_ref.3, f32[1,2048]{1,0:T(1,128)} %get-tuple-element.225.gain_ref, bf16[512,2048]{1,0:T(8,128)(2,1)} %copy-done.17, ...), custom_call_target="tpu_custom_call" | custom-call | flops 6899999744 | bytes 1000000 | tf_op jit(solution)/shard_map/mix/pallas_call | solution.py:518
  202.4 21.0 %all-gather.5.cloned.1.call-done.refs_2_.refs_4_ = bf16[3,2048,1408]{2,1,0:T(8,128)(2,1)} async-done(((bf16[3,256,1408]{2,1,0:T(8,128)(2,1)}), bf16[3,2048,1408]{2,1,0:T(8,128)(2,1)}) %all-gather.5.cloned.1.call-update) | async-done | bytes 17301520 | tf_op jit(solution)/shard_map/all_gather | solution.py:880
  223.5 14.7 %feed.3 = (bf16[3,256,1408]{2,1,0:T(8,128)(2,1)}, bf16[256,2048]{1,0:T(8,128)(2,1)}) custom-call(bf16[256,2048]{1,0:T(8,128)(2,1)} %get-tuple-element.134.x_ref.refs_0_, bf16[256,2048]{1,0:T(8,128)(2,1)} %refs_1_, bf16[3,2048,1408]{2,1,0:T(8,128)(2,1)} %all-gather.5.cloned.1.call-done.refs_2_.refs_4_), custom_call_target="tpu_custom_call" | custom-call | flops 1150000000 | bytes 1000000 | tf_op jit(solution)/shard_map/feed/pallas_call | solution.py:739
  245.6 26.3 %feed.4 = (bf16[3,512,1408]{2,1,0:T(8,128)(2,1)}, bf16[512,2048]{1,0:T(8,128)(2,1)}) custom-call(bf16[256,2048]{1,0:T(8,128)(2,1)} %copy-done.24, bf16[256,2048]{1,0:T(8,128)(2,1)} %copy-done.25, bf16[256,2048]{1,0:T(8,128)(2,1)} %collective-permute-done.6.x_ref.refs_2_, bf16[256,2048]{1,0:T(8,128)(2,1)} %copy-done.23, ...), custom_call_target="tpu_custom_call" | custom-call | flops 1150000000 | bytes 1000000 | tf_op jit(solution)/shard_map/feed/pallas_call | solution.py:739
  272.9 14.9 %feed.5 = (bf16[3,256,1408]{2,1,0:T(8,128)(2,1)}, bf16[256,2048]{1,0:T(8,128)(2,1)}) custom-call(bf16[256,2048]{1,0:T(8,128)(2,1)} %copy-done.21, bf16[256,2048]{1,0:T(8,128)(2,1)} %copy-done.19, bf16[3,2048,1408]{2,1,0:T(8,128)(2,1)} %all-gather.5.cloned.1.call-done.refs_2_.refs_4_), custom_call_target="tpu_custom_call" | custom-call | flops 1150000000 | bytes 1000000 | tf_op jit(solution)/shard_map/feed/pallas_call | solution.py:739
  294.2 18.3 %feed_grad.2.refs_7_ = bf16[3,2048,1408]{2,1,0:T(8,128)(2,1)} custom-call(bf16[3,256,1408]{2,1,0:T(8,128)(2,1)} %get-tuple-element.153.refs_0_, bf16[3,512,1408]{2,1,0:T(8,128)(2,1)} %get-tuple-element.154.refs_1_, bf16[3,256,1408]{2,1,0:T(8,128)(2,1)} %get-tuple-element.155.refs_2_, bf16[2048,256]{1,0:T(8,128)(2,1)} %turned.12.refs_3_, ...), custom_call_target="tpu_custom_call" | custom-call | flops 1150000000 | bytes 1000000 | tf_op jit(solution)/shard_map/feed_grad/pallas_call | solution.py:792
  321.0 11.2 %feed_grad.3 = bf16[3,2048,1408]{2,1,0:T(8,128)(2,1)} custom-call(bf16[3,256,1408]{2,1,0:T(8,128)(2,1)} %get-tuple-element.153.refs_0_, bf16[3,512,1408]{2,1,0:T(8,128)(2,1)} %get-tuple-element.154.refs_1_, bf16[3,256,1408]{2,1,0:T(8,128)(2,1)} %get-tuple-element.155.refs_2_, bf16[2048,256]{1,0:T(8,128)(2,1)} %turned.8.refs_3_, ...), custom_call_target="tpu_custom_call", output_to_operand_aliasing={{}: (7, {})} | custom-call | flops 1150000000 | bytes 1000000 | tf_op jit(solution)/shard_map/feed_grad/pallas_call | solution.py:792
  345.0 7.9 %fusion.3 = bf16[512,2048]{1,0:T(8,128)(2,1)S(1)} fusion(bf16[3,2048,1408]{2,1,0:T(8,128)(2,1)} %all-gather.5.cloned.1.call-done.refs_2_.refs_4_, bf16[3,512,1408]{2,1,0:T(8,128)(2,1)} %get-tuple-element.154.refs_1_), kind=kOutput, calls=%fused_computation.6 | convolution fusion | flops 2953838592 | bytes 9306112 | tf_op jit(solution)/shard_map/dot_general | solution.py:39
  353.0 7.0 %collective-permute-done.23 = bf16[256,2048]{1,0:T(8,128)(2,1)S(1)} collective-permute-done((bf16[256,2048]{1,0:T(8,128)(2,1)}, bf16[256,2048]{1,0:T(8,128)(2,1)S(1)}, u32[]{:S(2)}, u32[]{:S(2)}) %collective-permute-start.23) | collective-permute-done | bytes 1048608 | tf_op jit(solution)/shard_map/ppermute | solution.py:49
  369.4 40.4 %attend_back.1 = (bf16[2048,256]{1,0:T(8,128)(2,1)}, bf16[4,512,256]{2,1,0:T(8,128)(2,1)}) custom-call(s32[25]{0:T(128)} %concatenate.35.meta_ref, s32[1,256]{1,0:T(1,128)} %bitcast.103, bf16[2048,256]{1,0:T(8,128)(2,1)} %project.1.q_ref, bf16[4,512,256]{2,1,0:T(8,128)(2,1)} %pad_maximum_fusion.3.kv_ref, bf16[256,2048]{1,0:T(8,128)(2,1)} %fusion.27.back_ref.rows_ref, ...), custom_call_target="tpu_custom_call" | custom-call | flops 200000000753664 | bytes 1000000 | tf_op jit(solution)/shard_map/attend_back/pallas_call | solution.py:459
  419.3 27.2 %collective-permute-done.27 = bf16[512,256]{1,0:T(8,128)(2,1)S(1)} collective-permute-done((bf16[512,256]{1,0:T(8,128)(2,1)S(1)}, bf16[512,256]{1,0:T(8,128)(2,1)S(1)}, u32[]{:S(2)}, u32[]{:S(2)}) %collective-permute-start.27) | collective-permute-done | bytes 262176 | tf_op jit(solution)/shard_map/ppermute | solution.py:49
  451.3 7.7 %weight_grad.7.rest_0_ = bf16[2048,2560]{1,0:T(8,128)(2,1)} custom-call(s32[16]{0:T(128)} %iota.13.order_ref, bf16[256,2048]{1,0:T(8,128)(2,1)} %fusion.27.back_ref.rows_ref, bf16[2048,256]{1,0:T(8,128)(2,1)} %get-tuple-element.161.refs_4_.x_ref), custom_call_target="tpu_custom_call" | custom-call | flops 7850666496 | bytes 1000000 | tf_op jit(solution)/shard_map/weight_grad/pallas_call | solution.py:654
  472.7 8.7 %collective-permute-done.30.rest_0_ = bf16[1024,2048]{1,0:T(8,128)(2,1)} collective-permute-done((bf16[1024,2048]{1,0:T(8,128)(2,1)}, bf16[1024,2048]{1,0:T(8,128)(2,1)}, u32[]{:S(2)}, u32[]{:S(2)}) %collective-permute-start.30) | collective-permute-done | bytes 4194336 | tf_op jit(solution)/shard_map/ppermute | solution.py:116
  501.3 9.8 %multiply_reduce_fusion.1 = (f32[2048]{0:T(1024)S(1)}, f32[256]{0:T(256)S(1)}, f32[256,2048]{1,0:T(8,128)}) fusion(bf16[256,2048]{1,0:T(8,128)(2,1)S(1)} %copy-done.10, f32[256]{0:T(256)S(1)} %reduce.1, f32[2048]{0:T(1024)S(1)} %bitcast.98, bf16[2048,2688]{1,0:T(8,128)(2,1)} %all-gather.3.cloned.1.call-done.gain_ref.weight_ref, ...), kind=kOutput, calls=%fused_computation.16 | convolution fusion | flops 2826368768 | bytes 15490304 | tf_op jit(solution)/shard_map/dot_general | solution.py:39
  512.2 9.1 %adamw_turned.1 = (f32[1408,256]{1,0:T(8,128)}, f32[1408,256]{1,0:T(8,128)}, f32[1408,256]{1,0:T(8,128)}) custom-call(f32[1408,256]{1,0:T(8,128)} %weight.1, f32[1408,256]{1,0:T(8,128)} %first.1, f32[1408,256]{1,0:T(8,128)} %second.1, bf16[256,1408]{1,0:T(8,128)(2,1)} %slice_bitcast_fusion.10.grad), custom_call_target="tpu_custom_call" | custom-call | flops 4325376 | bytes 10092544 | tf_op jit(solution)/shard_map/adamw_turned/pallas_call | solution.py:820
  527.4 10.0 %collective-permute-done.32 = bf16[1024,512]{1,0:T(8,128)(2,1)} collective-permute-done((bf16[1024,512]{1,0:T(8,128)(2,1)}, bf16[1024,512]{1,0:T(8,128)(2,1)}, u32[]{:S(2)}, u32[]{:S(2)}) %collective-permute-start.32) | collective-permute-done | bytes 1048608 | tf_op jit(solution)/shard_map/ppermute | solution.py:49
  553.7 10.6 %collective-permute-done.33 = bf16[1024,512]{1,0:T(8,128)(2,1)} collective-permute-done((bf16[1024,512]{1,0:T(8,128)(2,1)}, bf16[1024,512]{1,0:T(8,128)(2,1)}, u32[]{:S(2)}, u32[]{:S(2)}) %collective-permute-start.33) | collective-permute-done | bytes 1048608 | tf_op jit(solution)/shard_map/ppermute | solution.py:49
  (275 shorter events, 241.8 us)
Async XLA Ops:
  7.2 102.1 %all-gather.3.cloned.1.call-start = ((), (), s32[]{:S(2)}) async-start(), calls=%async_computation.2 | async-start | bytes 12386304 | tf_op jit(solution)/shard_map/all_gather | solution.py:874
  40.7 182.7 %all-gather.5.cloned.1.call-start = ((), (), s32[]{:S(2)}) async-start(), calls=%async_computation.3 | async-start | bytes 19464192 | tf_op jit(solution)/shard_map/all_gather | solution.py:880
  60.3 404.9 %reduce-scatter.3.cloned.1.call-start = ((), (), s32[]{:S(2)}) async-start(), calls=%async_computation.4 | async-start | bytes 19464192 | tf_op jit(solution)/shard_map/reduce_scatter | solution.py:945
  63.4 56.0 %collective-permute-start.7 = (bf16[256,2048]{1,0:T(8,128)(2,1)S(1)}, bf16[256,2048]{1,0:T(8,128)(2,1)S(1)}, u32[]{:S(2)}, u32[]{:S(2)}) collective-permute-start(bf16[256,2048]{1,0:T(8,128)(2,1)S(1)} %copy-done.7), channel_id=1, source_target_pairs={{0,3},{1,0},{2,1},{3,2},{4,7},{5,4},{6,5},{7,6},{8,11},{9,8},{10,9... | collective-permute-start | bytes 3145736 | tf_op jit(solution)/shard_map/ppermute | solution.py:49
  63.6 55.8 %collective-permute-start.6 = (bf16[256,2048]{1,0:T(8,128)(2,1)S(1)}, bf16[256,2048]{1,0:T(8,128)(2,1)}, u32[]{:S(2)}, u32[]{:S(2)}) collective-permute-start(bf16[256,2048]{1,0:T(8,128)(2,1)S(1)} %copy-done.7), channel_id=1, source_target_pairs={{0,1},{1,2},{2,3},{3,0},{4,5},{5,6},{6,7},{7,4},{8,9},{9,10},{10,1... | collective-permute-start | bytes 3145736 | tf_op jit(solution)/shard_map/ppermute | solution.py:49
  65.7 49.1 %collective-permute-start.12 = (bf16[128,2048]{1,0:T(8,128)(2,1)S(1)}, bf16[128,2048]{1,0:T(8,128)(2,1)}, u32[]{:S(2)}, u32[]{:S(2)}) collective-permute-start(bf16[128,2048]{1,0:T(8,128)(2,1)S(1)} %get-tuple-element.220), channel_id=1, source_target_pairs={{0,16},{4,20},{8,24},{12,28},{16,0},{20,4},{24,8},{28,12},{1,17},{... | collective-permute-start | bytes 1572872 | tf_op jit(solution)/shard_map/ppermute | solution.py:116
  67.3 48.6 %collective-permute-start.11 = (bf16[128,2048]{1,0:T(8,128)(2,1)S(1)}, bf16[128,2048]{1,0:T(8,128)(2,1)}, u32[]{:S(2)}, u32[]{:S(2)}) collective-permute-start(bf16[128,2048]{1,0:T(8,128)(2,1)S(1)} %get-tuple-element.221), channel_id=1, source_target_pairs={{0,8},{4,12},{8,0},{12,4},{16,24},{20,28},{24,16},{28,20},{1,9},{5... | collective-permute-start | bytes 1572872 | tf_op jit(solution)/shard_map/ppermute | solution.py:116
  119.4 46.3 %collective-permute-start.13 = (bf16[256,2048]{1,0:T(8,128)(2,1)S(1)}, bf16[256,2048]{1,0:T(8,128)(2,1)S(1)}, u32[]{:S(2)}, u32[]{:S(2)}) collective-permute-start(bf16[256,2048]{1,0:T(8,128)(2,1)S(1)} %pad_maximum_fusion.4), channel_id=1, source_target_pairs={{0,16},{4,20},{8,24},{12,28},{16,0},{20,4},{24,8},{28,12},{1,17},{... | collective-permute-start | bytes 3145736 | tf_op jit(solution)/shard_map/ppermute | solution.py:116
  120.0 46.9 %collective-permute-start.14 = (bf16[256,2048]{1,0:T(8,128)(2,1)S(1)}, bf16[256,2048]{1,0:T(8,128)(2,1)S(1)}, u32[]{:S(2)}, u32[]{:S(2)}) collective-permute-start(bf16[256,2048]{1,0:T(8,128)(2,1)S(1)} %pad_maximum_fusion.5), channel_id=1, source_target_pairs={{0,8},{4,12},{8,0},{12,4},{16,24},{20,28},{24,16},{28,20},{1,9},{5... | collective-permute-start | bytes 3145736 | tf_op jit(solution)/shard_map/ppermute | solution.py:116
  136.1 32.3 %collective-permute-start.15 = (bf16[256,2048]{1,0:T(8,128)(2,1)}, bf16[256,2048]{1,0:T(8,128)(2,1)S(1)}, u32[]{:S(2)}, u32[]{:S(2)}) collective-permute-start(bf16[256,2048]{1,0:T(8,128)(2,1)} %collective-permute-done.6.x_ref.refs_2_), channel_id=1, source_target_pairs={{0,1},{1,2},{2,3},{3,0},{4,5},{5,6},{6,7},{7,4},{8,9},{9,10},{10,1... | collective-permute-start | bytes 3145736 | tf_op jit(solution)/shard_map/ppermute | solution.py:49
  185.6 52.6 %collective-permute-start.18 = (bf16[256,2048]{1,0:T(8,128)(2,1)}, bf16[256,2048]{1,0:T(8,128)(2,1)S(1)}, u32[]{:S(2)}, u32[]{:S(2)}) collective-permute-start(bf16[256,2048]{1,0:T(8,128)(2,1)} %get-tuple-element.134.x_ref.refs_0_), channel_id=1, source_target_pairs={{0,1},{1,2},{2,3},{3,0},{4,5},{5,6},{6,7},{7,4},{8,9},{9,10},{10,1... | collective-permute-start | bytes 3145736 | tf_op jit(solution)/shard_map/ppermute | solution.py:49
  185.7 54.5 %collective-permute-start.19 = (bf16[256,2048]{1,0:T(8,128)(2,1)}, bf16[256,2048]{1,0:T(8,128)(2,1)S(1)}, u32[]{:S(2)}, u32[]{:S(2)}) collective-permute-start(bf16[256,2048]{1,0:T(8,128)(2,1)} %get-tuple-element.134.x_ref.refs_0_), channel_id=1, source_target_pairs={{0,3},{1,0},{2,1},{3,2},{4,7},{5,4},{6,5},{7,6},{8,11},{9,8},{10,9... | collective-permute-start | bytes 3145736 | tf_op jit(solution)/shard_map/ppermute | solution.py:49
  238.2 33.7 %collective-permute-start.21 = (bf16[256,2048]{1,0:T(8,128)(2,1)S(1)}, bf16[256,2048]{1,0:T(8,128)(2,1)S(1)}, u32[]{:S(2)}, u32[]{:S(2)}) collective-permute-start(bf16[256,2048]{1,0:T(8,128)(2,1)S(1)} %collective-permute-done.18.x_ref.refs_0_), channel_id=1, source_target_pairs={{0,1},{1,2},{2,3},{3,0},{4,5},{5,6},{6,7},{7,4},{8,9},{9,10},{10,1... | collective-permute-start | bytes 3145736 | tf_op jit(solution)/shard_map/ppermute | solution.py:49
  291.5 61.5 %collective-permute-start.20 = (bf16[256,2048]{1,0:T(8,128)(2,1)}, bf16[256,2048]{1,0:T(8,128)(2,1)S(1)}, u32[]{:S(2)}, u32[]{:S(2)}) collective-permute-start(bf16[256,2048]{1,0:T(8,128)(2,1)} %slice.103), channel_id=1, source_target_pairs={{0,1},{1,2},{2,3},{3,0},{4,5},{5,6},{6,7},{7,4},{8,9},{9,10},{10,1... | collective-permute-start | bytes 3145736 | tf_op jit(solution)/shard_map/ppermute | solution.py:49
  316.7 43.3 %collective-permute-start.23 = (bf16[256,2048]{1,0:T(8,128)(2,1)}, bf16[256,2048]{1,0:T(8,128)(2,1)S(1)}, u32[]{:S(2)}, u32[]{:S(2)}) collective-permute-start(bf16[256,2048]{1,0:T(8,128)(2,1)} %add_convert_fusion.3), channel_id=1, source_target_pairs={{0,3},{1,0},{2,1},{3,2},{4,7},{5,4},{6,5},{7,6},{8,11},{9,8},{10,9... | collective-permute-start | bytes 3145736 | tf_op jit(solution)/shard_map/ppermute | solution.py:49
  332.2 234.4 %reduce-scatter.5.cloned.1.call-start = ((), (), s32[]{:S(2)}) async-start(), calls=%async_computation.5 | async-start | bytes 11796480 | tf_op jit(solution)/shard_map/reduce_scatter | solution.py:991
  365.2 44.6 %collective-permute-start.24 = (bf16[256,2048]{1,0:T(8,128)(2,1)}, bf16[256,2048]{1,0:T(8,128)(2,1)}, u32[]{:S(2)}, u32[]{:S(2)}) collective-permute-start(bf16[256,2048]{1,0:T(8,128)(2,1)} %slice.109), channel_id=1, source_target_pairs={{0,1},{1,2},{2,3},{3,0},{4,5},{5,6},{6,7},{7,4},{8,9},{9,10},{10,1... | collective-permute-start | bytes 3145736 | tf_op jit(solution)/shard_map/ppermute | solution.py:49
  365.8 48.0 %collective-permute-start.25 = (bf16[256,2048]{1,0:T(8,128)(2,1)}, bf16[256,2048]{1,0:T(8,128)(2,1)}, u32[]{:S(2)}, u32[]{:S(2)}) collective-permute-start(bf16[256,2048]{1,0:T(8,128)(2,1)} %fusion.7), channel_id=1, source_target_pairs={{0,3},{1,0},{2,1},{3,2},{4,7},{5,4},{6,5},{7,6},{8,11},{9,8},{10,9... | collective-permute-start | bytes 3145736 | tf_op jit(solution)/shard_map/ppermute | solution.py:49
  415.4 31.1 %collective-permute-start.26 = (bf16[256,2048]{1,0:T(8,128)(2,1)S(1)}, bf16[256,2048]{1,0:T(8,128)(2,1)}, u32[]{:S(2)}, u32[]{:S(2)}) collective-permute-start(bf16[256,2048]{1,0:T(8,128)(2,1)S(1)} %add_convert_fusion.2), channel_id=1, source_target_pairs={{0,3},{1,0},{2,1},{3,2},{4,7},{5,4},{6,5},{7,6},{8,11},{9,8},{10,9... | collective-permute-start | bytes 3145736 | tf_op jit(solution)/shard_map/ppermute | solution.py:49
  417.2 29.2 %collective-permute-start.27 = (bf16[512,256]{1,0:T(8,128)(2,1)S(1)}, bf16[512,256]{1,0:T(8,128)(2,1)S(1)}, u32[]{:S(2)}, u32[]{:S(2)}) collective-permute-start(bf16[512,256]{1,0:T(8,128)(2,1)S(1)} %get-tuple-element.218), channel_id=1, source_target_pairs={{0,3},{1,0},{2,1},{3,2},{4,7},{5,4},{6,5},{7,6},{8,11},{9,8},{10,9... | collective-permute-start | bytes 786440 | tf_op jit(solution)/shard_map/ppermute | solution.py:49
  418.7 40.3 %collective-permute-start.29 = (bf16[512,256]{1,0:T(8,128)(2,1)S(1)}, bf16[512,256]{1,0:T(8,128)(2,1)S(1)}, u32[]{:S(2)}, u32[]{:S(2)}) collective-permute-start(bf16[512,256]{1,0:T(8,128)(2,1)S(1)} %get-tuple-element.219), channel_id=1, source_target_pairs={{0,1},{1,2},{2,3},{3,0},{4,5},{5,6},{6,7},{7,4},{8,9},{9,10},{10,1... | collective-permute-start | bytes 786440 | tf_op jit(solution)/shard_map/ppermute | solution.py:49
  489.4 64.3 %collective-permute-start.31 = (bf16[1024,512]{1,0:T(8,128)(2,1)}, bf16[1024,512]{1,0:T(8,128)(2,1)}, u32[]{:S(2)}, u32[]{:S(2)}) collective-permute-start(bf16[1024,512]{1,0:T(8,128)(2,1)} %weight_grad.11), channel_id=1, source_target_pairs={{0,1},{1,2},{2,3},{3,0},{4,5},{5,6},{6,7},{7,4},{8,9},{9,10},{10,1... | collective-permute-start | bytes 3145736 | tf_op jit(solution)/shard_map/ppermute | solution.py:49
  489.4 47.9 %collective-permute-start.32 = (bf16[1024,512]{1,0:T(8,128)(2,1)}, bf16[1024,512]{1,0:T(8,128)(2,1)}, u32[]{:S(2)}, u32[]{:S(2)}) collective-permute-start(bf16[1024,512]{1,0:T(8,128)(2,1)} %weight_grad.10), channel_id=1, source_target_pairs={{0,3},{1,0},{2,1},{3,2},{4,7},{5,4},{6,5},{7,6},{8,11},{9,8},{10,9... | collective-permute-start | bytes 3145736 | tf_op jit(solution)/shard_map/ppermute | solution.py:49
  511.2 30.6 %collective-permute-start.34 = (f32[2,2048]{1,0:T(2,128)S(1)}, f32[2,2048]{1,0:T(2,128)S(1)}, u32[]{:S(2)}, u32[]{:S(2)}) collective-permute-start(f32[2,2048]{1,0:T(2,128)S(1)} %pad_maximum_fusion.9), channel_id=1, source_target_pairs={{0,4},{4,0},{8,12},{12,8},{16,20},{20,16},{24,28},{28,24},{1,5},{5... | collective-permute-start | bytes 49160 | tf_op jit(solution)/shard_map/ppermute | solution.py:116
  (72 other events, 755.8 us)
Sparse Core Ops, SparseCore 0:
  40.8 68.4 all-gather.2
  111.8 111.6 all-gather.4
  332.3 115.8 reduce-scatter.2
  465.4 83.8 reduce-scatter.4

commit v5 on v4

--- a/solution.py
+++ b/solution.py
@@ -966,9 +966,8 @@
     block_right = ring_last(mlp_slots, n, block_far, grad_kv)
     kv_far = ring_most(kv_parts, n)
     own_kv = ring_sum(kv_parts[0], ring_last(kv_parts, n, kv_far, block_right), kv_left)
-    query_rows, _ = after(first_normalized, kv_far)
     partner = weight_grad(
-        query_rows, grad_q_t, n * cols, cols, n, lambda i: i, lambda i: i, places[1]
+        first_normalized, grad_q_t, n * cols, cols, n, lambda i: i, lambda i: i, places[1]
     )
     partner = swap(partner, sizes["dp"], 1)
     out_rows, _ = after(back, grad_q_t)
@@ -977,6 +976,7 @@
         out_rows, mixed_t, span, 2 * KVD, heads_cols, lambda i: i, lambda i: i
     )
 
+    own_kv, _ = after(own_kv, partner)
     grad_k = own_kv[:KVD].reshape(KVH, 2, HD // 2, rows)
     upper, lower = grad_k[:, 0], grad_k[:, 1]
     grad_k = jnp.stack([upper * cosine + lower * sine, lower * cosine - upper * sine], 1)

time: 618 us -> 607 us (0.982)
  waiting for transfers between devices: 197 us -> 190 us
    ppermute x14, waiting for transfers between devices: 27.1 us -> 20.6 us  [swap(): return lax.ppermute(x, 'dp', [(i, i ^ bit) for i in range(size)])]
  transfers between devices with their start and end apart: 48 -> 48, of which waited for: 26 -> 26; matrix products, arithmetic and copies ran while one was open for 13% -> 14% of each run, Pallas kernels for 35% -> 36%
where the time goes in v5:
time: 607 us; the launch traced here: 601 us
  Pallas kernels  244 us (40%)
  waiting for transfers between devices  190 us (31%)
  starting transfers between devices  65.3 us (11%)
  other arithmetic  38 us (6%)
  matrix products  30.2 us (5%)
  local copies, waits for them, and re-layouts  18.4 us (3%)
  between operations  14.9 us (2%)
    ppermute x30, waiting for transfers between devices, shift(): return lax.ppermute(x, 'tensor', [(i, (i + by) % n) for i in range(n)])  108 us
    pallas_call x3, Pallas kernels, feed(): pl.pallas_call(functools.partial(feed_kernel, pieces, count), in_specs=[v...  56 us
    ppermute x30, starting transfers between devices, shift(): return lax.ppermute(x, 'tensor', [(i, (i + by) % n) for i in range(n)])  53.6 us
    all_gather x1, waiting for transfers between devices, on_device(): attn_low = lax.all_gather(attn_in, 'dp', axis=0, tiled=True)  40.5 us
    pallas_call x1, Pallas kernels, attend_back(): pl.pallas_call(functools.partial(attend_back_kernel, slots, heads, len(we...  40.2 us
    pallas_call x7, Pallas kernels, weight_grad(): pl.pallas_call(functools.partial(weight_grad_kernel, count, add is not No...  34.1 us
    dot_general x4, matrix products, contract(): lax.dot_general(left, right, (((dim_left,), (dim_right,)), ((), ())), pre...  30.2 us
    pallas_call x2, Pallas kernels, feed_grad(): pl.pallas_call(functools.partial(feed_grad_kernel, halves, n), grid=(part...  29.5 us
  transfers between devices with their start and end apart: 48, of which 26 were waited for; matrix products, arithmetic and copies ran while one was open for 14% of the time, Pallas kernels for 36%

profile of v5, /device:TPU:0, one launch (start us, length us, event | category | flops | bytes accessed | tf_op | source)
XLA Modules:
  0.0 601.1 jit_solution(6894562470138044490)
XLA Ops:
  14.3 9.1 %collective-permute-done.refs_1_ = bf16[336,512]{1,0:T(8,128)(2,1)S(1)} collective-permute-done((bf16[336,512]{1,0:T(8,128)(2,1)}, bf16[336,512]{1,0:T(8,128)(2,1)S(1)}, u32[]{:S(2)}, u32[]{:S(2)}) %collective-permute-start) | collective-permute-done | bytes 344096 | tf_op jit(solution)/shard_map/ppermute | solution.py:49
  29.7 7.8 %collective-permute-done.1.refs_2_ = bf16[336,512]{1,0:T(8,128)(2,1)} collective-permute-done((bf16[336,512]{1,0:T(8,128)(2,1)S(1)}, bf16[336,512]{1,0:T(8,128)(2,1)}, u32[]{:S(2)}, u32[]{:S(2)}) %collective-permute-start.1) | collective-permute-done | bytes 344096 | tf_op jit(solution)/shard_map/ppermute | solution.py:49
  44.8 7.3 %collective-permute-done.3 = bf16[256,512]{1,0:T(8,128)(2,1)S(1)} collective-permute-done((bf16[256,512]{1,0:T(8,128)(2,1)S(1)}, bf16[256,512]{1,0:T(8,128)(2,1)S(1)}, u32[]{:S(2)}, u32[]{:S(2)}) %collective-permute-start.3) | collective-permute-done | bytes 262176 | tf_op jit(solution)/shard_map/ppermute | solution.py:49
  68.7 40.5 %all-gather.3.cloned.1.call-done.gain_ref.weight_ref = bf16[2048,2688]{1,0:T(8,128)(2,1)} async-done(((bf16[256,2688]{1,0:T(8,128)(2,1)}), bf16[2048,2688]{1,0:T(8,128)(2,1)}) %all-gather.3.cloned.1.call-update) | async-done | bytes 11010064 | tf_op jit(solution)/shard_map/all_gather | solution.py:874
  124.4 7.0 %project.1.q_ref = bf16[2048,256]{1,0:T(8,128)(2,1)} custom-call(bf16[256,2048]{1,0:T(8,128)(2,1)} %get-tuple-element.176.rows_ref, bf16[2048,2688]{1,0:T(8,128)(2,1)} %all-gather.3.cloned.1.call-done.gain_ref.weight_ref, f32[32,256]{1,0:T(8,128)} %get-tuple-element.111.cos_ref.refs_6_, f32[32,256]{1,0:T(8,128)} %get-tuple-element.112.sin_ref.refs_7_), custom_call_target="tpu_custom_call" | custom-call | flops 9200000000 | bytes 1000000 | tf_op jit(solution)/shard_map/project/pallas_call | solution.py:308
  136.3 22.0 %attend.1 = (bf16[2048,256]{1,0:T(8,128)(2,1)}, bf16[256,2048]{1,0:T(8,128)(2,1)}, f32[4,8,256]{2,1,0:T(8,128)}) custom-call(s32[25]{0:T(128)} %concatenate.35.meta_ref, s32[1,256]{1,0:T(1,128)} %bitcast.102, bf16[2048,256]{1,0:T(8,128)(2,1)} %project.1.q_ref, bf16[4,512,256]{2,1,0:T(8,128)(2,1)} %pad_maximum_fusion.3.kv_ref), custom_call_target="tpu_custom_call" | custom-call | flops 8589934592 | bytes 2097152 | tf_op jit(solution)/shard_map/attend/pallas_call | solution.py:368
  158.3 7.4 %collective-permute-done.13 = bf16[256,2048]{1,0:T(8,128)(2,1)S(1)} collective-permute-done((bf16[256,2048]{1,0:T(8,128)(2,1)S(1)}, bf16[256,2048]{1,0:T(8,128)(2,1)S(1)}, u32[]{:S(2)}, u32[]{:S(2)}) %collective-permute-start.13) | collective-permute-done | bytes 1048608 | tf_op jit(solution)/shard_map/ppermute | solution.py:116
  176.8 8.8 %mix.1 = (f32[256,2048]{1,0:T(8,128)}, bf16[256,2048]{1,0:T(8,128)(2,1)}, f32[256,1]{1,0:T(8,128)}) custom-call(s32[16]{0:T(128)} %concatenate.34.order_ref, bf16[256,2048]{1,0:T(8,128)(2,1)} %get-tuple-element.118.o_ref, bf16[256,2048]{1,0:T(8,128)(2,1)} %x_ref.3, f32[1,2048]{1,0:T(1,128)} %get-tuple-element.225.gain_ref, bf16[512,2048]{1,0:T(8,128)(2,1)} %copy-done.17, ...), custom_call_target="tpu_custom_call" | custom-call | flops 6899999744 | bytes 1000000 | tf_op jit(solution)/shard_map/mix/pallas_call | solution.py:518
  202.3 21.1 %all-gather.5.cloned.1.call-done.refs_2_.refs_4_ = bf16[3,2048,1408]{2,1,0:T(8,128)(2,1)} async-done(((bf16[3,256,1408]{2,1,0:T(8,128)(2,1)}), bf16[3,2048,1408]{2,1,0:T(8,128)(2,1)}) %all-gather.5.cloned.1.call-update) | async-done | bytes 17301520 | tf_op jit(solution)/shard_map/all_gather | solution.py:880
  223.5 14.7 %feed.3 = (bf16[3,256,1408]{2,1,0:T(8,128)(2,1)}, bf16[256,2048]{1,0:T(8,128)(2,1)}) custom-call(bf16[256,2048]{1,0:T(8,128)(2,1)} %get-tuple-element.134.x_ref.refs_0_, bf16[256,2048]{1,0:T(8,128)(2,1)} %refs_1_, bf16[3,2048,1408]{2,1,0:T(8,128)(2,1)} %all-gather.5.cloned.1.call-done.refs_2_.refs_4_), custom_call_target="tpu_custom_call" | custom-call | flops 1150000000 | bytes 1000000 | tf_op jit(solution)/shard_map/feed/pallas_call | solution.py:739
  245.6 26.3 %feed.4 = (bf16[3,512,1408]{2,1,0:T(8,128)(2,1)}, bf16[512,2048]{1,0:T(8,128)(2,1)}) custom-call(bf16[256,2048]{1,0:T(8,128)(2,1)} %copy-done.24, bf16[256,2048]{1,0:T(8,128)(2,1)} %copy-done.25, bf16[256,2048]{1,0:T(8,128)(2,1)} %collective-permute-done.6.x_ref.refs_2_, bf16[256,2048]{1,0:T(8,128)(2,1)} %copy-done.23, ...), custom_call_target="tpu_custom_call" | custom-call | flops 1150000000 | bytes 1000000 | tf_op jit(solution)/shard_map/feed/pallas_call | solution.py:739
  273.0 14.9 %feed.5 = (bf16[3,256,1408]{2,1,0:T(8,128)(2,1)}, bf16[256,2048]{1,0:T(8,128)(2,1)}) custom-call(bf16[256,2048]{1,0:T(8,128)(2,1)} %copy-done.21, bf16[256,2048]{1,0:T(8,128)(2,1)} %copy-done.20, bf16[3,2048,1408]{2,1,0:T(8,128)(2,1)} %all-gather.5.cloned.1.call-done.refs_2_.refs_4_), custom_call_target="tpu_custom_call" | custom-call | flops 1150000000 | bytes 1000000 | tf_op jit(solution)/shard_map/feed/pallas_call | solution.py:739
  294.8 18.3 %feed_grad.2.refs_7_ = bf16[3,2048,1408]{2,1,0:T(8,128)(2,1)} custom-call(bf16[3,256,1408]{2,1,0:T(8,128)(2,1)} %get-tuple-element.153.refs_0_, bf16[3,512,1408]{2,1,0:T(8,128)(2,1)} %get-tuple-element.154.refs_1_, bf16[3,256,1408]{2,1,0:T(8,128)(2,1)} %get-tuple-element.155.refs_2_, bf16[2048,256]{1,0:T(8,128)(2,1)} %turned.12.refs_3_, ...), custom_call_target="tpu_custom_call" | custom-call | flops 1150000000 | bytes 1000000 | tf_op jit(solution)/shard_map/feed_grad/pallas_call | solution.py:792
  321.0 11.2 %feed_grad.3 = bf16[3,2048,1408]{2,1,0:T(8,128)(2,1)} custom-call(bf16[3,256,1408]{2,1,0:T(8,128)(2,1)} %get-tuple-element.153.refs_0_, bf16[3,512,1408]{2,1,0:T(8,128)(2,1)} %get-tuple-element.154.refs_1_, bf16[3,256,1408]{2,1,0:T(8,128)(2,1)} %get-tuple-element.155.refs_2_, bf16[2048,256]{1,0:T(8,128)(2,1)} %turned.8.refs_3_, ...), custom_call_target="tpu_custom_call", output_to_operand_aliasing={{}: (7, {})} | custom-call | flops 1150000000 | bytes 1000000 | tf_op jit(solution)/shard_map/feed_grad/pallas_call | solution.py:792
  338.1 7.0 %fusion.7 = bf16[256,2048]{1,0:T(8,128)(2,1)} fusion(bf16[3,2048,1408]{2,1,0:T(8,128)(2,1)} %all-gather.5.cloned.1.call-done.refs_2_.refs_4_, bf16[3,256,1408]{2,1,0:T(8,128)(2,1)} %get-tuple-element.155.refs_2_), kind=kOutput, calls=%fused_computation.11 | convolution fusion | flops 1476919296 | bytes 7536640 | tf_op jit(solution)/shard_map/dot_general | solution.py:39
  345.1 7.9 %fusion.3 = bf16[512,2048]{1,0:T(8,128)(2,1)S(1)} fusion(bf16[3,2048,1408]{2,1,0:T(8,128)(2,1)} %all-gather.5.cloned.1.call-done.refs_2_.refs_4_, bf16[3,512,1408]{2,1,0:T(8,128)(2,1)} %get-tuple-element.154.refs_1_), kind=kOutput, calls=%fused_computation.6 | convolution fusion | flops 2953838592 | bytes 9306112 | tf_op jit(solution)/shard_map/dot_general | solution.py:39
  353.0 7.0 %collective-permute-done.23 = bf16[256,2048]{1,0:T(8,128)(2,1)S(1)} collective-permute-done((bf16[256,2048]{1,0:T(8,128)(2,1)}, bf16[256,2048]{1,0:T(8,128)(2,1)S(1)}, u32[]{:S(2)}, u32[]{:S(2)}) %collective-permute-start.23) | collective-permute-done | bytes 1048608 | tf_op jit(solution)/shard_map/ppermute | solution.py:49
  369.5 40.2 %attend_back.1 = (bf16[2048,256]{1,0:T(8,128)(2,1)}, bf16[4,512,256]{2,1,0:T(8,128)(2,1)}) custom-call(s32[25]{0:T(128)} %concatenate.35.meta_ref, s32[1,256]{1,0:T(1,128)} %bitcast.103, bf16[2048,256]{1,0:T(8,128)(2,1)} %project.1.q_ref, bf16[4,512,256]{2,1,0:T(8,128)(2,1)} %pad_maximum_fusion.3.kv_ref, bf16[256,2048]{1,0:T(8,128)(2,1)} %fusion.27.back_ref.rows_ref, ...), custom_call_target="tpu_custom_call" | custom-call | flops 200000000753664 | bytes 1000000 | tf_op jit(solution)/shard_map/attend_back/pallas_call | solution.py:459
  425.7 27.3 %collective-permute-done.27 = bf16[512,256]{1,0:T(8,128)(2,1)S(1)} collective-permute-done((bf16[512,256]{1,0:T(8,128)(2,1)S(1)}, bf16[512,256]{1,0:T(8,128)(2,1)S(1)}, u32[]{:S(2)}, u32[]{:S(2)}) %collective-permute-start.27) | collective-permute-done | bytes 262176 | tf_op jit(solution)/shard_map/ppermute | solution.py:49
  457.6 7.7 %weight_grad.8.rest_0_ = bf16[2048,2560]{1,0:T(8,128)(2,1)} custom-call(s32[16]{0:T(128)} %iota.13.order_ref, bf16[256,2048]{1,0:T(8,128)(2,1)} %fusion.27.back_ref.rows_ref, bf16[2048,256]{1,0:T(8,128)(2,1)} %get-tuple-element.161.refs_4_.x_ref), custom_call_target="tpu_custom_call" | custom-call | flops 7850666496 | bytes 1000000 | tf_op jit(solution)/shard_map/weight_grad/pallas_call | solution.py:654
  492.6 9.6 %multiply_reduce_fusion.1 = (f32[2048]{0:T(1024)S(1)}, f32[256]{0:T(256)S(1)}, f32[256,2048]{1,0:T(8,128)}) fusion(bf16[256,2048]{1,0:T(8,128)(2,1)S(1)} %copy-done.10, f32[256]{0:T(256)S(1)} %reduce.1, f32[2048]{0:T(1024)S(1)} %bitcast.98, bf16[2048,2688]{1,0:T(8,128)(2,1)} %all-gather.3.cloned.1.call-done.gain_ref.weight_ref, ...), kind=kOutput, calls=%fused_computation.16 | convolution fusion | flops 2826368768 | bytes 15490304 | tf_op jit(solution)/shard_map/dot_general | solution.py:39
  503.2 9.4 %adamw_turned.1 = (f32[1408,256]{1,0:T(8,128)}, f32[1408,256]{1,0:T(8,128)}, f32[1408,256]{1,0:T(8,128)}) custom-call(f32[1408,256]{1,0:T(8,128)} %weight.1, f32[1408,256]{1,0:T(8,128)} %first.1, f32[1408,256]{1,0:T(8,128)} %second.1, bf16[256,1408]{1,0:T(8,128)(2,1)} %slice_bitcast_fusion.10.grad), custom_call_target="tpu_custom_call" | custom-call | flops 4325376 | bytes 10092544 | tf_op jit(solution)/shard_map/adamw_turned/pallas_call | solution.py:820
  518.6 9.7 %collective-permute-done.32 = bf16[1024,512]{1,0:T(8,128)(2,1)} collective-permute-done((bf16[1024,512]{1,0:T(8,128)(2,1)}, bf16[1024,512]{1,0:T(8,128)(2,1)}, u32[]{:S(2)}, u32[]{:S(2)}) %collective-permute-start.32) | collective-permute-done | bytes 1048608 | tf_op jit(solution)/shard_map/ppermute | solution.py:49
  544.7 10.8 %collective-permute-done.33 = bf16[1024,512]{1,0:T(8,128)(2,1)} collective-permute-done((bf16[1024,512]{1,0:T(8,128)(2,1)}, bf16[1024,512]{1,0:T(8,128)(2,1)}, u32[]{:S(2)}, u32[]{:S(2)}) %collective-permute-start.33) | collective-permute-done | bytes 1048608 | tf_op jit(solution)/shard_map/ppermute | solution.py:49
  (275 shorter events, 233.0 us)
Async XLA Ops:
  7.2 102.1 %all-gather.3.cloned.1.call-start = ((), (), s32[]{:S(2)}) async-start(), calls=%async_computation.2 | async-start | bytes 12386304 | tf_op jit(solution)/shard_map/all_gather | solution.py:874
  40.7 182.7 %all-gather.5.cloned.1.call-start = ((), (), s32[]{:S(2)}) async-start(), calls=%async_computation.3 | async-start | bytes 19464192 | tf_op jit(solution)/shard_map/all_gather | solution.py:880
  60.3 411.2 %reduce-scatter.3.cloned.1.call-start = ((), (), s32[]{:S(2)}) async-start(), calls=%async_computation.4 | async-start | bytes 19464192 | tf_op jit(solution)/shard_map/reduce_scatter | solution.py:945
  63.4 56.0 %collective-permute-start.7 = (bf16[256,2048]{1,0:T(8,128)(2,1)S(1)}, bf16[256,2048]{1,0:T(8,128)(2,1)S(1)}, u32[]{:S(2)}, u32[]{:S(2)}) collective-permute-start(bf16[256,2048]{1,0:T(8,128)(2,1)S(1)} %copy-done.7), channel_id=1, source_target_pairs={{0,3},{1,0},{2,1},{3,2},{4,7},{5,4},{6,5},{7,6},{8,11},{9,8},{10,9... | collective-permute-start | bytes 3145736 | tf_op jit(solution)/shard_map/ppermute | solution.py:49
  63.6 55.8 %collective-permute-start.6 = (bf16[256,2048]{1,0:T(8,128)(2,1)S(1)}, bf16[256,2048]{1,0:T(8,128)(2,1)}, u32[]{:S(2)}, u32[]{:S(2)}) collective-permute-start(bf16[256,2048]{1,0:T(8,128)(2,1)S(1)} %copy-done.7), channel_id=1, source_target_pairs={{0,1},{1,2},{2,3},{3,0},{4,5},{5,6},{6,7},{7,4},{8,9},{9,10},{10,1... | collective-permute-start | bytes 3145736 | tf_op jit(solution)/shard_map/ppermute | solution.py:49
  65.7 49.1 %collective-permute-start.12 = (bf16[128,2048]{1,0:T(8,128)(2,1)S(1)}, bf16[128,2048]{1,0:T(8,128)(2,1)}, u32[]{:S(2)}, u32[]{:S(2)}) collective-permute-start(bf16[128,2048]{1,0:T(8,128)(2,1)S(1)} %get-tuple-element.220), channel_id=1, source_target_pairs={{0,16},{4,20},{8,24},{12,28},{16,0},{20,4},{24,8},{28,12},{1,17},{... | collective-permute-start | bytes 1572872 | tf_op jit(solution)/shard_map/ppermute | solution.py:116
  67.2 48.6 %collective-permute-start.11 = (bf16[128,2048]{1,0:T(8,128)(2,1)S(1)}, bf16[128,2048]{1,0:T(8,128)(2,1)}, u32[]{:S(2)}, u32[]{:S(2)}) collective-permute-start(bf16[128,2048]{1,0:T(8,128)(2,1)S(1)} %get-tuple-element.221), channel_id=1, source_target_pairs={{0,8},{4,12},{8,0},{12,4},{16,24},{20,28},{24,16},{28,20},{1,9},{5... | collective-permute-start | bytes 1572872 | tf_op jit(solution)/shard_map/ppermute | solution.py:116
  119.4 46.3 %collective-permute-start.13 = (bf16[256,2048]{1,0:T(8,128)(2,1)S(1)}, bf16[256,2048]{1,0:T(8,128)(2,1)S(1)}, u32[]{:S(2)}, u32[]{:S(2)}) collective-permute-start(bf16[256,2048]{1,0:T(8,128)(2,1)S(1)} %pad_maximum_fusion.4), channel_id=1, source_target_pairs={{0,16},{4,20},{8,24},{12,28},{16,0},{20,4},{24,8},{28,12},{1,17},{... | collective-permute-start | bytes 3145736 | tf_op jit(solution)/shard_map/ppermute | solution.py:116
  120.0 46.9 %collective-permute-start.14 = (bf16[256,2048]{1,0:T(8,128)(2,1)S(1)}, bf16[256,2048]{1,0:T(8,128)(2,1)S(1)}, u32[]{:S(2)}, u32[]{:S(2)}) collective-permute-start(bf16[256,2048]{1,0:T(8,128)(2,1)S(1)} %pad_maximum_fusion.5), channel_id=1, source_target_pairs={{0,8},{4,12},{8,0},{12,4},{16,24},{20,28},{24,16},{28,20},{1,9},{5... | collective-permute-start | bytes 3145736 | tf_op jit(solution)/shard_map/ppermute | solution.py:116
  136.1 32.3 %collective-permute-start.15 = (bf16[256,2048]{1,0:T(8,128)(2,1)}, bf16[256,2048]{1,0:T(8,128)(2,1)S(1)}, u32[]{:S(2)}, u32[]{:S(2)}) collective-permute-start(bf16[256,2048]{1,0:T(8,128)(2,1)} %collective-permute-done.6.x_ref.refs_2_), channel_id=1, source_target_pairs={{0,1},{1,2},{2,3},{3,0},{4,5},{5,6},{6,7},{7,4},{8,9},{9,10},{10,1... | collective-permute-start | bytes 3145736 | tf_op jit(solution)/shard_map/ppermute | solution.py:49
  185.6 52.6 %collective-permute-start.18 = (bf16[256,2048]{1,0:T(8,128)(2,1)}, bf16[256,2048]{1,0:T(8,128)(2,1)S(1)}, u32[]{:S(2)}, u32[]{:S(2)}) collective-permute-start(bf16[256,2048]{1,0:T(8,128)(2,1)} %get-tuple-element.134.x_ref.refs_0_), channel_id=1, source_target_pairs={{0,1},{1,2},{2,3},{3,0},{4,5},{5,6},{6,7},{7,4},{8,9},{9,10},{10,1... | collective-permute-start | bytes 3145736 | tf_op jit(solution)/shard_map/ppermute | solution.py:49
  185.7 54.5 %collective-permute-start.19 = (bf16[256,2048]{1,0:T(8,128)(2,1)}, bf16[256,2048]{1,0:T(8,128)(2,1)S(1)}, u32[]{:S(2)}, u32[]{:S(2)}) collective-permute-start(bf16[256,2048]{1,0:T(8,128)(2,1)} %get-tuple-element.134.x_ref.refs_0_), channel_id=1, source_target_pairs={{0,3},{1,0},{2,1},{3,2},{4,7},{5,4},{6,5},{7,6},{8,11},{9,8},{10,9... | collective-permute-start | bytes 3145736 | tf_op jit(solution)/shard_map/ppermute | solution.py:49
  238.2 33.7 %collective-permute-start.21 = (bf16[256,2048]{1,0:T(8,128)(2,1)S(1)}, bf16[256,2048]{1,0:T(8,128)(2,1)S(1)}, u32[]{:S(2)}, u32[]{:S(2)}) collective-permute-start(bf16[256,2048]{1,0:T(8,128)(2,1)S(1)} %collective-permute-done.18.x_ref.refs_0_), channel_id=1, source_target_pairs={{0,1},{1,2},{2,3},{3,0},{4,5},{5,6},{6,7},{7,4},{8,9},{9,10},{10,1... | collective-permute-start | bytes 3145736 | tf_op jit(solution)/shard_map/ppermute | solution.py:49
  292.1 60.9 %collective-permute-start.20 = (bf16[256,2048]{1,0:T(8,128)(2,1)}, bf16[256,2048]{1,0:T(8,128)(2,1)S(1)}, u32[]{:S(2)}, u32[]{:S(2)}) collective-permute-start(bf16[256,2048]{1,0:T(8,128)(2,1)} %slice.103), channel_id=1, source_target_pairs={{0,1},{1,2},{2,3},{3,0},{4,5},{5,6},{6,7},{7,4},{8,9},{9,10},{10,1... | collective-permute-start | bytes 3145736 | tf_op jit(solution)/shard_map/ppermute | solution.py:49
  316.7 43.3 %collective-permute-start.23 = (bf16[256,2048]{1,0:T(8,128)(2,1)}, bf16[256,2048]{1,0:T(8,128)(2,1)S(1)}, u32[]{:S(2)}, u32[]{:S(2)}) collective-permute-start(bf16[256,2048]{1,0:T(8,128)(2,1)} %add_convert_fusion.3), channel_id=1, source_target_pairs={{0,3},{1,0},{2,1},{3,2},{4,7},{5,4},{6,5},{7,6},{8,11},{9,8},{10,9... | collective-permute-start | bytes 3145736 | tf_op jit(solution)/shard_map/ppermute | solution.py:49
  332.2 225.6 %reduce-scatter.5.cloned.1.call-start = ((), (), s32[]{:S(2)}) async-start(), calls=%async_computation.5 | async-start | bytes 11796480 | tf_op jit(solution)/shard_map/reduce_scatter | solution.py:991
  365.3 44.4 %collective-permute-start.24 = (bf16[256,2048]{1,0:T(8,128)(2,1)}, bf16[256,2048]{1,0:T(8,128)(2,1)}, u32[]{:S(2)}, u32[]{:S(2)}) collective-permute-start(bf16[256,2048]{1,0:T(8,128)(2,1)} %slice.109), channel_id=1, source_target_pairs={{0,1},{1,2},{2,3},{3,0},{4,5},{5,6},{6,7},{7,4},{8,9},{9,10},{10,1... | collective-permute-start | bytes 3145736 | tf_op jit(solution)/shard_map/ppermute | solution.py:49
  365.8 48.0 %collective-permute-start.25 = (bf16[256,2048]{1,0:T(8,128)(2,1)}, bf16[256,2048]{1,0:T(8,128)(2,1)}, u32[]{:S(2)}, u32[]{:S(2)}) collective-permute-start(bf16[256,2048]{1,0:T(8,128)(2,1)} %fusion.7), channel_id=1, source_target_pairs={{0,3},{1,0},{2,1},{3,2},{4,7},{5,4},{6,5},{7,6},{8,11},{9,8},{10,9... | collective-permute-start | bytes 3145736 | tf_op jit(solution)/shard_map/ppermute | solution.py:49
  420.0 45.4 %collective-permute-start.30 = (bf16[1024,2048]{1,0:T(8,128)(2,1)}, bf16[1024,2048]{1,0:T(8,128)(2,1)}, u32[]{:S(2)}, u32[]{:S(2)}) collective-permute-start(bf16[1024,2048]{1,0:T(8,128)(2,1)} %weight_grad.7), channel_id=1, source_target_pairs={{0,4},{4,0},{8,12},{12,8},{16,20},{20,16},{24,28},{28,24},{1,5},{5... | collective-permute-start | bytes 12582920 | tf_op jit(solution)/shard_map/ppermute | solution.py:116
  421.8 31.3 %collective-permute-start.26 = (bf16[256,2048]{1,0:T(8,128)(2,1)S(1)}, bf16[256,2048]{1,0:T(8,128)(2,1)}, u32[]{:S(2)}, u32[]{:S(2)}) collective-permute-start(bf16[256,2048]{1,0:T(8,128)(2,1)S(1)} %add_convert_fusion.2), channel_id=1, source_target_pairs={{0,3},{1,0},{2,1},{3,2},{4,7},{5,4},{6,5},{7,6},{8,11},{9,8},{10,9... | collective-permute-start | bytes 3145736 | tf_op jit(solution)/shard_map/ppermute | solution.py:49
  425.1 40.3 %collective-permute-start.29 = (bf16[512,256]{1,0:T(8,128)(2,1)S(1)}, bf16[512,256]{1,0:T(8,128)(2,1)S(1)}, u32[]{:S(2)}, u32[]{:S(2)}) collective-permute-start(bf16[512,256]{1,0:T(8,128)(2,1)S(1)} %get-tuple-element.219), channel_id=1, source_target_pairs={{0,1},{1,2},{2,3},{3,0},{4,5},{5,6},{6,7},{7,4},{8,9},{9,10},{10,1... | collective-permute-start | bytes 786440 | tf_op jit(solution)/shard_map/ppermute | solution.py:49
  480.4 64.3 %collective-permute-start.31 = (bf16[1024,512]{1,0:T(8,128)(2,1)}, bf16[1024,512]{1,0:T(8,128)(2,1)}, u32[]{:S(2)}, u32[]{:S(2)}) collective-permute-start(bf16[1024,512]{1,0:T(8,128)(2,1)} %weight_grad.11), channel_id=1, source_target_pairs={{0,1},{1,2},{2,3},{3,0},{4,5},{5,6},{6,7},{7,4},{8,9},{9,10},{10,1... | collective-permute-start | bytes 3145736 | tf_op jit(solution)/shard_map/ppermute | solution.py:49
  480.4 47.9 %collective-permute-start.32 = (bf16[1024,512]{1,0:T(8,128)(2,1)}, bf16[1024,512]{1,0:T(8,128)(2,1)}, u32[]{:S(2)}, u32[]{:S(2)}) collective-permute-start(bf16[1024,512]{1,0:T(8,128)(2,1)} %weight_grad.10), channel_id=1, source_target_pairs={{0,3},{1,0},{2,1},{3,2},{4,7},{5,4},{6,5},{7,6},{8,11},{9,8},{10,9... | collective-permute-start | bytes 3145736 | tf_op jit(solution)/shard_map/ppermute | solution.py:49
  502.2 30.6 %collective-permute-start.34 = (f32[2,2048]{1,0:T(2,128)S(1)}, f32[2,2048]{1,0:T(2,128)S(1)}, u32[]{:S(2)}, u32[]{:S(2)}) collective-permute-start(f32[2,2048]{1,0:T(2,128)S(1)} %pad_maximum_fusion.9), channel_id=1, source_target_pairs={{0,4},{4,0},{8,12},{12,8},{16,20},{20,16},{24,28},{28,24},{1,5},{5... | collective-permute-start | bytes 49160 | tf_op jit(solution)/shard_map/ppermute | solution.py:116
  (72 other events, 719.8 us)
Sparse Core Ops, SparseCore 0:
  40.8 68.4 all-gather.2
  111.8 111.6 all-gather.4
  332.4 115.8 reduce-scatter.2
  471.6 80.2 reduce-scatter.4
